TPU v7x, 128 devices: a whole 4x4x4 slice. The times are simulated.
128 devices in a mesh: cells: 32 (over x, z, core), split: 4 (over y).
Axes of the slice: x: 4, y: 4, z: 4, core: 2. Of those that a mesh axis runs over, the one named last changes fastest.
Arguments:
- voltage: float32 [4, 32, 131072], P('split', None, 'cells'), may hold values from -4 to 4
- gate_state: float32 [4, 32, 131072], P('split', None, 'cells'), may hold values from 0 to 1
- stimulus: float32 [4, 32, 131072], P('split', None, 'cells'), may hold values from -6 to 6
- gate_rate: float32 [4, 32, 131072], P('split', None, 'cells'), may hold values from 0.05 to 1
- gate_conductance: float32 [4, 32, 131072], P('split', None, 'cells'), may hold values from 0.2 to 2
- soma_voltage: float32 [131072], P('cells'), may hold values from -4 to 4
- soma_stimulus: float32 [131072], P('cells'), may hold values from -12 to 12
- axial_conductance: float32 [4, 32], replicated, may hold values from 0.5 to 4
- gap_source: int32 [262144], P(('cells', 'split')), may hold values from 0 to 131071
- gap_route: int32 [262144, 1], P(('cells', 'split')), may hold values from 0 to 127; in each aligned block of 2048 rows (0 to 2047, 2048 to 4095, ...) at most 32 rows name the same one
- gap_target: int32 [262144], P(('cells', 'split')), may hold values from 0 to 131071
- gap_conductance: float32 [262144], P(('cells', 'split')), may hold values from 0.05 to 0.5
- vox_index: int32 [4, 4, 131072], P('split', None, 'cells'), may hold values from 0 to 65535, as said below
- field_resist: float32 [65536], P(('cells', 'split')), may hold values from 0.5 to 5
Outputs:
- voltage_out: float32 [4, 32, 131072], P('split', None, 'cells')
- gate_out: float32 [4, 32, 131072], P('split', None, 'cells')
- soma_out: float32 [131072], P('cells')
- field_potential: float32 [65536], P(('cells', 'split'))
Inputs may be any that keep to these rules, and one draw needn't show every extreme that they name: `gap_route`: among the rows of one device at most 32 name the same device, and some device is named by exactly 32 rows of one device. `vox_index`: among the 16384 blocks of one device at most 256 fall on voxels of one owner; on every device exactly 256 fall on one owner, and the others are spread evenly over the remaining owners.
All inputs are finite; a program needn't handle non-finite values.
Results may differ from a plain program's by a relative error of at most 0.0001.
Values sent between devices are 32-bit elements; how exact they have to be, the bound alone decides.
No kernel may reach another device: no remote copies, remote signals or barrier semaphores. Data moves between devices by JAX's collectives and lax.ppermute only.
A program may use at most 128 MiB of HBM per device.

v0:
```python
import math

import jax
import jax.numpy as jnp
from jax import lax
from jax.sharding import PartitionSpec as P

SUB = 2


membrane_diag = 4.0
soma_diag = 8.0
reversal = -1.0
ephaptic = 0.5
block_limit = 1024


def branch_inverses(axial_conductance):
    comp_count = axial_conductance.shape[1]
    beyond = jnp.concatenate(
        [
            axial_conductance[:, 1:],
            jnp.zeros((axial_conductance.shape[0], 1), axial_conductance.dtype),
        ],
        axis=1,
    )
    diagonal = membrane_diag + axial_conductance + beyond

    def single_inverse(diag_row, off_row):
        matrix = jnp.diag(diag_row) - jnp.diag(off_row[:-1], 1) - jnp.diag(off_row[:-1], -1)
        factor = jnp.linalg.cholesky(matrix)
        identity = jnp.eye(comp_count, dtype=diag_row.dtype)
        lower_inv = lax.linalg.triangular_solve(factor, identity, left_side=True, lower=True)
        return jnp.dot(lower_inv.T, lower_inv, precision=lax.Precision.HIGHEST)

    return jax.vmap(single_inverse)(diagonal, beyond)


def slot_positions(owner, devices, capacity):
    onehot = (owner[:, None] == jnp.arange(devices, dtype=jnp.int32)[None, :]).astype(jnp.int32)
    before = jnp.cumsum(onehot, axis=0) - onehot
    rank = jnp.sum(before * onehot, axis=1)
    return owner * capacity + rank


def hot_pick(table, indices):
    row_count, col_count = table.shape
    item_count = indices.shape[0]
    step_size = math.gcd(item_count, block_limit)
    pieces = indices.reshape(item_count // step_size, step_size)

    def single_block(chosen):
        low_hot = (
            jnp.arange(col_count, dtype=jnp.int32)[:, None] == (chosen % col_count)[None, :]
        ).astype(jnp.float32)
        high_hot = (
            jnp.arange(row_count, dtype=jnp.int32)[:, None] == (chosen // col_count)[None, :]
        ).astype(jnp.float32)
        between = jnp.dot(table, low_hot, precision=lax.Precision.HIGHEST)
        return jnp.sum(between * high_hot, axis=0)

    return lax.map(single_block, pieces).reshape(item_count)


def hot_add(values, indices, row_count, col_count):
    item_count = indices.shape[0]
    step_size = math.gcd(item_count, block_limit)
    value_pieces = values.reshape(item_count // step_size, step_size)
    index_pieces = indices.reshape(item_count // step_size, step_size)

    def accumulate(carry, pieces):
        amounts, chosen = pieces
        low_hot = (
            (chosen % col_count)[:, None] == jnp.arange(col_count, dtype=jnp.int32)[None, :]
        ).astype(jnp.float32)
        high_hot = (
            jnp.arange(row_count, dtype=jnp.int32)[:, None] == (chosen // col_count)[None, :]
        ).astype(jnp.float32)
        weighted = high_hot * amounts[None, :]
        return (carry + jnp.dot(weighted, low_hot, precision=lax.Precision.HIGHEST), None)

    start_value = jnp.zeros((row_count, col_count), jnp.float32)
    result, unused = lax.scan(accumulate, start_value, (value_pieces, index_pieces))
    return result


def per_device(
    voltage,
    gate_state,
    stimulus,
    gate_rate,
    gate_conductance,
    soma_voltage,
    soma_stimulus,
    axial_conductance,
    gap_source,
    gap_route,
    gap_target,
    gap_conductance,
    vox_index,
    field_resist,
):
    n_cells = lax.axis_size("cells")
    n_split = lax.axis_size("split")
    devices = n_cells * n_split
    comp_count = voltage.shape[1]
    cell_dev = voltage.shape[2]
    block_count = vox_index.shape[1]
    block_size = comp_count // block_count
    gap_rows = gap_source.shape[0]
    slot_count = max(2, 2 * gap_rows // devices)
    vox_dev = field_resist.shape[0]
    field_scale = vox_dev / (comp_count * cell_dev)
    inverses = branch_inverses(axial_conductance)
    head_all = axial_conductance[:, 0]
    shared = jnp.sum(head_all * head_all * inverses[:, 0, 0])
    soma_total = soma_diag + jnp.sum(head_all)
    branch_index = lax.axis_index("split")
    inverse = lax.dynamic_index_in_dim(inverses, branch_index, 0, keepdims=False)
    head_axial = lax.dynamic_index_in_dim(head_all, branch_index, 0, keepdims=False)
    first_column = inverse[:, 0:1]
    destination = gap_route[:, 0]
    position = slot_positions(destination, devices, slot_count)
    send_target = jnp.zeros((devices * slot_count,), jnp.int32).at[position].set(gap_target)
    send_weight = jnp.zeros((devices * slot_count,), jnp.float32).at[position].set(gap_conductance)
    slot_source = jnp.zeros((devices * slot_count,), jnp.int32).at[position].set(gap_source)
    recv_target = lax.all_to_all(
        send_target, ("cells", "split"), split_axis=0, concat_axis=0, tiled=True
    )
    recv_weight = lax.all_to_all(
        send_weight, ("cells", "split"), split_axis=0, concat_axis=0, tiled=True
    )
    weight_total = hot_add(recv_weight, recv_target, comp_count, cell_dev)
    vox_local = vox_index[0].reshape(-1)
    volts_now = voltage[0]
    gating = gate_state[0]
    stim_local = stimulus[0]
    rate_local = gate_rate[0]
    cond_local = gate_conductance[0]
    soma = soma_voltage
    phi_comp = jnp.zeros_like(volts_now)
    potential_own = jnp.zeros_like(field_resist)
    for substep in range(SUB):
        sent = send_weight * hot_pick(volts_now, slot_source)
        received = lax.all_to_all(sent, ("cells", "split"), split_axis=0, concat_axis=0, tiled=True)
        gap_in = hot_add(received, recv_target, comp_count, cell_dev) - weight_total * volts_now
        settle = jax.nn.sigmoid(2.0 * volts_now)
        gating = settle + (gating - settle) * jnp.exp(-rate_local * (1.0 + volts_now * volts_now))
        current = cond_local * gating * (volts_now - reversal)
        block_sums = current.reshape(block_count, block_size, cell_dev).sum(axis=1)
        local_voxel = hot_add(block_sums.reshape(-1), vox_local, devices, vox_dev).reshape(-1)
        own_current = lax.psum_scatter(
            local_voxel, ("cells", "split"), scatter_dimension=0, tiled=True
        )
        potential_own = field_resist * own_current * field_scale
        potential = lax.all_gather(potential_own, ("cells", "split"), axis=0, tiled=True)
        looked_flat = hot_pick(potential.reshape(devices, vox_dev), vox_local)
        rhs = membrane_diag * volts_now + stim_local - current + gap_in - ephaptic * phi_comp
        solved = jnp.dot(inverse, rhs, precision=lax.Precision.HIGHEST)
        partial_value = lax.psum(head_axial * solved[0], "split")
        soma = (soma_diag * soma + soma_stimulus + partial_value) / (soma_total - shared)
        volts_now = solved + head_axial * first_column * soma[None, :]
        looked = looked_flat.reshape(block_count, 1, cell_dev)
        phi_comp = jnp.broadcast_to(looked, (block_count, block_size, cell_dev)).reshape(
            comp_count, cell_dev
        )
    return (volts_now[None], gating[None], soma, potential_own)


def solution(mesh):
    in_specs = (
        P("split", None, "cells"),
        P("split", None, "cells"),
        P("split", None, "cells"),
        P("split", None, "cells"),
        P("split", None, "cells"),
        P("cells"),
        P("cells"),
        P(),
        P(("cells", "split")),
        P(("cells", "split"), None),
        P(("cells", "split")),
        P(("cells", "split")),
        P("split", None, "cells"),
        P(("cells", "split")),
    )
    out_specs = (
        P("split", None, "cells"),
        P("split", None, "cells"),
        P("cells"),
        P(("cells", "split")),
    )
    return jax.shard_map(
        per_device, mesh=mesh, in_specs=in_specs, out_specs=out_specs, check_vma=False
    )
```

profile of v0, /device:TPU:0, one launch (start us, length us, event | category | flops | bytes accessed | tf_op | source)
XLA Modules:
  0.0 539.5 jit_solution(2554767863776636247)
XLA Ops:
  9.8 8.2 %scatter_custom_fusion.2 = s32[4096]{0:T(1024)S(1)} fusion(s32[2048]{0:T(1024)S(1)} %bitcast.298, s32[2048]{0:T(1024)} %param.38, s32[]{:T(128)} %constant.545.clone.1), kind=kCustom, calls=%fused_computation.216 | custom fusion | bytes 16896 | tf_op jit(solution)/shard_map/scatter | solution.py:126
  18.1 23.7 %while.101 = (s32[]{:T(128)}, f32[4,1024]{1,0:T(4,128)S(1)}, s32[4,1024]{1,0:T(4,128)S(1)}, f32[32,4096]{1,0:T(8,128)S(1)}, s32[]{:T(128)}, /*index=5*/s32[]{:T(128)}) while((s32[]{:T(128)}, f32[4,1024]{1,0:T(4,128)S(1)}, s32[4,1024]{1,0:T(4,128)S(1)}, f32[32,4096]{1,0:T(8,128)S(1)}, s32[]{:T(128)}, /*index=5*/s32[]{:T(128)}) %tuple.260), condition=%wide.region_9.10_spmd, body=%wide.region_7.9_spmd.sunk | while | flops 1614924800 | bytes 565325 | solution.py:62
  41.8 8.4 %scatter_custom_fusion.1 = f32[4096]{0:T(1024)S(1)} fusion(s32[2048]{0:T(1024)S(1)} %bitcast.299, f32[2048]{0:T(1024)} %param.41, f32[]{:T(128)} %constant.538.clone.1), kind=kCustom, calls=%fused_computation.214 | custom fusion | bytes 16896 | tf_op jit(solution)/shard_map/scatter | solution.py:125
  50.9 11.6 %all-to-all-start.1 = ((f32[128,32,1]{1,2,0:T(1,128)}), f32[128,32,1]{1,2,0:T(1,128)S(1)}, u32[]{:S(2)}, u32[]{:S(2)}) async-start(f32[128,32,1]{1,2,0:T(1,128)} %bitcast.28), calls=%async_computation.1 | async-start | bytes 131072 | tf_op jit(solution)/shard_map/all_to_all | solution.py:145
  63.6 11.7 %custom-call.7 = f32[4,32,32]{2,1,0:T(8,128)S(1)} custom-call(f32[4,32,32]{2,1,0:T(8,128)S(1)} %add_multiply_fusion), custom_call_target="Cholesky" | custom-call | tf_op jit(solution)/shard_map/vmap(jit(cholesky))/cholesky | solution.py:31
  75.6 9.8 %custom-call.8 = f32[4,1,32,32]{2,3,1,0:T(8,128)S(1)} custom-call(f32[4,1,32,32]{3,2,1,0:T(8,128)S(1)} %select_bitcast_fusion), custom_call_target="InvertDiagBlocksLowerTriangular" | custom-call | tf_op jit(solution)/shard_map/vmap()/triangular_solve | solution.py:33
  87.2 8.2 %scatter_custom_fusion = s32[4096]{0:T(1024)S(1)} fusion(s32[2048]{0:T(1024)S(1)} %bitcast.300, s32[2048]{0:T(1024)} %param.40, s32[]{:T(128)} %constant.545.clone.1), kind=kCustom, calls=%fused_computation.218 | custom fusion | bytes 16896 | tf_op jit(solution)/shard_map/scatter | solution.py:124
  96.2 9.9 %all-to-all-start = ((s32[128,32,1]{1,2,0:T(1,128)}), s32[128,32,1]{1,2,0:T(1,128)S(1)}, u32[]{:S(2)}, u32[]{:S(2)}) async-start(s32[128,32,1]{1,2,0:T(1,128)} %bitcast.27), calls=%async_computation | async-start | bytes 131072 | tf_op jit(solution)/shard_map/all_to_all | solution.py:127
  121.4 25.3 %while.104 = (s32[]{:T(128)}, f32[32,4096]{1,0:T(8,128)S(1)}, s32[4,1024]{1,0:T(4,128)S(1)}, f32[4,1024]{1,0:T(4,128)S(1)}, s32[]{:T(128)}, /*index=5*/s32[]{:T(128)}) while((s32[]{:T(128)}, f32[32,4096]{1,0:T(8,128)S(1)}, s32[4,1024]{1,0:T(4,128)S(1)}, f32[4,1024]{1,0:T(4,128)S(1)}, s32[]{:T(128)}, /*index=5*/s32[]{:T(128)}) %tuple.236), condition=%wide.region_12.13_spmd.clone, body=%wide.region_11.12_spmd.clone.sunk | while | flops 1615161344 | bytes 1089623 | solution.py:83
  121.5 6.2 %fusion.147 = f32[32,4096]{1,0:T(8,128)S(1)} fusion(s32[1024]{0:T(1024)S(1)} %add_select_fusion.10, f32[32,4096]{1,0:T(8,128)S(1)} %get-tuple-element.892, pred[]{:T(512)S(6)} %compare.98, f32[1024]{0:T(1024)S(1)} %bitcast.279, s32[1024]{0:T(1024)S(1)} %bitcast.271), kind=kOutput, calls=%fused_computation.42.clone.1 | convolution fusion | flops 1615134720 | bytes 1060865 | tf_op jit(solution)/shard_map/while/body/eval_jaxpr/dot_general | solution.py:80
  127.8 6.2 %fusion.147 = f32[32,4096]{1,0:T(8,128)S(1)} fusion(s32[1024]{0:T(1024)S(1)} %add_select_fusion.10, f32[32,4096]{1,0:T(8,128)S(1)} %get-tuple-element.892, pred[]{:T(512)S(6)} %compare.98, f32[1024]{0:T(1024)S(1)} %bitcast.279, s32[1024]{0:T(1024)S(1)} %bitcast.271), kind=kOutput, calls=%fused_computation.42.clone.1 | convolution fusion | flops 1615134720 | bytes 1060865 | tf_op jit(solution)/shard_map/while/body/eval_jaxpr/dot_general | solution.py:80
  134.1 6.2 %fusion.147 = f32[32,4096]{1,0:T(8,128)S(1)} fusion(s32[1024]{0:T(1024)S(1)} %add_select_fusion.10, f32[32,4096]{1,0:T(8,128)S(1)} %get-tuple-element.892, pred[]{:T(512)S(6)} %compare.98, f32[1024]{0:T(1024)S(1)} %bitcast.279, s32[1024]{0:T(1024)S(1)} %bitcast.271), kind=kOutput, calls=%fused_computation.42.clone.1 | convolution fusion | flops 1615134720 | bytes 1060865 | tf_op jit(solution)/shard_map/while/body/eval_jaxpr/dot_general | solution.py:80
  140.5 6.2 %fusion.147 = f32[32,4096]{1,0:T(8,128)S(1)} fusion(s32[1024]{0:T(1024)S(1)} %add_select_fusion.10, f32[32,4096]{1,0:T(8,128)S(1)} %get-tuple-element.892, pred[]{:T(512)S(6)} %compare.98, f32[1024]{0:T(1024)S(1)} %bitcast.279, s32[1024]{0:T(1024)S(1)} %bitcast.271), kind=kOutput, calls=%fused_computation.42.clone.1 | convolution fusion | flops 1615134720 | bytes 1060865 | tf_op jit(solution)/shard_map/while/body/eval_jaxpr/dot_general | solution.py:80
  147.7 25.5 %while.105 = (s32[]{:T(128)}, f32[32,4096]{1,0:T(8,128)S(1)}, s32[4,1024]{1,0:T(4,128)S(1)}, f32[4,1024]{1,0:T(4,128)S(1)}, s32[]{:T(128)}, /*index=5*/s32[]{:T(128)}) while((s32[]{:T(128)}, f32[32,4096]{1,0:T(8,128)S(1)}, s32[4,1024]{1,0:T(4,128)S(1)}, f32[4,1024]{1,0:T(4,128)S(1)}, s32[]{:T(128)}, /*index=5*/s32[]{:T(128)}) %tuple.261), condition=%wide.region_14.15_spmd.clone, body=%wide.region_13.14_spmd.clone.sunk | while | flops 1615161344 | bytes 1089623 | solution.py:83
  147.8 6.2 %fusion.149 = f32[32,4096]{1,0:T(8,128)S(1)} fusion(s32[1024]{0:T(1024)S(1)} %add_select_fusion.11, f32[32,4096]{1,0:T(8,128)S(1)} %get-tuple-element.910, pred[]{:T(512)S(6)} %compare.99, f32[1024]{0:T(1024)S(1)} %bitcast.280, s32[1024]{0:T(1024)S(1)} %bitcast.272), kind=kOutput, calls=%fused_computation.62.clone.1 | convolution fusion | flops 1615134720 | bytes 1060865 | tf_op jit(solution)/shard_map/while/body/eval_jaxpr/dot_general | solution.py:80
  154.1 6.2 %fusion.149 = f32[32,4096]{1,0:T(8,128)S(1)} fusion(s32[1024]{0:T(1024)S(1)} %add_select_fusion.11, f32[32,4096]{1,0:T(8,128)S(1)} %get-tuple-element.910, pred[]{:T(512)S(6)} %compare.99, f32[1024]{0:T(1024)S(1)} %bitcast.280, s32[1024]{0:T(1024)S(1)} %bitcast.272), kind=kOutput, calls=%fused_computation.62.clone.1 | convolution fusion | flops 1615134720 | bytes 1060865 | tf_op jit(solution)/shard_map/while/body/eval_jaxpr/dot_general | solution.py:80
  160.4 6.2 %fusion.149 = f32[32,4096]{1,0:T(8,128)S(1)} fusion(s32[1024]{0:T(1024)S(1)} %add_select_fusion.11, f32[32,4096]{1,0:T(8,128)S(1)} %get-tuple-element.910, pred[]{:T(512)S(6)} %compare.99, f32[1024]{0:T(1024)S(1)} %bitcast.280, s32[1024]{0:T(1024)S(1)} %bitcast.272), kind=kOutput, calls=%fused_computation.62.clone.1 | convolution fusion | flops 1615134720 | bytes 1060865 | tf_op jit(solution)/shard_map/while/body/eval_jaxpr/dot_general | solution.py:80
  166.8 6.2 %fusion.149 = f32[32,4096]{1,0:T(8,128)S(1)} fusion(s32[1024]{0:T(1024)S(1)} %add_select_fusion.11, f32[32,4096]{1,0:T(8,128)S(1)} %get-tuple-element.910, pred[]{:T(512)S(6)} %compare.99, f32[1024]{0:T(1024)S(1)} %bitcast.280, s32[1024]{0:T(1024)S(1)} %bitcast.272), kind=kOutput, calls=%fused_computation.62.clone.1 | convolution fusion | flops 1615134720 | bytes 1060865 | tf_op jit(solution)/shard_map/while/body/eval_jaxpr/dot_general | solution.py:80
  176.4 16.4 %psum.14 = f32[4096]{0:T(1024)S(1)} all-reduce(f32[4096]{0:T(1024)S(1)} %bitcast.295), channel_id=1, replica_groups=mesh['cells'=32,'split'=4] {'split'}, use_global_device_ids=true, to_apply=%region_15.16 | all-reduce | flops 4096 | bytes 32768 | tf_op jit(solution)/shard_map/psum | solution.py:160
  195.1 41.9 %while.107 = (s32[]{:T(128)}, f32[128,512]{1,0:T(8,128)}, s32[16,1024]{1,0:T(8,128)S(1)}, f32[16,1024]{1,0:T(8,128)S(1)}, s32[]{:T(128)}, /*index=5*/s32[]{:T(128)}) while((s32[]{:T(128)}, f32[128,512]{1,0:T(8,128)}, s32[16,1024]{1,0:T(8,128)S(1)}, f32[16,1024]{1,0:T(8,128)S(1)}, s32[]{:T(128)}, /*index=5*/s32[]{:T(128)}) %tuple.248), condition=%wide.region_25.26_spmd.clone, body=%wide.region_24.25_spmd.clone.sunk | while | flops 806250496 | bytes 565335 | solution.py:83
  237.0 23.7 %while.102 = (s32[]{:T(128)}, f32[4,1024]{1,0:T(4,128)S(1)}, s32[4,1024]{1,0:T(4,128)S(1)}, f32[32,4096]{1,0:T(8,128)S(1)}, s32[]{:T(128)}, /*index=5*/s32[]{:T(128)}) while((s32[]{:T(128)}, f32[4,1024]{1,0:T(4,128)S(1)}, s32[4,1024]{1,0:T(4,128)S(1)}, f32[32,4096]{1,0:T(8,128)S(1)}, s32[]{:T(128)}, /*index=5*/s32[]{:T(128)}) %tuple.267), condition=%wide.region_20.21_spmd, body=%wide.region_18.20_spmd.sunk | while | flops 1614924800 | bytes 565325 | solution.py:62
  261.4 8.2 %all-to-all-start.3 = ((f32[128,32,1]{1,2,0:T(1,128)}), f32[128,32,1]{1,2,0:T(1,128)S(1)}, u32[]{:S(2)}, u32[]{:S(2)}) async-start(f32[128,32,1]{1,2,0:T(1,128)} %bitcast.33), calls=%async_computation.3 | async-start | bytes 131072 | tf_op jit(solution)/shard_map/all_to_all | solution.py:145
  269.7 17.5 %while.108 = (s32[]{:T(128)}, f32[128,512]{1,0:T(8,128)S(1)}, s32[16,1024]{1,0:T(8,128)S(1)}, f32[16,1024]{1,0:T(8,128)S(1)}, s32[]{:T(128)}, /*index=5*/s32[]{:T(128)}) while((s32[]{:T(128)}, f32[128,512]{1,0:T(8,128)S(1)}, s32[16,1024]{1,0:T(8,128)S(1)}, f32[16,1024]{1,0:T(8,128)S(1)}, s32[]{:T(128)}, ...), condition=%wide.region_33.34_spmd.clone, body=%wide.region_32.33_spmd.clone.sunk | while | flops 806250496 | bytes 565335 | solution.py:83
  289.7 25.3 %while.106 = (s32[]{:T(128)}, f32[32,4096]{1,0:T(8,128)S(1)}, s32[4,1024]{1,0:T(4,128)S(1)}, f32[4,1024]{1,0:T(4,128)S(1)}, s32[]{:T(128)}, /*index=5*/s32[]{:T(128)}) while((s32[]{:T(128)}, f32[32,4096]{1,0:T(8,128)S(1)}, s32[4,1024]{1,0:T(4,128)S(1)}, f32[4,1024]{1,0:T(4,128)S(1)}, s32[]{:T(128)}, /*index=5*/s32[]{:T(128)}) %tuple.262), condition=%wide.region_22.23_spmd.clone, body=%wide.region_21.22_spmd.clone.sunk | while | flops 1615161344 | bytes 1089623 | solution.py:83
  289.8 6.2 %fusion.151 = f32[32,4096]{1,0:T(8,128)S(1)} fusion(s32[1024]{0:T(1024)S(1)} %add_select_fusion.12, f32[32,4096]{1,0:T(8,128)S(1)} %get-tuple-element.946, pred[]{:T(512)S(6)} %compare.100, f32[1024]{0:T(1024)S(1)} %bitcast.283, s32[1024]{0:T(1024)S(1)} %bitcast.275), kind=kOutput, calls=%fused_computation.82.clone.1 | convolution fusion | flops 1615134720 | bytes 1060865 | tf_op jit(solution)/shard_map/while/body/eval_jaxpr/dot_general | solution.py:80
  296.1 6.2 %fusion.151 = f32[32,4096]{1,0:T(8,128)S(1)} fusion(s32[1024]{0:T(1024)S(1)} %add_select_fusion.12, f32[32,4096]{1,0:T(8,128)S(1)} %get-tuple-element.946, pred[]{:T(512)S(6)} %compare.100, f32[1024]{0:T(1024)S(1)} %bitcast.283, s32[1024]{0:T(1024)S(1)} %bitcast.275), kind=kOutput, calls=%fused_computation.82.clone.1 | convolution fusion | flops 1615134720 | bytes 1060865 | tf_op jit(solution)/shard_map/while/body/eval_jaxpr/dot_general | solution.py:80
  302.4 6.2 %fusion.151 = f32[32,4096]{1,0:T(8,128)S(1)} fusion(s32[1024]{0:T(1024)S(1)} %add_select_fusion.12, f32[32,4096]{1,0:T(8,128)S(1)} %get-tuple-element.946, pred[]{:T(512)S(6)} %compare.100, f32[1024]{0:T(1024)S(1)} %bitcast.283, s32[1024]{0:T(1024)S(1)} %bitcast.275), kind=kOutput, calls=%fused_computation.82.clone.1 | convolution fusion | flops 1615134720 | bytes 1060865 | tf_op jit(solution)/shard_map/while/body/eval_jaxpr/dot_general | solution.py:80
  308.8 6.2 %fusion.151 = f32[32,4096]{1,0:T(8,128)S(1)} fusion(s32[1024]{0:T(1024)S(1)} %add_select_fusion.12, f32[32,4096]{1,0:T(8,128)S(1)} %get-tuple-element.946, pred[]{:T(512)S(6)} %compare.100, f32[1024]{0:T(1024)S(1)} %bitcast.283, s32[1024]{0:T(1024)S(1)} %bitcast.275), kind=kOutput, calls=%fused_computation.82.clone.1 | convolution fusion | flops 1615134720 | bytes 1060865 | tf_op jit(solution)/shard_map/while/body/eval_jaxpr/dot_general | solution.py:80
  315.0 119.8 %all-reduce.7.cloned.1.call-done = (f32[65536]{0:T(1024)}, f32[65536]{0:T(1024)}) async-done(((f32[65536]{0:T(1024)}, f32[65536]{0:T(1024)}), (f32[65536]{0:T(1024)}, f32[65536]{0:T(1024)})) %all-reduce.7.cloned.1.call-update) | async-done | bytes 524304
  436.2 60.3 %all-gather = f32[128,1,512]{2,1,0:T(1,128)S(1)} all-gather(f32[1,1,512]{2,1,0:T(1,128)S(1)} %bitcast.297), channel_id=1, replica_groups=mesh['cells'=32,'split'=4] {'cells','split'}, dimensions={0}, use_global_device_ids=true | all-gather | bytes 264192 | tf_op jit(solution)/shard_map/all_gather | solution.py:156
  496.5 16.7 %while.103 = (s32[]{:T(128)}, f32[16,1024]{1,0:T(8,128)S(1)}, s32[16,1024]{1,0:T(8,128)S(1)}, f32[128,512]{1,0:T(8,128)S(1)}, s32[]{:T(128)}, /*index=5*/s32[]{:T(128)}) while((s32[]{:T(128)}, f32[16,1024]{1,0:T(8,128)S(1)}, s32[16,1024]{1,0:T(8,128)S(1)}, f32[128,512]{1,0:T(8,128)S(1)}, s32[]{:T(128)}, /*index=5*/s32[]{:T(128)}) %tuple.266), condition=%wide.region_29.30_spmd, body=%wide.region_27.29_spmd.sunk | while | flops 806243328 | bytes 303181 | solution.py:62
  515.7 15.8 %psum.15 = f32[4096]{0:T(1024)S(1)} all-reduce(f32[4096]{0:T(1024)S(1)} %bitcast.294), channel_id=1, replica_groups=mesh['cells'=32,'split'=4] {'split'}, use_global_device_ids=true, to_apply=%region_30.31 | all-reduce | flops 4096 | bytes 32768 | tf_op jit(solution)/shard_map/psum | solution.py:160
  (368 shorter events, 157.1 us)
Async XLA Ops:
  8.4 0.7 copy-start.7
  8.8 9.3 %copy-start.4 = (f32[1,32,4096]{2,1,0:T(8,128)S(1)}, f32[1,32,4096]{2,1,0:T(8,128)}, u32[]{:S(2)}) copy-start(f32[1,32,4096]{2,1,0:T(8,128)} %param.30) | copy-start | bytes 1572868
  18.1 44.5 %copy-start.11 = (f32[4,32]{1,0:T(4,128)S(1)}, f32[4,32]{1,0:T(4,128)}, u32[]{:S(2)}) copy-start(f32[4,32]{1,0:T(4,128)} %param.37) | copy-start | bytes 1540
  41.8 65.7 %copy-start.9 = (s32[1,4,4096]{2,1,0:T(4,128)S(1)}, s32[1,4,4096]{2,1,0:T(4,128)}, u32[]{:S(2)}) copy-start(s32[1,4,4096]{2,1,0:T(4,128)} %param.42) | copy-start | bytes 196612
  50.9 45.3 %all-to-all-start.1 = ((f32[128,32,1]{1,2,0:T(1,128)}), f32[128,32,1]{1,2,0:T(1,128)S(1)}, u32[]{:S(2)}, u32[]{:S(2)}) async-start(f32[128,32,1]{1,2,0:T(1,128)} %bitcast.28), calls=%async_computation.1 | async-start | bytes 131072 | tf_op jit(solution)/shard_map/all_to_all | solution.py:145
  96.2 19.0 %all-to-all-start = ((s32[128,32,1]{1,2,0:T(1,128)}), s32[128,32,1]{1,2,0:T(1,128)S(1)}, u32[]{:S(2)}, u32[]{:S(2)}) async-start(s32[128,32,1]{1,2,0:T(1,128)} %bitcast.27), calls=%async_computation | async-start | bytes 131072 | tf_op jit(solution)/shard_map/all_to_all | solution.py:127
  115.2 31.6 %all-to-all-start.2 = ((f32[128,32,1]{1,2,0:T(1,128)}), f32[128,32,1]{1,2,0:T(1,128)S(1)}, u32[]{:S(2)}, u32[]{:S(2)}) async-start(f32[128,32,1]{1,2,0:T(1,128)} %bitcast.29), calls=%async_computation.2 | async-start | bytes 131072 | tf_op jit(solution)/shard_map/all_to_all | solution.py:130
  146.7 0.9 copy-start.14
  147.7 25.5 %copy-start = (f32[1,32,4096]{2,1,0:T(8,128)S(1)}, f32[1,32,4096]{2,1,0:T(8,128)}, u32[]{:S(2)}) copy-start(f32[1,32,4096]{2,1,0:T(8,128)} %param.34) | copy-start | bytes 1572868
  147.7 25.5 %copy-start.2 = (f32[1,32,4096]{2,1,0:T(8,128)S(1)}, f32[1,32,4096]{2,1,0:T(8,128)}, u32[]{:S(2)}) copy-start(f32[1,32,4096]{2,1,0:T(8,128)} %param.32) | copy-start | bytes 1572868
  173.2 2.6 copy-start.3
  173.2 19.5 %copy-start.10 = (f32[4096]{0:T(1024)S(1)}, f32[4096]{0:T(1024)}, u32[]{:S(2)}) copy-start(f32[4096]{0:T(1024)} %param.36) | copy-start | bytes 49156
  173.2 19.5 %copy-start.12 = (f32[4096]{0:T(1024)S(1)}, f32[4096]{0:T(1024)}, u32[]{:S(2)}) copy-start(f32[4096]{0:T(1024)} %param.35) | copy-start | bytes 49156
  195.0 318.3 %copy-start.1 = (f32[32,4096]{1,0:T(8,128)}, f32[32,4096]{1,0:T(8,128)S(1)}, u32[]{:S(2)}) copy-start(f32[32,4096]{1,0:T(8,128)S(1)} %get-tuple-element.621) | copy-start | bytes 1572868
  237.0 32.6 %copy-start.5 = (f32[128,512]{1,0:T(8,128)S(1)}, f32[128,512]{1,0:T(8,128)}, u32[]{:S(2)}) copy-start(f32[128,512]{1,0:T(8,128)} %custom-call.13) | copy-start | bytes 786436
  261.4 27.4 %all-to-all-start.3 = ((f32[128,32,1]{1,2,0:T(1,128)}), f32[128,32,1]{1,2,0:T(1,128)S(1)}, u32[]{:S(2)}, u32[]{:S(2)}) async-start(f32[128,32,1]{1,2,0:T(1,128)} %bitcast.33), calls=%async_computation.3 | async-start | bytes 131072 | tf_op jit(solution)/shard_map/all_to_all | solution.py:145
  269.6 165.3 %all-reduce.7.cloned.1.call-start = ((), (), s32[]{:S(2)}) async-start(), calls=%async_computation.4 | async-start | bytes 1048576
  269.7 17.5 %copy-start.6 = (f32[128,512]{1,0:T(8,128)S(1)}, f32[128,512]{1,0:T(8,128)}, u32[]{:S(2)}) copy-start(f32[128,512]{1,0:T(8,128)} %get-tuple-element.457) | copy-start | bytes 786436
  289.7 145.2 %copy-start.13 = (f32[512]{0:T(512)S(1)}, f32[512]{0:T(512)}, u32[]{:S(2)}) copy-start(f32[512]{0:T(512)} %param.43) | copy-start | bytes 6148
  531.5 0.9 copy-start.8
Sparse Core Ops, SparseCore 0:
  288.9 145.9 all-reduce.6
where the time goes:
time: 548 us; the launch traced here: 540 us
  matrix products  196 us (36%)
  waiting for transfers between devices  125 us (23%)
  blocking collectives  92.5 us (17%)
  other arithmetic  36.6 us (7%)
  local copies, waits for them, and re-layouts  36 us (7%)
  starting transfers between devices  34.5 us (6%)
  between operations  16.1 us (3%)
    dot_general x44, matrix products, accumulate(): jnp.dot(weighted, low_hot, precision=lax.Precision.HIGHEST)  131 us
    unnamed x2, waiting for transfers between devices  120 us
    all_gather x1, blocking collectives, per_device(): lax.all_gather(potential_own, ('cells', 'split'), axis=0, tiled=True)  60.3 us
    dot_general x24, matrix products, single_block(): between = jnp.dot(table, low_hot, precision=lax.Precision.HIGHEST)  59.7 us
    psum x2, blocking collectives, per_device(): partial_value = lax.psum(head_axial * solved[0], 'split')  32.2 us
    all_to_all x2, starting transfers between devices, per_device(): lax.all_to_all(sent, ('cells', 'split'), split_axis=0, concat_axis=0, til...  19.8 us
    another operation x3, other arithmetic, single_inverse(): factor = jnp.linalg.cholesky(matrix)  11.9 us
  transfers between devices with their start and end apart: 5, of which 2 were waited for; matrix products, arithmetic and copies ran while one was open for 20% of the time, Pallas kernels for 0%

commit v1 on v0

v1 whole, which is shorter than its diff:
```python
import jax
import jax.numpy as jnp
from jax import lax
from jax.experimental import pallas as pl
from jax.experimental.pallas import tpu as pltpu
from jax.sharding import PartitionSpec as P

SUB = 2
CAP = 32
LOW = 512
STEP = 512

membrane_diag = 4.0
soma_diag = 8.0
reversal = -1.0
ephaptic = 0.5

f32 = jnp.float32
bf16 = jnp.bfloat16
AXES = ("cells", "split")
PARAMS = pltpu.CompilerParams(vmem_limit_bytes=48 * 2**20)
LANES = (((1,), (1,)), ((), ()))


def halves(x):
    high = x.astype(bf16)
    return high, (x - high.astype(f32)).astype(bf16)


def hits(row, size):
    rows = lax.broadcasted_iota(jnp.int16, (size, row.shape[1]), 0)
    return rows == row.astype(jnp.int16)


def chosen(mask, row):
    return jnp.where(mask, row, jnp.zeros((), bf16))


def hot(row, size):
    return jnp.where(hits(row, size), jnp.ones((), bf16), jnp.zeros((), bf16))


def comp_digits(index, cell_dev, comp_count):
    chunks = cell_dev // LOW
    low = index % LOW
    chunk = (index // LOW) % chunks
    return chunk * comp_count + index // cell_dev, low


def inverse_kernel(axial_ref, inverse_ref, soma_ref):
    n = axial_ref.shape[0]
    lanes = axial_ref.shape[1]
    axial = axial_ref[...]
    row = [axial[i : i + 1, :] for i in range(n)]
    lane = lax.broadcasted_iota(jnp.int32, (1, lanes), 1)
    pivot = [None] * n
    ratio = [None] * n
    pivot[n - 1] = membrane_diag + row[n - 1]
    ratio[n - 1] = row[n - 1] / pivot[n - 1]
    for i in range(n - 2, -1, -1):
        pivot[i] = membrane_diag + row[i] + row[i + 1] - row[i + 1] * ratio[i + 1]
        ratio[i] = row[i] / pivot[i]
    upper = [None] * n
    upper[n - 1] = jnp.where(lane == n - 1, 1.0, 0.0)
    for i in range(n - 2, -1, -1):
        upper[i] = jnp.where(lane == i, 1.0, 0.0) + ratio[i + 1] * upper[i + 1]
    result = upper[0] / pivot[0]
    inverse_ref[0:1, :] = result
    for i in range(1, n):
        result = upper[i] / pivot[i] + ratio[i] * result
        inverse_ref[i : i + 1, :] = result
    branch = (lane >= n) & (lane < n + 4)
    total = soma_diag + jnp.sum(jnp.where(branch, row[0], 0.0), axis=1, keepdims=True)
    shared = jnp.sum(jnp.where(branch, row[0] * ratio[0], 0.0), axis=1, keepdims=True)
    head = row[0][:, 0:1]
    soma_ref[0:1, :] = jnp.broadcast_to(total - shared, (1, lanes))
    soma_ref[1:2, :] = jnp.broadcast_to(head, (1, lanes))


def membrane(volts, gating, rate, cond):
    settle = jax.nn.sigmoid(2.0 * volts)
    gating = settle + (gating - settle) * jnp.exp(-rate * (1.0 + volts * volts))
    return gating, cond * gating * (volts - reversal)


def fill_table(table_ref, volts, comp_count, cell_dev):
    chunks = cell_dev // LOW
    high, low = halves(volts)
    for j in range(chunks):
        at = j * comp_count
        table_ref[at : at + comp_count, :] = high[:, j * LOW : (j + 1) * LOW]
        at += chunks * comp_count
        table_ref[at : at + comp_count, :] = low[:, j * LOW : (j + 1) * LOW]


def pick_rows(table_ref, source, comp_count, cell_dev):
    size = table_ref.shape[0] // 2
    pieces = []
    for at in range(0, source.shape[1], STEP):
        high, low = comp_digits(source[:, at : at + STEP], cell_dev, comp_count)
        found = jnp.dot(table_ref[...], hot(low, LOW), preferred_element_type=f32)
        rows = lax.broadcasted_iota(jnp.int32, (size, STEP), 0)
        both = jnp.where(rows == high, found[:size] + found[size:], 0.0)
        pieces.append(jnp.sum(both, axis=0, keepdims=True))
    return jnp.concatenate(pieces, axis=1)


def add_voxels(sums_ref, vox_ref, current_ref, block_size, devices):
    block_count = vox_ref.shape[0]
    sums_ref[...] = jnp.zeros_like(sums_ref)

    def add(c, unused):
        cols = pl.ds(pl.multiple_of(c * STEP, STEP), STEP)
        owners, voxels = [], []
        for k in range(block_count):
            index = vox_ref[k : k + 1, cols]
            rows = slice(k * block_size, (k + 1) * block_size)
            high, low = halves(jnp.sum(current_ref[rows, cols], axis=0, keepdims=True))
            mask = hits(index // LOW, devices)
            owners.append(jnp.concatenate([chosen(mask, high), chosen(mask, low)], axis=0))
            voxels.append(hot(index % LOW, LOW))
        sums_ref[...] += lax.dot_general(
            jnp.concatenate(owners, axis=1),
            jnp.concatenate(voxels, axis=1),
            LANES,
            preferred_element_type=f32,
        )
        return unused

    lax.fori_loop(0, vox_ref.shape[1] // STEP, add, 0)


def put_voxels(send_ref, sums_ref, devices, stride):
    sums = sums_ref[:devices, :] + sums_ref[devices:, :]
    for j in range(LOW // 128):
        send_ref[pl.ds(j, devices, stride=stride), :] = sums[:, j * 128 : (j + 1) * 128]


def slot_rows(values, dest_hot, rank_mask):
    parts = []
    for value in values:
        high, low = halves(value)
        parts += [chosen(rank_mask, high), chosen(rank_mask, low)]
    laid = lax.dot_general(
        jnp.concatenate(parts, axis=0), dest_hot, LANES, preferred_element_type=f32
    )
    return [
        laid[(2 * q) * CAP : (2 * q + 1) * CAP] + laid[(2 * q + 1) * CAP : (2 * q + 2) * CAP]
        for q in range(len(values))
    ]


def first_kernel(
    devices, stride,
    volts_ref, gate_ref, rate_ref, cond_ref, vox_ref,
    source_ref, route_ref, target_ref, weight_ref,
    send_ref, rank_ref, gate_out, current_out,
    table_ref, sums_ref,
):
    comp_count, cell_dev = volts_ref.shape
    rows = source_ref.shape[1]
    span = 256
    earlier = jnp.where(
        lax.broadcasted_iota(jnp.int32, (span, span), 0)
        < lax.broadcasted_iota(jnp.int32, (span, span), 1),
        1.0, 0.0,
    ).astype(bf16)
    before = jnp.zeros((devices, 1), f32)
    ranks, dests = [], []
    for at in range(0, rows, span):
        dest = hot(route_ref[:, at : at + span], devices)
        count = jnp.dot(dest, earlier, preferred_element_type=f32) + before
        full = dest.astype(f32)
        ranks.append(jnp.sum(full * count, axis=0, keepdims=True))
        before = count[:, span - 1 : span] + full[:, span - 1 : span]
        dests.append(dest)
    rank = jnp.concatenate(ranks, axis=1).astype(jnp.int32)
    rank_ref[...] = rank
    dest_hot = jnp.concatenate(dests, axis=1)
    volts = volts_ref[...]
    fill_table(table_ref, volts, comp_count, cell_dev)
    weight = weight_ref[...]
    sent = weight * pick_rows(table_ref, source_ref[...], comp_count, cell_dev)
    slots = slot_rows([target_ref[...].astype(f32), weight, sent], dest_hot, hits(rank, CAP))
    slots.append(jnp.zeros((128 - 3 * CAP, devices), f32))
    send_ref[pl.ds(LOW // 128, devices, stride=stride), :] = jnp.concatenate(slots, axis=0).T
    gating, current = membrane(volts, gate_ref[...], rate_ref[...], cond_ref[...])
    gate_out[...] = gating
    current_out[...] = current
    add_voxels(sums_ref, vox_ref, current_out, comp_count // vox_ref.shape[0], devices)
    put_voxels(send_ref, sums_ref, devices, stride)


def scatter_slots(target, values, comp_count, cell_dev):
    size = cell_dev // LOW * comp_count
    lefts, rights = [], []
    for k in range(0, CAP, 2):
        pair = lambda x: jnp.concatenate([x[k : k + 1], x[k + 1 : k + 2]], axis=1)
        high, low = comp_digits(pair(target), cell_dev, comp_count)
        mask = hits(high, size)
        parts = []
        for value in values:
            parts += [chosen(mask, half) for half in halves(pair(value))]
        lefts.append(jnp.concatenate(parts, axis=0))
        rights.append(hot(low, LOW))
    laid = lax.dot_general(
        jnp.concatenate(lefts, axis=1),
        jnp.concatenate(rights, axis=1),
        LANES,
        preferred_element_type=f32,
    )
    out = []
    for q in range(len(values)):
        total = laid[2 * q * size : (2 * q + 1) * size] + laid[(2 * q + 1) * size : (2 * q + 2) * size]
        out.append(total)
    return out


def as_cells(total, comp_count):
    chunks = total.shape[0] // comp_count
    return jnp.concatenate(
        [total[j * comp_count : (j + 1) * comp_count] for j in range(chunks)], axis=1
    )


def second_kernel(
    devices, stride, field_scale,
    recv_ref, volts_ref, stim_ref, current_ref, inverse_ref, soma_ref, resist_ref,
    solved_ref, partial_ref, weight_ref, target_ref, potential_ref,
):
    comp_count, cell_dev = volts_ref.shape
    for j in range(LOW // 128):
        own = jnp.sum(recv_ref[pl.ds(j, devices, stride=stride), :], axis=0, keepdims=True)
        potential_ref[j : j + 1, :] = resist_ref[j : j + 1, :] * own * field_scale
    slots = recv_ref[pl.ds(LOW // 128, devices, stride=stride), :].T
    target = slots[:CAP].astype(jnp.int32)
    target_ref[...] = target
    weight_total, gap = scatter_slots(
        target, [slots[CAP : 2 * CAP], slots[2 * CAP : 3 * CAP]], comp_count, cell_dev
    )
    weight_total = as_cells(weight_total, comp_count)
    weight_ref[...] = weight_total
    volts = volts_ref[...]
    gap_in = as_cells(gap, comp_count) - weight_total * volts
    rhs = membrane_diag * volts + stim_ref[...] - current_ref[...] + gap_in
    solved = jnp.dot(
        inverse_ref[:, :comp_count], rhs, precision=lax.Precision.HIGHEST,
        preferred_element_type=f32,
    )
    solved_ref[...] = solved
    partial_ref[...] = soma_ref[1:2, 0:1] * solved[0:1, :]


def next_soma(soma, stimulus, partials, total):
    partial = (partials[0] + partials[1]) + (partials[2] + partials[3])
    return (soma_diag * soma + stimulus + partial) / total


def third_kernel(
    devices, stride,
    solved_ref, p0_ref, p1_ref, p2_ref, p3_ref, soma_v_ref, soma_stim_ref,
    inverse_ref, soma_ref, gate_ref, rate_ref, cond_ref, stim_ref, weight_total_ref,
    vox_ref, source_ref, route_ref, rank_ref, weight_ref, potential_ref,
    send_ref, gate_out, soma_out, base_ref,
    table_ref, sums_ref, current_ref,
):
    comp_count, cell_dev = solved_ref.shape
    soma = next_soma(
        soma_v_ref[...], soma_stim_ref[...],
        [p0_ref[...], p1_ref[...], p2_ref[...], p3_ref[...]], soma_ref[0:1, 0:1],
    )
    soma_out[...] = soma
    volts = solved_ref[...] + soma_ref[1:2, 0:1] * inverse_ref[:, 0:1] * soma
    fill_table(table_ref, volts, comp_count, cell_dev)
    gating, current = membrane(volts, gate_ref[...], rate_ref[...], cond_ref[...])
    gate_out[...] = gating
    current_ref[...] = current
    base_ref[...] = membrane_diag * volts + stim_ref[...] - current - weight_total_ref[...] * volts
    sent = weight_ref[...] * pick_rows(table_ref, source_ref[...], comp_count, cell_dev)
    slots = slot_rows([sent], hot(route_ref[...], devices), hits(rank_ref[...], CAP))
    slots.append(jnp.zeros((128 - CAP, devices), f32))
    parts = LOW // 128
    send_ref[pl.ds(2 * parts, devices, stride=stride), :] = jnp.concatenate(slots, axis=0).T
    add_voxels(sums_ref, vox_ref, current_ref, comp_count // vox_ref.shape[0], devices)
    put_voxels(send_ref, sums_ref, devices, stride)
    for j in range(parts):
        send_ref[pl.ds(parts + j, devices, stride=stride), :] = jnp.broadcast_to(
            potential_ref[j : j + 1, :], (devices, 128)
        )


def fourth_kernel(
    devices, stride, field_scale,
    recv_ref, target_ref, base_ref, vox_ref, inverse_ref, soma_ref, resist_ref,
    solved_ref, partial_ref, potential_ref,
    rhs_ref,
):
    comp_count, cell_dev = base_ref.shape
    block_count = vox_ref.shape[0]
    block_size = comp_count // block_count
    parts = LOW // 128
    for j in range(parts):
        own = jnp.sum(recv_ref[pl.ds(j, devices, stride=stride), :], axis=0, keepdims=True)
        potential_ref[j : j + 1, :] = resist_ref[j : j + 1, :] * own * field_scale
    slots = recv_ref[pl.ds(2 * parts, devices, stride=stride), :].T
    (gap,) = scatter_slots(target_ref[...], [slots[:CAP]], comp_count, cell_dev)
    rhs_ref[...] = base_ref[...] + as_cells(gap, comp_count)
    table = jnp.concatenate(
        [recv_ref[pl.ds(parts + j, devices, stride=stride), :] for j in range(parts)], axis=1
    )
    table = jnp.concatenate(halves(table), axis=0)

    def look(c, unused):
        cols = pl.ds(pl.multiple_of(c * STEP, STEP), STEP)
        for k in range(block_count):
            index = vox_ref[k : k + 1, cols]
            found = jnp.dot(table, hot(index % LOW, LOW), preferred_element_type=f32)
            owners = lax.broadcasted_iota(jnp.int32, (devices, STEP), 0)
            both = jnp.where(owners == index // LOW, found[:devices] + found[devices:], 0.0)
            phi = jnp.sum(both, axis=0, keepdims=True)
            rows = slice(k * block_size, (k + 1) * block_size)
            rhs_ref[rows, cols] = rhs_ref[rows, cols] - ephaptic * phi
        return unused

    lax.fori_loop(0, cell_dev // STEP, look, 0)
    solved = jnp.dot(
        inverse_ref[:, :comp_count], rhs_ref[...], precision=lax.Precision.HIGHEST,
        preferred_element_type=f32,
    )
    solved_ref[...] = solved
    partial_ref[...] = soma_ref[1:2, 0:1] * solved[0:1, :]


def last_kernel(
    solved_ref, p0_ref, p1_ref, p2_ref, p3_ref, soma_v_ref, soma_stim_ref,
    inverse_ref, soma_ref, volts_ref, soma_out,
):
    soma = next_soma(
        soma_v_ref[...], soma_stim_ref[...],
        [p0_ref[...], p1_ref[...], p2_ref[...], p3_ref[...]], soma_ref[0:1, 0:1],
    )
    soma_out[...] = soma
    volts_ref[...] = solved_ref[...] + soma_ref[1:2, 0:1] * inverse_ref[:, 0:1] * soma


def call(kernel, outs, scratch=()):
    shapes = [jax.ShapeDtypeStruct(shape, dtype) for shape, dtype in outs]
    return pl.pallas_call(
        kernel, out_shape=shapes, scratch_shapes=list(scratch), compiler_params=PARAMS
    )


def bind(kernel, *sizes):
    def bound(*refs):
        kernel(*sizes, *refs)

    return bound


def exchange(send, devices):
    flat = lax.all_to_all(
        send.reshape(devices, send.size // devices), AXES, split_axis=0, concat_axis=0, tiled=True
    )
    return flat.reshape(send.shape)


def split_terms(partial, n_split):
    terms = [partial]
    for k in range(1, n_split):
        pairs = [(i, (i + k) % n_split) for i in range(n_split)]
        terms.append(lax.ppermute(partial, "split", pairs))
    return terms


def per_device(
    voltage, gate_state, stimulus, gate_rate, gate_conductance, soma_voltage, soma_stimulus,
    axial_conductance, gap_source, gap_route, gap_target, gap_conductance, vox_index, field_resist,
):
    n_split = lax.axis_size("split")
    devices = lax.axis_size("cells") * n_split
    comp_count, cell_dev = voltage.shape[1:]
    rows = gap_source.shape[0]
    vox_dev = field_resist.shape[0]
    field_scale = vox_dev / (comp_count * cell_dev)
    volts, gate, stim = voltage[0], gate_state[0], stimulus[0]
    rate, cond, vox = gate_rate[0], gate_conductance[0], vox_index[0]
    source = gap_source.reshape(1, rows)
    route = gap_route.reshape(1, rows)
    target = gap_target.reshape(1, rows)
    weight = gap_conductance.reshape(1, rows)
    soma_v = soma_voltage.reshape(1, cell_dev)
    soma_stim = soma_stimulus.reshape(1, cell_dev)
    resist = field_resist.reshape(vox_dev // 128, 128)

    own = lax.dynamic_index_in_dim(axial_conductance, lax.axis_index("split"), 0, keepdims=False)
    own = own[:, None]
    axial = jnp.concatenate(
        [
            jnp.broadcast_to(own, (comp_count, comp_count)),
            axial_conductance.T,
            jnp.broadcast_to(own, (comp_count, 128 - comp_count - n_split)),
        ],
        axis=1,
    )
    inverse, soma_consts = call(
        inverse_kernel, [((comp_count, 128), f32), ((2, 128), f32)]
    )(axial)

    full = ((comp_count, cell_dev), f32)
    line = ((1, cell_dev), f32)
    parts = vox_dev // 128
    table = pltpu.VMEM((2 * cell_dev // LOW * comp_count, LOW), bf16)
    sums = pltpu.VMEM((2 * devices, LOW), f32)

    stride = parts + 1
    send, rank, gate, current = call(
        bind(first_kernel, devices, stride),
        [((devices * stride, 128), f32), ((1, rows), jnp.int32), full, full],
        [table, sums],
    )(volts, gate, rate, cond, vox, source, route, target, weight)
    received = exchange(send, devices)
    solved, partial, weight_total, slot_target, potential = call(
        bind(second_kernel, devices, stride, field_scale),
        [full, line, full, ((CAP, devices), jnp.int32), ((parts, 128), f32)],
    )(received, volts, stim, current, inverse, soma_consts, resist)

    stride = 2 * parts + 1
    send, gate, soma, base = call(
        bind(third_kernel, devices, stride),
        [((devices * stride, 128), f32), full, line, full],
        [table, sums, pltpu.VMEM((comp_count, cell_dev), f32)],
    )(
        solved, *split_terms(partial, n_split), soma_v, soma_stim, inverse, soma_consts,
        gate, rate, cond, stim, weight_total, vox, source, route, rank, weight, potential,
    )
    received = exchange(send, devices)
    solved, partial, potential = call(
        bind(fourth_kernel, devices, stride, field_scale),
        [full, line, ((parts, 128), f32)],
        [pltpu.VMEM((comp_count, cell_dev), f32)],
    )(received, slot_target, base, vox, inverse, soma_consts, resist)

    volts, soma = call(last_kernel, [full, line])(
        solved, *split_terms(partial, n_split), soma, soma_stim, inverse, soma_consts
    )
    return volts[None], gate[None], soma.reshape(cell_dev), potential.reshape(vox_dev)


def solution(mesh):
    wide = P("split", None, "cells")
    every = P(AXES)
    in_specs = (
        wide, wide, wide, wide, wide, P("cells"), P("cells"), P(),
        every, P(AXES, None), every, every, wide, every,
    )
    out_specs = (wide, wide, P("cells"), every)
    return jax.shard_map(
        per_device, mesh=mesh, in_specs=in_specs, out_specs=out_specs, check_vma=False
    )
```

time: 548 us -> 97.7 us (0.18); the launches traced: 540 us -> 97.1 us
  matrix products: 196 us -> 0 us
  waiting for transfers between devices: 125 us -> 19.7 us
  blocking collectives: 92.5 us -> 18.4 us
  other arithmetic: 36.6 us -> 0.08 us
  Pallas kernels: 0 us -> 32.8 us
  local copies, waits for them, and re-layouts: 36 us -> 8.71 us
  starting transfers between devices: 34.5 us -> 16.6 us
  between operations: 16.1 us -> 0.73 us
    dot_general x71 -> x0, matrix products: 196 us -> none  [the longest x44 131 us: accumulate(): jnp.dot(weighted, low_hot, precision=lax.Precision.HIGHEST)]
    unnamed x2 -> x0, waiting for transfers between devices: 120 us -> none
    all_gather x1 -> x0, blocking collectives: 60.3 us -> none  [per_device(): lax.all_gather(potential_own, ('cells', 'split'), axis=0, tiled=True)]
    pallas_call x0 -> x6, Pallas kernels: none -> 32.8 us  [the longest x1 9.04 us: per_device(): call(bind(first_kernel, devices, stride), [((devices * stride, 128), f32)...]
    psum x2 -> x0, blocking collectives: 32.2 us -> none  [per_device(): partial_value = lax.psum(head_axial * solved[0], 'split')]
    scatter x3 -> x0, local copies, waits for them, and re-layouts: 24.8 us -> none  [the longest x1 8.36 us: per_device(): jnp.zeros((devices * slot_count,), jnp.float32).at[position]]
    all_to_all x4 -> x1, starting transfers between devices: 34.4 us -> 11.1 us  [exchange(): lax.all_to_all(send.reshape(devices, send.size // devices), AXES, split_a...]
    another operation x9 -> x0, other arithmetic: 22.3 us -> none  [the longest x3 11.9 us: single_inverse(): factor = jnp.linalg.cholesky(matrix)]
  transfers between devices with their start and end apart: 5 -> 7, of which waited for: 2 -> 7; matrix products, arithmetic and copies ran while one was open for 20% -> 0% of each run, Pallas kernels for 0% -> 0%
where the time goes in v1:
time: 97.7 us; the launch traced here: 97.1 us
  Pallas kernels  32.8 us (34%)
  waiting for transfers between devices  19.7 us (20%)
  blocking collectives  18.4 us (19%)
  starting transfers between devices  16.6 us (17%)
  local copies, waits for them, and re-layouts  8.71 us (9%)
    all_to_all x1, blocking collectives, exchange(): lax.all_to_all(send.reshape(devices, send.size // devices), AXES, split_a...  18.4 us
    all_to_all x1, starting transfers between devices, exchange(): lax.all_to_all(send.reshape(devices, send.size // devices), AXES, split_a...  11.1 us
    ppermute x6, waiting for transfers between devices, split_terms(): terms.append(lax.ppermute(partial, 'split', pairs))  9.89 us
    all_to_all x1, waiting for transfers between devices, exchange(): lax.all_to_all(send.reshape(devices, send.size // devices), AXES, split_a...  9.79 us
    pallas_call x1, Pallas kernels, per_device(): call(bind(first_kernel, devices, stride), [((devices * stride, 128), f32)...  9.04 us
    pallas_call x1, Pallas kernels, per_device(): call(bind(fourth_kernel, devices, stride, field_scale), [full, line, ((pa...  8.94 us
    unnamed x39, local copies, waits for them, and re-layouts  8.57 us
    pallas_call x1, Pallas kernels, per_device(): call(bind(third_kernel, devices, stride), [((devices * stride, 128), f32)...  8.23 us
  transfers between devices with their start and end apart: 7, of which 7 were waited for; matrix products, arithmetic and copies ran while one was open for 0% of the time, Pallas kernels for 0%

profile of v1, /device:TPU:0, one launch (start us, length us, event | category | flops | bytes accessed | tf_op | source)
XLA Modules:
  0.0 97.1 jit_solution(13787204823442870585)
XLA Ops:
  0.7 0.7 copy-done.12
  1.3 1.0 %copy-done = f32[1,32,4096]{2,1,0:T(8,128)S(1)} copy-done((f32[1,32,4096]{2,1,0:T(8,128)S(1)}, f32[1,32,4096]{2,1,0:T(8,128)}, u32[]{:S(2)}) %copy-start) | copy-done | bytes 524312
  2.4 1.0 %copy-done.2 = f32[1,32,4096]{2,1,0:T(8,128)S(1)} copy-done((f32[1,32,4096]{2,1,0:T(8,128)S(1)}, f32[1,32,4096]{2,1,0:T(8,128)}, u32[]{:S(2)}) %copy-start.2) | copy-done | bytes 524312
  3.4 1.0 %copy-done.4 = f32[1,32,4096]{2,1,0:T(8,128)S(1)} copy-done((f32[1,32,4096]{2,1,0:T(8,128)S(1)}, f32[1,32,4096]{2,1,0:T(8,128)}, u32[]{:S(2)}) %copy-start.4) | copy-done | bytes 524312
  4.5 0.8 copy-done.7
  5.3 1.0 %copy-done.9 = f32[1,32,4096]{2,1,0:T(8,128)S(1)} copy-done((f32[1,32,4096]{2,1,0:T(8,128)S(1)}, f32[1,32,4096]{2,1,0:T(8,128)}, u32[]{:S(2)}) %copy-start.9) | copy-done | bytes 524312
  6.4 0.7 copy-done.13
  7.1 0.7 copy-done.16
  7.8 9.0 %shard_map.165 = (f32[640,128]{1,0:T(8,128)}, s32[1,2048]{1,0:T(1,128)S(1)}, f32[32,4096]{1,0:T(8,128)S(1)}, f32[32,4096]{1,0:T(8,128)S(1)}) custom-call(f32[32,4096]{1,0:T(8,128)S(1)} %bitcast.25, f32[32,4096]{1,0:T(8,128)S(1)} %bitcast.38, f32[32,4096]{1,0:T(8,128)S(1)} %bitcast.27, f32[32,4096]{1,0:T(8,128)S(1)} %bitcast.29, s32[4,4096]{1,0:T(4,128)S(1)} %bitcast.34, ...), custom_call_target="tpu_custom_call" | custom-call | tf_op jit(solution)/shard_map/pallas_call | solution.py:416
  16.8 11.1 %all-to-all-start = ((f32[128,1,640]{2,1,0:T(1,128)}), f32[128,1,640]{2,1,0:T(1,128)S(1)}, u32[]{:S(2)}, u32[]{:S(2)}) async-start(f32[128,1,640]{2,1,0:T(1,128)} %bitcast.9), calls=%async_computation | async-start | bytes 655360 | tf_op jit(solution)/shard_map/all_to_all | solution.py:361
  28.0 0.7 copy-done.18
  28.6 0.1 copy.20
  28.7 0.1 broadcast_in_dim.21
  28.9 0.1 pad_maximum_fusion.axial_ref
  29.0 0.4 shard_map.166
  29.4 9.8 %all-to-all-done = f32[128,1,640]{2,1,0:T(1,128)S(1)} async-done(((f32[128,1,640]{2,1,0:T(1,128)}), f32[128,1,640]{2,1,0:T(1,128)S(1)}, u32[]{:S(2)}, u32[]{:S(2)}) %all-to-all-start) | async-done | bytes 327712 | tf_op jit(solution)/shard_map/all_to_all | solution.py:361
  39.2 0.7 copy-done.17
  39.9 5.2 %shard_map.167 = (f32[32,4096]{1,0:T(8,128)S(1)}, f32[1,4096]{1,0:T(1,128)S(1)}, f32[32,4096]{1,0:T(8,128)S(1)}, s32[32,128]{1,0:T(8,128)S(1)}, f32[4,128]{1,0:T(4,128)S(1)}) custom-call(f32[640,128]{1,0:T(8,128)S(1)} %bitcast.33, f32[32,4096]{1,0:T(8,128)S(1)} %bitcast.26, f32[32,4096]{1,0:T(8,128)S(1)} %bitcast.31, ...), custom_call_target="tpu_custom_call" | custom-call | tf_op jit(solution)/shard_map/pallas_call | solution.py:422
  45.1 1.6 %collective-permute-start.2 = (f32[1,4096]{1,0:T(1,128)S(1)}, f32[1,4096]{1,0:T(1,128)S(1)}, u32[]{:S(2)}, u32[]{:S(2)}) collective-permute-start(f32[1,4096]{1,0:T(1,128)S(1)} %get-tuple-element.29.refs_1_), channel_id=1, source_target_pairs={{0,3},{1,0},{2,1},{3,2},{4,7},{5,4},{6,5},{7,6},{8,11},{9,8},{10,9... | collective-permute-start | bytes 49160 | tf_op jit(solution)/shard_map/ppermute | solution.py:371
  46.7 1.2 %collective-permute-start.1 = (f32[1,4096]{1,0:T(1,128)S(1)}, f32[1,4096]{1,0:T(1,128)S(1)}, u32[]{:S(2)}, u32[]{:S(2)}) collective-permute-start(f32[1,4096]{1,0:T(1,128)S(1)} %get-tuple-element.29.refs_1_), channel_id=1, source_target_pairs={{0,2},{1,3},{2,0},{3,1},{4,6},{5,7},{6,4},{7,5},{8,10},{9,11},{10,... | collective-permute-start | bytes 49160 | tf_op jit(solution)/shard_map/ppermute | solution.py:371
  47.9 1.0 %collective-permute-done.2.refs_4_ = f32[1,4096]{1,0:T(1,128)S(1)} collective-permute-done((f32[1,4096]{1,0:T(1,128)S(1)}, f32[1,4096]{1,0:T(1,128)S(1)}, u32[]{:S(2)}, u32[]{:S(2)}) %collective-permute-start.2) | collective-permute-done | bytes 16416 | tf_op jit(solution)/shard_map/ppermute | solution.py:371
  48.9 3.0 %collective-permute-done.1.refs_3_ = f32[1,4096]{1,0:T(1,128)S(1)} collective-permute-done((f32[1,4096]{1,0:T(1,128)S(1)}, f32[1,4096]{1,0:T(1,128)S(1)}, u32[]{:S(2)}, u32[]{:S(2)}) %collective-permute-start.1) | collective-permute-done | bytes 16416 | tf_op jit(solution)/shard_map/ppermute | solution.py:371
  52.0 0.9 collective-permute-done.refs_2_
  52.9 8.2 %shard_map.168 = (f32[1152,128]{1,0:T(8,128)S(1)}, f32[32,4096]{1,0:T(8,128)}, f32[1,4096]{1,0:T(1,128)S(1)}, f32[32,4096]{1,0:T(8,128)S(1)}) custom-call(f32[32,4096]{1,0:T(8,128)S(1)} %get-tuple-element.28.refs_0_, f32[1,4096]{1,0:T(1,128)S(1)} %get-tuple-element.29.refs_1_, f32[1,4096]{1,0:T(1,128)S(1)} %collective-permute-done.refs_2_, ...), custom_call_target="tpu_custom_call" | custom-call | tf_op jit(solution)/shard_map/pallas_call | solution.py:428
  61.1 18.4 %all_to_all.18 = f32[128,1,1152]{2,1,0:T(1,128)S(1)} all-to-all(f32[128,1,1152]{2,1,0:T(1,128)S(1)} %bitcast.37), channel_id=1, replica_groups=mesh['cells'=32,'split'=4] {'cells','split'}, dimensions={0} | all-to-all | bytes 1179648 | tf_op jit(solution)/shard_map/all_to_all | solution.py:361
  79.5 8.9 %shard_map.169 = (f32[32,4096]{1,0:T(8,128)S(1)}, f32[1,4096]{1,0:T(1,128)S(1)}, f32[4,128]{1,0:T(4,128)}) custom-call(f32[1152,128]{1,0:T(8,128)S(1)} %bitcast.24, s32[32,128]{1,0:T(8,128)S(1)} %get-tuple-element.35.refs_1_, f32[32,4096]{1,0:T(8,128)S(1)} %get-tuple-element.36.refs_2_, s32[4,4096]{1,0:T(4,128)S(1)} %bitcast.36, ...), custom_call_target="tpu_custom_call" | custom-call | tf_op jit(solution)/shard_map/pallas_call | solution.py:437
  88.4 1.6 %collective-permute-start.5 = (f32[1,4096]{1,0:T(1,128)S(1)}, f32[1,4096]{1,0:T(1,128)S(1)}, u32[]{:S(2)}, u32[]{:S(2)}) collective-permute-start(f32[1,4096]{1,0:T(1,128)S(1)} %get-tuple-element.38.p0_ref), channel_id=1, source_target_pairs={{0,3},{1,0},{2,1},{3,2},{4,7},{5,4},{6,5},{7,6},{8,11},{9,8},{10,9... | collective-permute-start | bytes 49160 | tf_op jit(solution)/shard_map/ppermute | solution.py:371
  90.0 1.2 %collective-permute-start.4 = (f32[1,4096]{1,0:T(1,128)S(1)}, f32[1,4096]{1,0:T(1,128)S(1)}, u32[]{:S(2)}, u32[]{:S(2)}) collective-permute-start(f32[1,4096]{1,0:T(1,128)S(1)} %get-tuple-element.38.p0_ref), channel_id=1, source_target_pairs={{0,2},{1,3},{2,0},{3,1},{4,6},{5,7},{6,4},{7,5},{8,10},{9,11},{10,... | collective-permute-start | bytes 49160 | tf_op jit(solution)/shard_map/ppermute | solution.py:371
  91.2 1.1 %collective-permute-done.5.p3_ref = f32[1,4096]{1,0:T(1,128)S(1)} collective-permute-done((f32[1,4096]{1,0:T(1,128)S(1)}, f32[1,4096]{1,0:T(1,128)S(1)}, u32[]{:S(2)}, u32[]{:S(2)}) %collective-permute-start.5) | collective-permute-done | bytes 16416 | tf_op jit(solution)/shard_map/ppermute | solution.py:371
  92.2 3.0 %collective-permute-done.4.p2_ref = f32[1,4096]{1,0:T(1,128)S(1)} collective-permute-done((f32[1,4096]{1,0:T(1,128)S(1)}, f32[1,4096]{1,0:T(1,128)S(1)}, u32[]{:S(2)}, u32[]{:S(2)}) %collective-permute-start.4) | collective-permute-done | bytes 16416 | tf_op jit(solution)/shard_map/ppermute | solution.py:371
  95.3 0.9 collective-permute-done.3.p1_ref
  96.1 0.9 shard_map.170
  (32 shorter events, 0.1 us)
Async XLA Ops:
  0.6 0.7 copy-start.12
  0.6 0.7 copy-start.11
  1.3 1.0 %copy-start = (f32[1,32,4096]{2,1,0:T(8,128)S(1)}, f32[1,32,4096]{2,1,0:T(8,128)}, u32[]{:S(2)}) copy-start(f32[1,32,4096]{2,1,0:T(8,128)} %param.14) | copy-start | bytes 1572868
  2.4 1.0 %copy-start.2 = (f32[1,32,4096]{2,1,0:T(8,128)S(1)}, f32[1,32,4096]{2,1,0:T(8,128)}, u32[]{:S(2)}) copy-start(f32[1,32,4096]{2,1,0:T(8,128)} %param.17) | copy-start | bytes 1572868
  3.4 1.0 %copy-start.4 = (f32[1,32,4096]{2,1,0:T(8,128)S(1)}, f32[1,32,4096]{2,1,0:T(8,128)}, u32[]{:S(2)}) copy-start(f32[1,32,4096]{2,1,0:T(8,128)} %param.18) | copy-start | bytes 1572868
  4.5 0.8 copy-start.7
  5.3 1.0 %copy-start.9 = (f32[1,32,4096]{2,1,0:T(8,128)S(1)}, f32[1,32,4096]{2,1,0:T(8,128)}, u32[]{:S(2)}) copy-start(f32[1,32,4096]{2,1,0:T(8,128)} %param.15) | copy-start | bytes 1572868
  6.4 0.7 copy-start.13
  7.1 0.7 copy-start.16
  7.8 31.4 %copy-start.6 = (f32[1,32,4096]{2,1,0:T(8,128)S(1)}, f32[1,32,4096]{2,1,0:T(8,128)}, u32[]{:S(2)}) copy-start(f32[1,32,4096]{2,1,0:T(8,128)} %param.16) | copy-start | bytes 1572868
  16.8 22.4 %copy-start.1 = (f32[1,32,4096]{2,1,0:T(8,128)S(1)}, f32[1,32,4096]{2,1,0:T(8,128)}, u32[]{:S(2)}) copy-start(f32[1,32,4096]{2,1,0:T(8,128)} %param.14) | copy-start | bytes 1572868
  16.8 22.4 %all-to-all-start = ((f32[128,1,640]{2,1,0:T(1,128)}), f32[128,1,640]{2,1,0:T(1,128)S(1)}, u32[]{:S(2)}, u32[]{:S(2)}) async-start(f32[128,1,640]{2,1,0:T(1,128)} %bitcast.9), calls=%async_computation | async-start | bytes 655360 | tf_op jit(solution)/shard_map/all_to_all | solution.py:361
  27.9 0.7 copy-start.18
  39.2 0.7 copy-start.17
  39.8 13.0 %copy-start.3 = (f32[1,32,4096]{2,1,0:T(8,128)S(1)}, f32[1,32,4096]{2,1,0:T(8,128)}, u32[]{:S(2)}) copy-start(f32[1,32,4096]{2,1,0:T(8,128)} %param.17) | copy-start | bytes 1572868
  39.9 13.0 %copy-start.5 = (f32[1,32,4096]{2,1,0:T(8,128)S(1)}, f32[1,32,4096]{2,1,0:T(8,128)}, u32[]{:S(2)}) copy-start(f32[1,32,4096]{2,1,0:T(8,128)} %param.18) | copy-start | bytes 1572868
  39.9 13.0 %copy-start.8 = (s32[1,4,4096]{2,1,0:T(4,128)S(1)}, s32[1,4,4096]{2,1,0:T(4,128)}, u32[]{:S(2)}) copy-start(s32[1,4,4096]{2,1,0:T(4,128)} %param.26) | copy-start | bytes 196612
  39.9 13.0 %copy-start.10 = (f32[4096]{0:T(1024)S(1)}, f32[4096]{0:T(1024)}, u32[]{:S(2)}) copy-start(f32[4096]{0:T(1024)} %param.20) | copy-start | bytes 49156
  39.9 13.0 %copy-start.15 = (f32[4096]{0:T(1024)S(1)}, f32[4096]{0:T(1024)}, u32[]{:S(2)}) copy-start(f32[4096]{0:T(1024)} %param.19) | copy-start | bytes 49156
  45.1 7.7 %copy-start.14 = (f32[2048]{0:T(1024)S(1)}, f32[2048]{0:T(1024)}, u32[]{:S(2)}) copy-start(f32[2048]{0:T(1024)} %param.25) | copy-start | bytes 24580
  45.1 3.8 %collective-permute-start.2 = (f32[1,4096]{1,0:T(1,128)S(1)}, f32[1,4096]{1,0:T(1,128)S(1)}, u32[]{:S(2)}, u32[]{:S(2)}) collective-permute-start(f32[1,4096]{1,0:T(1,128)S(1)} %get-tuple-element.29.refs_1_), channel_id=1, source_target_pairs={{0,3},{1,0},{2,1},{3,2},{4,7},{5,4},{6,5},{7,6},{8,11},{9,8},{10,9... | collective-permute-start | bytes 49160 | tf_op jit(solution)/shard_map/ppermute | solution.py:371
  46.7 5.2 %collective-permute-start.1 = (f32[1,4096]{1,0:T(1,128)S(1)}, f32[1,4096]{1,0:T(1,128)S(1)}, u32[]{:S(2)}, u32[]{:S(2)}) collective-permute-start(f32[1,4096]{1,0:T(1,128)S(1)} %get-tuple-element.29.refs_1_), channel_id=1, source_target_pairs={{0,2},{1,3},{2,0},{3,1},{4,6},{5,7},{6,4},{7,5},{8,10},{9,11},{10,... | collective-permute-start | bytes 49160 | tf_op jit(solution)/shard_map/ppermute | solution.py:371
  47.9 4.9 %collective-permute-start = (f32[1,4096]{1,0:T(1,128)S(1)}, f32[1,4096]{1,0:T(1,128)S(1)}, u32[]{:S(2)}, u32[]{:S(2)}) collective-permute-start(f32[1,4096]{1,0:T(1,128)S(1)} %get-tuple-element.29.refs_1_), channel_id=1, source_target_pairs={{0,1},{1,2},{2,3},{3,0},{4,5},{5,6},{6,7},{7,4},{8,9},{9,10},{10,1... | collective-permute-start | bytes 49160 | tf_op jit(solution)/shard_map/ppermute | solution.py:371
  88.4 3.8 %collective-permute-start.5 = (f32[1,4096]{1,0:T(1,128)S(1)}, f32[1,4096]{1,0:T(1,128)S(1)}, u32[]{:S(2)}, u32[]{:S(2)}) collective-permute-start(f32[1,4096]{1,0:T(1,128)S(1)} %get-tuple-element.38.p0_ref), channel_id=1, source_target_pairs={{0,3},{1,0},{2,1},{3,2},{4,7},{5,4},{6,5},{7,6},{8,11},{9,8},{10,9... | collective-permute-start | bytes 49160 | tf_op jit(solution)/shard_map/ppermute | solution.py:371
  90.0 5.2 %collective-permute-start.4 = (f32[1,4096]{1,0:T(1,128)S(1)}, f32[1,4096]{1,0:T(1,128)S(1)}, u32[]{:S(2)}, u32[]{:S(2)}) collective-permute-start(f32[1,4096]{1,0:T(1,128)S(1)} %get-tuple-element.38.p0_ref), channel_id=1, source_target_pairs={{0,2},{1,3},{2,0},{3,1},{4,6},{5,7},{6,4},{7,5},{8,10},{9,11},{10,... | collective-permute-start | bytes 49160 | tf_op jit(solution)/shard_map/ppermute | solution.py:371
  91.2 4.9 %collective-permute-start.3 = (f32[1,4096]{1,0:T(1,128)S(1)}, f32[1,4096]{1,0:T(1,128)S(1)}, u32[]{:S(2)}, u32[]{:S(2)}) collective-permute-start(f32[1,4096]{1,0:T(1,128)S(1)} %get-tuple-element.38.p0_ref), channel_id=1, source_target_pairs={{0,1},{1,2},{2,3},{3,0},{4,5},{5,6},{6,7},{7,4},{8,9},{9,10},{10,1... | collective-permute-start | bytes 49160 | tf_op jit(solution)/shard_map/ppermute | solution.py:371

commit v2 on v1

v2 whole, which is shorter than its diff:
```python
import jax
import jax.numpy as jnp
from jax import lax
from jax.experimental import pallas as pl
from jax.experimental.pallas import tpu as pltpu
from jax.sharding import PartitionSpec as P

SUB = 2
CAP = 32
LOW = 512
STEP = 512

membrane_diag = 4.0
soma_diag = 8.0
reversal = -1.0
ephaptic = 0.5

f32 = jnp.float32
bf16 = jnp.bfloat16
AXES = ("cells", "split")
VMEM_BYTES = 48 * 2**20
LANES = (((1,), (1,)), ((), ()))


def halves(x):
    high = x.astype(bf16)
    return high, (x - high.astype(f32)).astype(bf16)


def hits(row, size):
    rows = lax.broadcasted_iota(jnp.int16, (size, row.shape[1]), 0)
    return rows == row.astype(jnp.int16)


def chosen(mask, row):
    return jnp.where(mask, row, jnp.zeros((), bf16))


def hot(row, size):
    return jnp.where(hits(row, size), jnp.ones((), bf16), jnp.zeros((), bf16))


def comp_digits(index, cell_dev, comp_count):
    chunks = cell_dev // LOW
    low = index % LOW
    chunk = (index // LOW) % chunks
    return chunk * comp_count + index // cell_dev, low


def write_inverse(axial, branch, inverse_ref, soma_ref):
    branches, n = axial.shape
    lanes = 128
    index = lax.broadcasted_iota(jnp.int32, (lanes, n), 0)
    table = jnp.zeros((lanes, n), f32)
    for b in range(branches):
        mine = (index == n + b) | ((index < n) | (index >= n + branches)) & (branch == b)
        table = jnp.where(mine, axial[b : b + 1, :], table)
    table = jnp.concatenate([table, jnp.zeros((lanes, lanes - n), f32)], axis=1).T
    row = [table[i : i + 1, :] for i in range(n)]
    lane = lax.broadcasted_iota(jnp.int32, (1, lanes), 1)
    pivot = [None] * n
    ratio = [None] * n
    pivot[n - 1] = membrane_diag + row[n - 1]
    ratio[n - 1] = row[n - 1] / pivot[n - 1]
    for i in range(n - 2, -1, -1):
        pivot[i] = membrane_diag + row[i] + row[i + 1] - row[i + 1] * ratio[i + 1]
        ratio[i] = row[i] / pivot[i]
    upper = [None] * n
    upper[n - 1] = jnp.where(lane == n - 1, 1.0, 0.0)
    for i in range(n - 2, -1, -1):
        upper[i] = jnp.where(lane == i, 1.0, 0.0) + ratio[i + 1] * upper[i + 1]
    result = upper[0] / pivot[0]
    inverse_ref[0:1, :] = result
    for i in range(1, n):
        result = upper[i] / pivot[i] + ratio[i] * result
        inverse_ref[i : i + 1, :] = result
    each = (lane >= n) & (lane < n + branches)
    total = soma_diag + jnp.sum(jnp.where(each, row[0], 0.0), axis=1, keepdims=True)
    shared = jnp.sum(jnp.where(each, row[0] * ratio[0], 0.0), axis=1, keepdims=True)
    soma_ref[0:1, :] = jnp.broadcast_to(total - shared, (1, lanes))
    soma_ref[1:2, :] = jnp.broadcast_to(row[0][:, 0:1], (1, lanes))


def membrane(volts, gating, rate, cond):
    settle = jax.nn.sigmoid(2.0 * volts)
    gating = settle + (gating - settle) * jnp.exp(-rate * (1.0 + volts * volts))
    return gating, cond * gating * (volts - reversal)


def fill_table(table_ref, volts, comp_count, cell_dev):
    chunks = cell_dev // LOW
    high, low = halves(volts)
    for j in range(chunks):
        at = j * comp_count
        table_ref[at : at + comp_count, :] = high[:, j * LOW : (j + 1) * LOW]
        at += chunks * comp_count
        table_ref[at : at + comp_count, :] = low[:, j * LOW : (j + 1) * LOW]


def pick_rows(table_ref, source, comp_count, cell_dev):
    size = table_ref.shape[0] // 2
    pieces = []
    for at in range(0, source.shape[1], STEP):
        high, low = comp_digits(source[:, at : at + STEP], cell_dev, comp_count)
        found = jnp.dot(table_ref[...], hot(low, LOW), preferred_element_type=f32)
        rows = lax.broadcasted_iota(jnp.int32, (size, STEP), 0)
        both = jnp.where(rows == high, found[:size] + found[size:], 0.0)
        pieces.append(jnp.sum(both, axis=0, keepdims=True))
    return jnp.concatenate(pieces, axis=1)


def put_voxels(send_ref, vox, current, devices, stride):
    block_count = vox.shape[0]
    block_size = current.shape[0] // block_count
    owners, voxels = [], []
    for k in range(block_count):
        index = vox[k : k + 1, :]
        rows = slice(k * block_size, (k + 1) * block_size)
        high, low = halves(jnp.sum(current[rows], axis=0, keepdims=True))
        mask = hits(index // LOW, devices)
        owners.append(jnp.concatenate([chosen(mask, high), chosen(mask, low)], axis=0))
        voxels.append(hot(index % LOW, LOW))
    sums = lax.dot_general(
        jnp.concatenate(owners, axis=1),
        jnp.concatenate(voxels, axis=1),
        LANES,
        preferred_element_type=f32,
    )
    sums = sums[:devices] + sums[devices:]
    for j in range(LOW // 128):
        send_ref[pl.ds(j, devices, stride=stride), :] = sums[:, j * 128 : (j + 1) * 128]


def slot_rows(values, dest_hot, rank_mask):
    parts = []
    for value in values:
        high, low = halves(value)
        parts += [chosen(rank_mask, high), chosen(rank_mask, low)]
    laid = lax.dot_general(
        jnp.concatenate(parts, axis=0), dest_hot, LANES, preferred_element_type=f32
    )
    return [
        laid[(2 * q) * CAP : (2 * q + 1) * CAP] + laid[(2 * q + 1) * CAP : (2 * q + 2) * CAP]
        for q in range(len(values))
    ]


def first_kernel(
    devices, stride,
    volts_hbm, rate_hbm, cond_hbm, stim_hbm, vox_hbm, source_hbm, route_hbm, weight_hbm,
    soma_v_hbm, soma_stim_hbm, resist_hbm, gate_hbm, target_hbm, axial_hbm,
    volts_ref, rate_ref, cond_ref, stim_ref, vox_ref, source_ref, route_ref, weight_ref,
    soma_v_ref, soma_stim_ref, resist_ref,
    send_ref, rank_ref, gate_out, current_out, inverse_ref, soma_ref,
    gate_ref, target_ref, axial_ref, table_ref, sems,
):
    pairs = [
        (axial_hbm, axial_ref), (route_hbm, route_ref), (volts_hbm, volts_ref),
        (source_hbm, source_ref), (target_hbm, target_ref), (weight_hbm, weight_ref),
        (gate_hbm, gate_ref), (rate_hbm, rate_ref), (cond_hbm, cond_ref), (vox_hbm, vox_ref),
        (stim_hbm, stim_ref), (soma_v_hbm, soma_v_ref), (soma_stim_hbm, soma_stim_ref),
        (resist_hbm, resist_ref),
    ]
    copies = [pltpu.make_async_copy(a, b, sems.at[i]) for i, (a, b) in enumerate(pairs)]
    for copy in copies:
        copy.start()
    comp_count, cell_dev = volts_ref.shape
    rows = source_ref.shape[1]
    copies[0].wait()
    write_inverse(axial_ref[...], lax.axis_index("split"), inverse_ref, soma_ref)
    span = 256
    earlier = jnp.where(
        lax.broadcasted_iota(jnp.int32, (span, span), 0)
        < lax.broadcasted_iota(jnp.int32, (span, span), 1),
        1.0, 0.0,
    ).astype(bf16)
    before = jnp.zeros((devices, 1), f32)
    ranks, dests = [], []
    copies[1].wait()
    for at in range(0, rows, span):
        dest = hot(route_ref[:, at : at + span], devices)
        count = jnp.dot(dest, earlier, preferred_element_type=f32) + before
        full = dest.astype(f32)
        ranks.append(jnp.sum(full * count, axis=0, keepdims=True))
        before = count[:, span - 1 : span] + full[:, span - 1 : span]
        dests.append(dest)
    rank = jnp.concatenate(ranks, axis=1).astype(jnp.int32)
    rank_ref[...] = rank
    dest_hot = jnp.concatenate(dests, axis=1)
    for copy in copies[2:6]:
        copy.wait()
    volts = volts_ref[...]
    fill_table(table_ref, volts, comp_count, cell_dev)
    weight = weight_ref[...]
    sent = weight * pick_rows(table_ref, source_ref[...], comp_count, cell_dev)
    slots = slot_rows([target_ref[...].astype(f32), weight, sent], dest_hot, hits(rank, CAP))
    slots.append(jnp.zeros((128 - 3 * CAP, devices), f32))
    send_ref[pl.ds(LOW // 128, devices, stride=stride), :] = jnp.concatenate(slots, axis=0).T
    for copy in copies[6:10]:
        copy.wait()
    gating, current = membrane(volts, gate_ref[...], rate_ref[...], cond_ref[...])
    gate_out[...] = gating
    current_out[...] = current
    put_voxels(send_ref, vox_ref[...], current, devices, stride)
    for copy in copies[10:]:
        copy.wait()


def wide(slots):
    return jnp.concatenate([slots[k : k + 1] for k in range(slots.shape[0])], axis=1)


def add_heads(values, target, cell_dev):
    size = cell_dev // 128
    cell = target % cell_dev
    high, low = halves(values)
    mask = hits(cell // 128, size)
    left = jnp.concatenate([chosen(mask, high), chosen(mask, low)], axis=0)
    laid = lax.dot_general(left, hot(cell % 128, 128), LANES, preferred_element_type=f32)
    return wide(laid[:size] + laid[size:])


def add_slots(values, target, comp_count, cell_dev):
    size = cell_dev // LOW * comp_count
    row, column = comp_digits(target, cell_dev, comp_count)
    high, low = halves(values)
    mask = hits(row, size)
    left = jnp.concatenate([chosen(mask, high), chosen(mask, low)], axis=0)
    laid = lax.dot_general(left, hot(column, LOW), LANES, preferred_element_type=f32)
    return as_cells(laid[:size] + laid[size:], comp_count)


def as_cells(total, comp_count):
    chunks = total.shape[0] // comp_count
    return jnp.concatenate(
        [total[j * comp_count : (j + 1) * comp_count] for j in range(chunks)], axis=1
    )


def head_term(inverse_ref, rhs):
    return jnp.sum(inverse_ref[:, 0:1] * rhs, axis=0, keepdims=True)


def second_kernel(
    devices, stride, field_scale,
    recv_ref, volts_ref, stim_ref, current_ref, inverse_ref, soma_ref, resist_ref,
    base_ref, partial_ref, target_ref, weight_ref, factor_ref, gap_ref, potential_ref,
    table_ref,
):
    comp_count, cell_dev = volts_ref.shape
    slots = recv_ref[pl.ds(LOW // 128, devices, stride=stride), :].T
    target = wide(slots[:CAP].astype(jnp.int32))
    target_ref[...] = target
    weight = wide(slots[CAP : 2 * CAP])
    weight_ref[...] = weight
    volts = volts_ref[...]
    base = membrane_diag * volts + stim_ref[...] - current_ref[...]
    base_ref[...] = base
    comps = lax.broadcasted_iota(jnp.int32, (comp_count, CAP * devices), 0)
    factor = jnp.sum(
        jnp.where(comps == target // cell_dev, inverse_ref[:, 0:1], 0.0),
        axis=0, keepdims=True,
    )
    factor_ref[...] = factor
    fill_table(table_ref, volts, comp_count, cell_dev)
    here = pick_rows(table_ref, target, comp_count, cell_dev)
    gap = wide(slots[2 * CAP : 3 * CAP]) - weight * here
    gap_ref[...] = gap
    first = head_term(inverse_ref, base) + add_heads(factor * gap, target, cell_dev)
    partial_ref[...] = soma_ref[1:2, 0:1] * first
    for j in range(LOW // 128):
        own = jnp.sum(recv_ref[pl.ds(j, devices, stride=stride), :], axis=0, keepdims=True)
        potential_ref[j : j + 1, :] = resist_ref[j : j + 1, :] * own * field_scale


def solve(inverse_ref, rhs):
    return jnp.dot(
        inverse_ref[:, : rhs.shape[0]], rhs, precision=lax.Precision.HIGHEST,
        preferred_element_type=f32,
    )


def solve_kernel(base_ref, target_ref, gap_ref, inverse_ref, solved_ref):
    comp_count, cell_dev = base_ref.shape
    gap_in = add_slots(gap_ref[...], target_ref[...], comp_count, cell_dev)
    solved_ref[...] = solve(inverse_ref, base_ref[...] + gap_in)


def pick_kernel(table_ref, target_ref, cells_ref, here_ref):
    comp_count, cell_dev = cells_ref.shape
    here_ref[...] = pick_rows(table_ref, target_ref[...], comp_count, cell_dev)


def next_soma(soma, stimulus, partials, total):
    partial = (partials[0] + partials[1]) + (partials[2] + partials[3])
    return (soma_diag * soma + stimulus + partial) / total


def third_kernel(
    devices, stride,
    solved_ref, p0_ref, p1_ref, p2_ref, p3_ref, soma_v_ref, soma_stim_ref,
    inverse_ref, soma_ref, gate_ref, rate_ref, cond_ref, stim_ref,
    vox_ref, source_ref, route_ref, rank_ref, weight_ref, potential_ref,
    send_ref, gate_hbm, soma_out, base_ref, table_ref,
    gate_out, sem,
):
    comp_count, cell_dev = solved_ref.shape
    soma = next_soma(
        soma_v_ref[...], soma_stim_ref[...],
        [p0_ref[...], p1_ref[...], p2_ref[...], p3_ref[...]], soma_ref[0:1, 0:1],
    )
    soma_out[...] = soma
    volts = solved_ref[...] + soma_ref[1:2, 0:1] * inverse_ref[:, 0:1] * soma
    fill_table(table_ref, volts, comp_count, cell_dev)
    gating, current = membrane(volts, gate_ref[...], rate_ref[...], cond_ref[...])
    gate_out[...] = gating
    copy = pltpu.make_async_copy(gate_out, gate_hbm, sem)
    copy.start()
    base_ref[...] = membrane_diag * volts + stim_ref[...] - current
    sent = weight_ref[...] * pick_rows(table_ref, source_ref[...], comp_count, cell_dev)
    slots = slot_rows([sent], hot(route_ref[...], devices), hits(rank_ref[...], CAP))
    slots.append(jnp.zeros((128 - CAP, devices), f32))
    parts = LOW // 128
    send_ref[pl.ds(2 * parts, devices, stride=stride), :] = jnp.concatenate(slots, axis=0).T
    put_voxels(send_ref, vox_ref[...], current, devices, stride)
    for j in range(parts):
        send_ref[pl.ds(parts + j, devices, stride=stride), :] = jnp.broadcast_to(
            potential_ref[j : j + 1, :], (devices, 128)
        )
    copy.wait()


def fourth_kernel(
    devices, stride, field_scale,
    recv_ref, here_ref, target_ref, weight_ref, factor_ref, base_ref, vox_ref,
    inverse_ref, soma_ref, resist_ref,
    rhs_ref, partial_ref, gap_ref, potential_ref,
):
    comp_count, cell_dev = base_ref.shape
    block_count = vox_ref.shape[0]
    block_size = comp_count // block_count
    parts = LOW // 128
    slots = recv_ref[pl.ds(2 * parts, devices, stride=stride), :].T
    gap = wide(slots[:CAP]) - weight_ref[...] * here_ref[...]
    gap_ref[...] = gap
    table = jnp.concatenate(
        [recv_ref[pl.ds(parts + j, devices, stride=stride), :] for j in range(parts)], axis=1
    )
    table = jnp.concatenate(halves(table), axis=0)
    looked = []
    for k in range(block_count):
        index = vox_ref[k : k + 1, :]
        found = jnp.dot(table, hot(index % LOW, LOW), preferred_element_type=f32)
        owners = lax.broadcasted_iota(jnp.int32, (devices, cell_dev), 0)
        both = jnp.where(owners == index // LOW, found[:devices] + found[devices:], 0.0)
        phi = jnp.sum(both, axis=0, keepdims=True)
        looked.append(jnp.broadcast_to(phi, (block_size, cell_dev)))
    rhs = base_ref[...] - ephaptic * jnp.concatenate(looked, axis=0)
    rhs_ref[...] = rhs
    heads = add_heads(factor_ref[...] * gap, target_ref[...], cell_dev)
    partial_ref[...] = soma_ref[1:2, 0:1] * (head_term(inverse_ref, rhs) + heads)
    for j in range(parts):
        own = jnp.sum(recv_ref[pl.ds(j, devices, stride=stride), :], axis=0, keepdims=True)
        potential_ref[j : j + 1, :] = resist_ref[j : j + 1, :] * own * field_scale


def last_kernel(
    solved_ref, p0_ref, p1_ref, p2_ref, p3_ref, soma_v_ref, soma_stim_ref,
    inverse_ref, soma_ref, volts_ref, soma_out,
):
    soma = next_soma(
        soma_v_ref[...], soma_stim_ref[...],
        [p0_ref[...], p1_ref[...], p2_ref[...], p3_ref[...]], soma_ref[0:1, 0:1],
    )
    soma_out[...] = soma
    volts_ref[...] = solved_ref[...] + soma_ref[1:2, 0:1] * inverse_ref[:, 0:1] * soma


def call(kernel, ins, outs, scratch=(), flops=0):
    space = lambda stays: pl.BlockSpec(memory_space=pltpu.HBM if stays else pltpu.VMEM)
    run = pl.pallas_call(
        kernel,
        in_specs=[space(stays) for stays in ins],
        out_specs=[space(out[2]) for out in outs],
        out_shape=[jax.ShapeDtypeStruct(out[0], out[1]) for out in outs],
        scratch_shapes=list(scratch),
        compiler_params=pltpu.CompilerParams(vmem_limit_bytes=VMEM_BYTES),
        cost_estimate=pl.CostEstimate(flops=flops, bytes_accessed=2**20, transcendentals=0),
    )

    def placed(*operands):
        return run(*[
            pltpu.with_memory_space_constraint(x, pltpu.HBM) if stays else x
            for x, stays in zip(operands, ins, strict=True)
        ])

    return placed


def bind(kernel, *sizes):
    def bound(*refs):
        kernel(*sizes, *refs)

    return bound


def exchange(send, devices):
    flat = lax.all_to_all(
        send.reshape(devices, send.size // devices), AXES, split_axis=0, concat_axis=0, tiled=True
    )
    return flat.reshape(send.shape)


def split_terms(partial, n_split):
    terms = [partial]
    for k in range(n_split - 1, 0, -1):
        pairs = [(i, (i + k) % n_split) for i in range(n_split)]
        terms.append(lax.ppermute(partial, "split", pairs))
    return terms


def per_device(
    voltage, gate_state, stimulus, gate_rate, gate_conductance, soma_voltage, soma_stimulus,
    axial_conductance, gap_source, gap_route, gap_target, gap_conductance, vox_index, field_resist,
):
    n_split = lax.axis_size("split")
    devices = lax.axis_size("cells") * n_split
    comp_count, cell_dev = voltage.shape[1:]
    rows = gap_source.shape[0]
    vox_dev = field_resist.shape[0]
    field_scale = vox_dev / (comp_count * cell_dev)
    volts, gate, stim = voltage[0], gate_state[0], stimulus[0]
    rate, cond, vox = gate_rate[0], gate_conductance[0], vox_index[0]
    source = gap_source.reshape(1, rows)
    route = gap_route.reshape(1, rows)
    target = gap_target.reshape(1, rows)
    weight = gap_conductance.reshape(1, rows)
    soma_v = soma_voltage.reshape(1, cell_dev)
    soma_stim = soma_stimulus.reshape(1, cell_dev)
    resist = field_resist.reshape(vox_dev // 128, 128)

    i32 = jnp.int32
    shape = (comp_count, cell_dev)
    full = (shape, f32, False)
    full_hbm = (shape, f32, True)
    line = ((1, cell_dev), f32, False)
    parts = vox_dev // 128
    quads = ((parts, 128), f32, False)
    table = pltpu.VMEM((2 * cell_dev // LOW * comp_count, LOW), bf16)
    field = pltpu.VMEM(shape, f32)

    row = ((1, CAP * devices), f32, False)
    row_i32 = ((1, CAP * devices), i32, False)

    stride = parts + 1
    kept = (volts, rate, cond, stim, vox, source, route, weight, soma_v, soma_stim, resist)
    used = (gate, target, axial_conductance)
    outs = call(
        bind(first_kernel, devices, stride),
        [True] * (len(kept) + len(used)),
        [(x.shape, x.dtype, False) for x in kept]
        + [
            ((devices * stride, 128), f32, False), ((1, rows), i32, False), full, full,
            ((comp_count, 128), f32, False), ((2, 128), f32, False),
        ],
        [pltpu.VMEM(x.shape, x.dtype) for x in used]
        + [table, pltpu.SemaphoreType.DMA((len(kept) + len(used),))],
    )(*kept, *used)
    volts, rate, cond, stim, vox, source, route, weight, soma_v, soma_stim, resist = outs[: len(kept)]
    send, rank, gate, current, inverse, soma_consts = outs[len(kept) :]
    received = exchange(send, devices)
    base, partial, slot_target, slot_weight, factor, gap, potential = call(
        bind(second_kernel, devices, stride, field_scale),
        [False] * 7,
        [full, line, row_i32, row, row, row, quads],
        [table],
    )(received, volts, stim, current, inverse, soma_consts, resist)
    terms = split_terms(partial, n_split)
    solve = call(solve_kernel, [False] * 4, [full], flops=3 * 10**9)
    (solved,) = solve(base, slot_target, gap, inverse)

    stride = 2 * parts + 1
    operands = (
        solved, *terms, soma_v, soma_stim, inverse, soma_consts,
        gate, rate, cond, stim, vox, source, route, rank, weight, potential,
    )
    send, gate, soma, base, volts_table = call(
        bind(third_kernel, devices, stride),
        [False] * len(operands),
        [((devices * stride, 128), f32, False), full_hbm, line, full, (table.shape, bf16, False)],
        [field, pltpu.SemaphoreType.DMA],
    )(*operands)
    received = exchange(send, devices)
    (here,) = call(pick_kernel, [False] * 3, [row], flops=3 * 10**9)(volts_table, slot_target, base)
    rhs, partial, gap, potential = call(
        bind(fourth_kernel, devices, stride, field_scale),
        [False] * 10,
        [full, line, row, quads],
    )(
        received, here, slot_target, slot_weight, factor, base, vox,
        inverse, soma_consts, resist,
    )
    terms = split_terms(partial, n_split)
    (solved,) = solve(rhs, slot_target, gap, inverse)

    operands = (solved, *terms, soma, soma_stim, inverse, soma_consts)
    volts, soma = call(
        last_kernel,
        [False] * len(operands),
        [full, line],
    )(*operands)
    return volts[None], gate[None], soma.reshape(cell_dev), potential.reshape(vox_dev)


def solution(mesh):
    wide = P("split", None, "cells")
    every = P(AXES)
    in_specs = (
        wide, wide, wide, wide, wide, P("cells"), P("cells"), P(),
        every, P(AXES, None), every, every, wide, every,
    )
    out_specs = (wide, wide, P("cells"), every)
    return jax.shard_map(
        per_device, mesh=mesh, in_specs=in_specs, out_specs=out_specs, check_vma=False
    )
```

time: 97.7 us -> 82.2 us (0.84)
  local copies, waits for them, and re-layouts: 8.71 us -> 0 us
  waiting for transfers between devices: 19.7 us -> 11.7 us
  blocking collectives: 18.4 us -> 22.2 us
  starting transfers between devices: 16.6 us -> 13.7 us
    ppermute x6, waiting for transfers between devices: 9.89 us -> 0.3 us  [split_terms(): terms.append(lax.ppermute(partial, 'split', pairs))]
    unnamed x39 -> x0, local copies, waits for them, and re-layouts: 8.57 us -> none
    all_to_all x1, starting transfers between devices: 11.1 us -> 6.27 us  [exchange(): lax.all_to_all(send.reshape(devices, send.size // devices), AXES, split_a...]
    all_to_all x1, blocking collectives: 18.4 us -> 22.2 us  [exchange(): lax.all_to_all(send.reshape(devices, send.size // devices), AXES, split_a...]
    ppermute x6, starting transfers between devices: 5.49 us -> 7.46 us  [split_terms(): terms.append(lax.ppermute(partial, 'split', pairs))]
    all_to_all x1, waiting for transfers between devices: 9.79 us -> 11.4 us  [exchange(): lax.all_to_all(send.reshape(devices, send.size // devices), AXES, split_a...]
    pallas_call x6 -> x8, Pallas kernels: 32.8 us -> 33.5 us  [placed(): run(*[pltpu.with_memory_space_constraint(x, pltpu.HBM) if stays else x fo...]
  transfers between devices with their start and end apart: 7 -> 7, of which waited for: 7 -> 2; matrix products, arithmetic and copies ran while one was open for 0% -> 0% of each run, Pallas kernels for 0% -> 10%
where the time goes in v2:
time: 82.2 us; the launch traced here: 81.9 us
  Pallas kernels  33.5 us (41%)
  blocking collectives  22.2 us (27%)
  starting transfers between devices  13.7 us (17%)
  waiting for transfers between devices  11.7 us (14%)
    pallas_call x8, Pallas kernels, placed(): run(*[pltpu.with_memory_space_constraint(x, pltpu.HBM) if stays else x fo...  33.5 us
    all_to_all x1, blocking collectives, exchange(): lax.all_to_all(send.reshape(devices, send.size // devices), AXES, split_a...  22.2 us
    all_to_all x1, waiting for transfers between devices, exchange(): lax.all_to_all(send.reshape(devices, send.size // devices), AXES, split_a...  11.4 us
    ppermute x6, starting transfers between devices, split_terms(): terms.append(lax.ppermute(partial, 'split', pairs))  7.46 us
    all_to_all x1, starting transfers between devices, exchange(): lax.all_to_all(send.reshape(devices, send.size // devices), AXES, split_a...  6.27 us
  transfers between devices with their start and end apart: 7, of which 2 were waited for; matrix products, arithmetic and copies ran while one was open for 0% of the time, Pallas kernels for 10%

profile of v2, /device:TPU:0, one launch (start us, length us, event | category | flops | bytes accessed | tf_op | source)
XLA Modules:
  0.0 81.9 jit_solution(17198319273036217571)
XLA Ops:
  0.6 8.5 %shard_map.165 = (f32[32,4096]{1,0:T(8,128)S(1)}, f32[32,4096]{1,0:T(8,128)S(1)}, f32[32,4096]{1,0:T(8,128)S(1)}, f32[32,4096]{1,0:T(8,128)S(1)}, s32[4,4096]{1,...) custom-call(f32[32,4096]{1,0:T(8,128)} %bitcast.24, ...), custom_call_target="tpu_custom_call" | custom-call | bytes 1048576 | tf_op jit(solution)/shard_map/pallas_call | solution.py:392
  9.1 22.2 %all_to_all.18 = f32[128,1,640]{2,1,0:T(1,128)S(1)} all-to-all(f32[128,1,640]{2,1,0:T(1,128)S(1)} %bitcast.23), channel_id=1, replica_groups=mesh['cells'=32,'split'=4] {'cells','split'}, dimensions={0} | all-to-all | bytes 655360 | tf_op jit(solution)/shard_map/all_to_all | solution.py:408
  31.3 3.0 %shard_map.166 = (f32[32,4096]{1,0:T(8,128)S(1)}, f32[1,4096]{1,0:T(1,128)S(1)}, s32[1,4096]{1,0:T(1,128)S(1)}, f32[1,4096]{1,0:T(1,128)S(1)}, f32[1,4096]{1,0:T...) custom-call(f32[640,128]{1,0:T(8,128)S(1)} %bitcast.22, f32[32,4096]{1,0:T(8,128)S(1)} %get-tuple-element.40.refs_1_, ...), custom_call_target="tpu_custom_call" | custom-call | bytes 1048576 | tf_op jit(solution)/shard_map/pallas_call | solution.py:392
  34.3 0.7 collective-permute-start.2
  35.0 2.4 %collective-permute-start.1 = (f32[1,4096]{1,0:T(1,128)S(1)}, f32[1,4096]{1,0:T(1,128)S(1)}, u32[]{:S(2)}, u32[]{:S(2)}) collective-permute-start(f32[1,4096]{1,0:T(1,128)S(1)} %get-tuple-element.49.refs_1_), channel_id=1, source_target_pairs={{0,2},{1,3},{2,0},{3,1},{4,6},{5,7},{6,4},{7,5},{8,10},{9,11},{10,... | collective-permute-start | bytes 49160 | tf_op jit(solution)/shard_map/ppermute | solution.py:418
  37.4 0.9 %collective-permute-start = (f32[1,4096]{1,0:T(1,128)S(1)}, f32[1,4096]{1,0:T(1,128)S(1)}, u32[]{:S(2)}, u32[]{:S(2)}) collective-permute-start(f32[1,4096]{1,0:T(1,128)S(1)} %get-tuple-element.49.refs_1_), channel_id=1, source_target_pairs={{0,3},{1,0},{2,1},{3,2},{4,7},{5,4},{6,5},{7,6},{8,11},{9,8},{10,9... | collective-permute-start | bytes 49160 | tf_op jit(solution)/shard_map/ppermute | solution.py:418
  38.3 2.9 %shard_map.167.refs_0_ = f32[32,4096]{1,0:T(8,128)S(1)} custom-call(f32[32,4096]{1,0:T(8,128)S(1)} %get-tuple-element.46.base_ref, s32[1,4096]{1,0:T(1,128)S(1)} %get-tuple-element.47.target_ref.refs_2_, f32[1,4096]{1,0:T(1,128)S(1)} %get-tuple-element.48.gap_ref, f32[32,128]{1,0:T(8,128)S(1)} %get-tuple-element.43.refs_4_.inverse_ref.refs_7_), custom_call_target="tpu_custom_call" | custom-call | flops 3000000000 | bytes 1048576 | tf_op jit(solution)/shard_map/pallas_call | solution.py:392
  41.2 0.0 collective-permute-done.2.refs_4_
  41.2 0.0 collective-permute-done.1.refs_3_
  41.2 0.0 collective-permute-done.refs_2_
  41.2 7.3 %shard_map.168 = (f32[1152,128]{1,0:T(8,128)}, f32[32,4096]{1,0:T(8,128)}, f32[1,4096]{1,0:T(1,128)S(1)}, f32[32,4096]{1,0:T(8,128)S(1)}, bf16[512,512]{1,0:T(8,128)(2,1)S(1)}) custom-call(f32[32,4096]{1,0:T(8,128)S(1)} %shard_map.167.refs_0_, f32[1,4096]{1,0:T(1,128)S(1)} %get-tuple-element.49.refs_1_, f32[1,4096]{1,0:T(1,128)S(1)} %collective-permute-done.refs_2_, ...), custom_call_target="tpu_custom_call" | custom-call | bytes 1048576 | tf_op jit(solution)/shard_map/pallas_call | solution.py:392
  48.5 6.3 %all-to-all-start.1 = ((f32[128,1,1152]{2,1,0:T(1,128)}), f32[128,1,1152]{2,1,0:T(1,128)S(1)}, u32[]{:S(2)}, u32[]{:S(2)}) async-start(f32[128,1,1152]{2,1,0:T(1,128)} %bitcast.15), calls=%async_computation.1 | async-start | bytes 1179648 | tf_op jit(solution)/shard_map/all_to_all | solution.py:408
  54.8 2.4 %shard_map.169.refs_1_ = f32[1,4096]{1,0:T(1,128)S(1)} custom-call(bf16[512,512]{1,0:T(8,128)(2,1)S(1)} %get-tuple-element.62.table_ref, s32[1,4096]{1,0:T(1,128)S(1)} %get-tuple-element.47.target_ref.refs_2_, f32[32,4096]{1,0:T(8,128)S(1)} %get-tuple-element.63.cells_ref.refs_5_), custom_call_target="tpu_custom_call" | custom-call | flops 3000000000 | bytes 1048576 | tf_op jit(solution)/shard_map/pallas_call | solution.py:392
  57.2 11.4 %all-to-all-done.1 = f32[128,1,1152]{2,1,0:T(1,128)S(1)} async-done(((f32[128,1,1152]{2,1,0:T(1,128)}), f32[128,1,1152]{2,1,0:T(1,128)S(1)}, u32[]{:S(2)}, u32[]{:S(2)}) %all-to-all-start.1) | async-done | bytes 589856 | tf_op jit(solution)/shard_map/all_to_all | solution.py:408
  68.6 5.6 %shard_map.170 = (f32[32,4096]{1,0:T(8,128)S(1)}, f32[1,4096]{1,0:T(1,128)S(1)}, f32[1,4096]{1,0:T(1,128)S(1)}, f32[4,128]{1,0:T(4,128)}) custom-call(f32[1152,128]{1,0:T(8,128)S(1)} %bitcast.21, f32[1,4096]{1,0:T(1,128)S(1)} %shard_map.169.refs_1_, s32[1,4096]{1,0:T(1,128)S(1)} %get-tuple-element.47.target_ref.refs_2_, ...), custom_call_target="tpu_custom_call" | custom-call | bytes 1048576 | tf_op jit(solution)/shard_map/pallas_call | solution.py:392
  74.2 0.6 collective-permute-start.5
  74.8 2.4 %collective-permute-start.4 = (f32[1,4096]{1,0:T(1,128)S(1)}, f32[1,4096]{1,0:T(1,128)S(1)}, u32[]{:S(2)}, u32[]{:S(2)}) collective-permute-start(f32[1,4096]{1,0:T(1,128)S(1)} %get-tuple-element.68.p0_ref), channel_id=1, source_target_pairs={{0,2},{1,3},{2,0},{3,1},{4,6},{5,7},{6,4},{7,5},{8,10},{9,11},{10,... | collective-permute-start | bytes 49160 | tf_op jit(solution)/shard_map/ppermute | solution.py:418
  77.2 0.5 collective-permute-start.3
  77.7 2.9 %shard_map.171.solved_ref = f32[32,4096]{1,0:T(8,128)S(1)} custom-call(f32[32,4096]{1,0:T(8,128)S(1)} %get-tuple-element.66.base_ref, s32[1,4096]{1,0:T(1,128)S(1)} %get-tuple-element.47.target_ref.refs_2_, f32[1,4096]{1,0:T(1,128)S(1)} %get-tuple-element.67.gap_ref, f32[32,128]{1,0:T(8,128)S(1)} %get-tuple-element.43.refs_4_.inverse_ref.refs_7_), custom_call_target="tpu_custom_call" | custom-call | flops 3000000000 | bytes 1048576 | tf_op jit(solution)/shard_map/pallas_call | solution.py:392
  80.6 0.0 collective-permute-done.5.p3_ref
  80.6 0.0 collective-permute-done.4.p2_ref
  80.6 0.3 collective-permute-done.3.p1_ref
  80.9 0.9 %shard_map.172 = (f32[32,4096]{1,0:T(8,128)}, f32[1,4096]{1,0:T(1,128)}) custom-call(f32[32,4096]{1,0:T(8,128)S(1)} %shard_map.171.solved_ref, f32[1,4096]{1,0:T(1,128)S(1)} %get-tuple-element.68.p0_ref, f32[1,4096]{1,0:T(1,128)S(1)} %collective-permute-done.3.p1_ref, f32[1,4096]{1,0:T(1,128)S(1)} %collective-permute-done.4.p2_ref, ...), custom_call_target="tpu_custom_call" | custom-call | bytes 1048576 | tf_op jit(solution)/shard_map/pallas_call | solution.py:392
Async XLA Ops:
  34.3 6.9 %collective-permute-start.2 = (f32[1,4096]{1,0:T(1,128)S(1)}, f32[1,4096]{1,0:T(1,128)S(1)}, u32[]{:S(2)}, u32[]{:S(2)}) collective-permute-start(f32[1,4096]{1,0:T(1,128)S(1)} %get-tuple-element.49.refs_1_), channel_id=1, source_target_pairs={{0,1},{1,2},{2,3},{3,0},{4,5},{5,6},{6,7},{7,4},{8,9},{9,10},{10,1... | collective-permute-start | bytes 49160 | tf_op jit(solution)/shard_map/ppermute | solution.py:418
  35.0 6.2 %collective-permute-start.1 = (f32[1,4096]{1,0:T(1,128)S(1)}, f32[1,4096]{1,0:T(1,128)S(1)}, u32[]{:S(2)}, u32[]{:S(2)}) collective-permute-start(f32[1,4096]{1,0:T(1,128)S(1)} %get-tuple-element.49.refs_1_), channel_id=1, source_target_pairs={{0,2},{1,3},{2,0},{3,1},{4,6},{5,7},{6,4},{7,5},{8,10},{9,11},{10,... | collective-permute-start | bytes 49160 | tf_op jit(solution)/shard_map/ppermute | solution.py:418
  37.4 3.8 %collective-permute-start = (f32[1,4096]{1,0:T(1,128)S(1)}, f32[1,4096]{1,0:T(1,128)S(1)}, u32[]{:S(2)}, u32[]{:S(2)}) collective-permute-start(f32[1,4096]{1,0:T(1,128)S(1)} %get-tuple-element.49.refs_1_), channel_id=1, source_target_pairs={{0,3},{1,0},{2,1},{3,2},{4,7},{5,4},{6,5},{7,6},{8,11},{9,8},{10,9... | collective-permute-start | bytes 49160 | tf_op jit(solution)/shard_map/ppermute | solution.py:418
  48.5 20.1 %all-to-all-start.1 = ((f32[128,1,1152]{2,1,0:T(1,128)}), f32[128,1,1152]{2,1,0:T(1,128)S(1)}, u32[]{:S(2)}, u32[]{:S(2)}) async-start(f32[128,1,1152]{2,1,0:T(1,128)} %bitcast.15), calls=%async_computation.1 | async-start | bytes 1179648 | tf_op jit(solution)/shard_map/all_to_all | solution.py:408
  74.2 6.4 %collective-permute-start.5 = (f32[1,4096]{1,0:T(1,128)S(1)}, f32[1,4096]{1,0:T(1,128)S(1)}, u32[]{:S(2)}, u32[]{:S(2)}) collective-permute-start(f32[1,4096]{1,0:T(1,128)S(1)} %get-tuple-element.68.p0_ref), channel_id=1, source_target_pairs={{0,1},{1,2},{2,3},{3,0},{4,5},{5,6},{6,7},{7,4},{8,9},{9,10},{10,1... | collective-permute-start | bytes 49160 | tf_op jit(solution)/shard_map/ppermute | solution.py:418
  74.8 5.8 %collective-permute-start.4 = (f32[1,4096]{1,0:T(1,128)S(1)}, f32[1,4096]{1,0:T(1,128)S(1)}, u32[]{:S(2)}, u32[]{:S(2)}) collective-permute-start(f32[1,4096]{1,0:T(1,128)S(1)} %get-tuple-element.68.p0_ref), channel_id=1, source_target_pairs={{0,2},{1,3},{2,0},{3,1},{4,6},{5,7},{6,4},{7,5},{8,10},{9,11},{10,... | collective-permute-start | bytes 49160 | tf_op jit(solution)/shard_map/ppermute | solution.py:418
  77.2 3.7 %collective-permute-start.3 = (f32[1,4096]{1,0:T(1,128)S(1)}, f32[1,4096]{1,0:T(1,128)S(1)}, u32[]{:S(2)}, u32[]{:S(2)}) collective-permute-start(f32[1,4096]{1,0:T(1,128)S(1)} %get-tuple-element.68.p0_ref), channel_id=1, source_target_pairs={{0,3},{1,0},{2,1},{3,2},{4,7},{5,4},{6,5},{7,6},{8,11},{9,8},{10,9... | collective-permute-start | bytes 49160 | tf_op jit(solution)/shard_map/ppermute | solution.py:418

commit v3 on v2

--- a/solution.py
+++ b/solution.py
@@ -8,7 +8,7 @@
 SUB = 2
 CAP = 32
 LOW = 512
-STEP = 512
+STEP = 4096
 
 membrane_diag = 4.0
 soma_diag = 8.0
@@ -103,7 +103,7 @@
     for at in range(0, source.shape[1], STEP):
         high, low = comp_digits(source[:, at : at + STEP], cell_dev, comp_count)
         found = jnp.dot(table_ref[...], hot(low, LOW), preferred_element_type=f32)
-        rows = lax.broadcasted_iota(jnp.int32, (size, STEP), 0)
+        rows = lax.broadcasted_iota(jnp.int32, (size, high.shape[1]), 0)
         both = jnp.where(rows == high, found[:size] + found[size:], 0.0)
         pieces.append(jnp.sum(both, axis=0, keepdims=True))
     return jnp.concatenate(pieces, axis=1)
@@ -145,6 +145,24 @@
     ]
 
 
+def ranks_of(owner, devices):
+    span = 256
+    index = lax.broadcasted_iota(jnp.int32, (2 * span, span), 0)
+    earlier = jnp.where(
+        (index < lax.broadcasted_iota(jnp.int32, (2 * span, span), 1)) | (index >= span), 1.0, 0.0
+    ).astype(bf16)
+    before = jnp.zeros((devices, span), bf16)
+    ranks, owners = [], []
+    for at in range(0, owner.shape[1], span):
+        one = hot(owner[:, at : at + span], devices)
+        both = jnp.concatenate([one, before], axis=1)
+        count = jnp.dot(both, earlier, preferred_element_type=f32)
+        ranks.append(jnp.sum(one.astype(f32) * count, axis=0, keepdims=True))
+        before = before + one
+        owners.append(one)
+    return jnp.concatenate(ranks, axis=1).astype(jnp.int32), jnp.concatenate(owners, axis=1)
+
+
 def first_kernel(
     devices, stride,
     volts_hbm, rate_hbm, cond_hbm, stim_hbm, vox_hbm, source_hbm, route_hbm, weight_hbm,
@@ -168,40 +186,22 @@
     rows = source_ref.shape[1]
     copies[0].wait()
     write_inverse(axial_ref[...], lax.axis_index("split"), inverse_ref, soma_ref)
-    span = 256
-    earlier = jnp.where(
-        lax.broadcasted_iota(jnp.int32, (span, span), 0)
-        < lax.broadcasted_iota(jnp.int32, (span, span), 1),
-        1.0, 0.0,
-    ).astype(bf16)
-    before = jnp.zeros((devices, 1), f32)
-    ranks, dests = [], []
     copies[1].wait()
-    for at in range(0, rows, span):
-        dest = hot(route_ref[:, at : at + span], devices)
-        count = jnp.dot(dest, earlier, preferred_element_type=f32) + before
-        full = dest.astype(f32)
-        ranks.append(jnp.sum(full * count, axis=0, keepdims=True))
-        before = count[:, span - 1 : span] + full[:, span - 1 : span]
-        dests.append(dest)
-    rank = jnp.concatenate(ranks, axis=1).astype(jnp.int32)
+    rank, dest_hot = ranks_of(route_ref[...], devices)
     rank_ref[...] = rank
-    dest_hot = jnp.concatenate(dests, axis=1)
-    for copy in copies[2:6]:
+    for copy in copies[2:10]:
         copy.wait()
     volts = volts_ref[...]
+    gating, current = membrane(volts, gate_ref[...], rate_ref[...], cond_ref[...])
+    gate_out[...] = gating
+    current_out[...] = current
+    put_voxels(send_ref, vox_ref[...], current, devices, stride)
     fill_table(table_ref, volts, comp_count, cell_dev)
     weight = weight_ref[...]
     sent = weight * pick_rows(table_ref, source_ref[...], comp_count, cell_dev)
     slots = slot_rows([target_ref[...].astype(f32), weight, sent], dest_hot, hits(rank, CAP))
     slots.append(jnp.zeros((128 - 3 * CAP, devices), f32))
     send_ref[pl.ds(LOW // 128, devices, stride=stride), :] = jnp.concatenate(slots, axis=0).T
-    for copy in copies[6:10]:
-        copy.wait()
-    gating, current = membrane(volts, gate_ref[...], rate_ref[...], cond_ref[...])
-    gate_out[...] = gating
-    current_out[...] = current
-    put_voxels(send_ref, vox_ref[...], current, devices, stride)
     for copy in copies[10:]:
         copy.wait()
 
@@ -286,9 +286,38 @@
     solved_ref[...] = solve(inverse_ref, base_ref[...] + gap_in)
 
 
-def pick_kernel(table_ref, target_ref, cells_ref, here_ref):
+def beside_kernel(
+    devices,
+    table_ref, target_ref, cells_ref, vox_ref,
+    here_ref, group_ref, column_ref, within_ref, heavy_ref,
+):
     comp_count, cell_dev = cells_ref.shape
     here_ref[...] = pick_rows(table_ref, target_ref[...], comp_count, cell_dev)
+    block_count = vox_ref.shape[0]
+    vox = jnp.concatenate([vox_ref[k : k + 1, :] for k in range(block_count)], axis=1)
+    owner = vox // LOW
+    rank, unused = ranks_of(owner, devices)
+    over = rank >= 128
+    group = jnp.where(over, devices // 2, owner // 2)
+    column = jnp.where(over, rank - 128, owner % 2 * 128 + rank)
+    for k in range(block_count):
+        group_ref[k : k + 1, :] = group[:, k * cell_dev : (k + 1) * cell_dev]
+        column_ref[k : k + 1, :] = column[:, k * cell_dev : (k + 1) * cell_dev]
+    heavy_ref[...] = jnp.max(jnp.where(over, owner, -1), axis=1, keepdims=True)
+    size = within_ref.shape[0]
+    mask = hits(group, size)
+    high, low = halves((vox % LOW).astype(f32))
+    left = jnp.concatenate([chosen(mask, high), chosen(mask, low)], axis=0)
+    laid = lax.dot_general(left, hot(column, 256), LANES, preferred_element_type=f32)
+    within_ref[...] = (laid[:size] + laid[size:]).astype(jnp.int32)
+
+
+def look_up(parts, index):
+    found = jnp.zeros(index.shape, f32)
+    for j, part in enumerate(parts):
+        there = jnp.take_along_axis(part, index % 128, axis=1, mode="promise_in_bounds")
+        found = jnp.where(index // 128 == j, there, found)
+    return found
 
 
 def next_soma(soma, stimulus, partials, total):
@@ -332,29 +361,51 @@
 
 def fourth_kernel(
     devices, stride, field_scale,
-    recv_ref, here_ref, target_ref, weight_ref, factor_ref, base_ref, vox_ref,
-    inverse_ref, soma_ref, resist_ref,
+    recv_ref, here_ref, group_ref, column_ref, within_ref, heavy_ref,
+    target_ref, weight_ref, factor_ref, base_ref, inverse_ref, soma_ref, resist_ref,
     rhs_ref, partial_ref, gap_ref, potential_ref,
 ):
     comp_count, cell_dev = base_ref.shape
-    block_count = vox_ref.shape[0]
+    block_count = group_ref.shape[0]
     block_size = comp_count // block_count
     parts = LOW // 128
     slots = recv_ref[pl.ds(2 * parts, devices, stride=stride), :].T
     gap = wide(slots[:CAP]) - weight_ref[...] * here_ref[...]
     gap_ref[...] = gap
+    half = devices // 2
+    size = within_ref.shape[0]
+    sides = []
+    for side in range(2):
+        owners = [
+            recv_ref[pl.ds(side * stride + parts + j, half, stride=2 * stride), :]
+            for j in range(parts)
+        ]
+        sides.append(look_up(owners, within_ref[:half, side * 128 : (side + 1) * 128]))
+    heavy = lax.broadcasted_iota(jnp.int32, (devices, 128), 0) == heavy_ref[...]
+    owner = []
+    for j in range(parts):
+        rows = recv_ref[pl.ds(parts + j, devices, stride=stride), :]
+        one = jnp.sum(jnp.where(heavy, rows, 0.0), axis=0, keepdims=True)
+        owner.append(jnp.broadcast_to(one, (size - half, 128)))
+    rest = look_up(owner, within_ref[half:, :128])
     table = jnp.concatenate(
-        [recv_ref[pl.ds(parts + j, devices, stride=stride), :] for j in range(parts)], axis=1
+        [
+            jnp.concatenate([sides[0], rest], axis=0),
+            jnp.concatenate([sides[1], jnp.zeros_like(rest)], axis=0),
+        ],
+        axis=1,
     )
     table = jnp.concatenate(halves(table), axis=0)
-    looked = []
-    for k in range(block_count):
-        index = vox_ref[k : k + 1, :]
-        found = jnp.dot(table, hot(index % LOW, LOW), preferred_element_type=f32)
-        owners = lax.broadcasted_iota(jnp.int32, (devices, cell_dev), 0)
-        both = jnp.where(owners == index // LOW, found[:devices] + found[devices:], 0.0)
-        phi = jnp.sum(both, axis=0, keepdims=True)
-        looked.append(jnp.broadcast_to(phi, (block_size, cell_dev)))
+    column = jnp.concatenate([column_ref[k : k + 1, :] for k in range(block_count)], axis=1)
+    group = jnp.concatenate([group_ref[k : k + 1, :] for k in range(block_count)], axis=1)
+    found = jnp.dot(table, hot(column, 256), preferred_element_type=f32)
+    groups = lax.broadcasted_iota(jnp.int32, (size, group.shape[1]), 0)
+    both = jnp.where(groups == group, found[:size] + found[size:], 0.0)
+    phi = jnp.sum(both, axis=0, keepdims=True)
+    looked = [
+        jnp.broadcast_to(phi[:, k * cell_dev : (k + 1) * cell_dev], (block_size, cell_dev))
+        for k in range(block_count)
+    ]
     rhs = base_ref[...] - ephaptic * jnp.concatenate(looked, axis=0)
     rhs_ref[...] = rhs
     heads = add_heads(factor_ref[...] * gap, target_ref[...], cell_dev)
@@ -491,14 +542,23 @@
         [field, pltpu.SemaphoreType.DMA],
     )(*operands)
     received = exchange(send, devices)
-    (here,) = call(pick_kernel, [False] * 3, [row], flops=3 * 10**9)(volts_table, slot_target, base)
+    groups = devices // 2 + 8
+    here, group, column, within, heavy = call(
+        bind(beside_kernel, devices),
+        [False] * 4,
+        [
+            row, (vox.shape, i32, False), (vox.shape, i32, False),
+            ((groups, 256), i32, False), ((1, 1), i32, False),
+        ],
+        flops=8 * 10**9,
+    )(volts_table, slot_target, base, vox)
     rhs, partial, gap, potential = call(
         bind(fourth_kernel, devices, stride, field_scale),
-        [False] * 10,
+        [False] * 13,
         [full, line, row, quads],
     )(
-        received, here, slot_target, slot_weight, factor, base, vox,
-        inverse, soma_consts, resist,
+        received, here, group, column, within, heavy,
+        slot_target, slot_weight, factor, base, inverse, soma_consts, resist,
     )
     terms = split_terms(partial, n_split)
     (solved,) = solve(rhs, slot_target, gap, inverse)

time: 82.2 us -> 79.7 us (0.970)
  waiting for transfers between devices: 11.7 us -> 4.76 us
  Pallas kernels: 33.5 us -> 38 us
    all_to_all x1, waiting for transfers between devices: 11.4 us -> 4.46 us  [exchange(): lax.all_to_all(send.reshape(devices, send.size // devices), AXES, split_a...]
    pallas_call x8, Pallas kernels: 33.5 us -> 38 us  [placed(): run(*[pltpu.with_memory_space_constraint(x, pltpu.HBM) if stays else x fo...]
  transfers between devices with their start and end apart: 7 -> 7, of which waited for: 2 -> 2; matrix products, arithmetic and copies ran while one was open for 0% -> 0% of each run, Pallas kernels for 10% -> 19%
where the time goes in v3:
time: 79.7 us; the launch traced here: 79.4 us
  Pallas kernels  38 us (48%)
  blocking collectives  22.2 us (28%)
  starting transfers between devices  13.8 us (17%)
  waiting for transfers between devices  4.76 us (6%)
    pallas_call x8, Pallas kernels, placed(): run(*[pltpu.with_memory_space_constraint(x, pltpu.HBM) if stays else x fo...  38 us
    all_to_all x1, blocking collectives, exchange(): lax.all_to_all(send.reshape(devices, send.size // devices), AXES, split_a...  22.2 us
    ppermute x6, starting transfers between devices, split_terms(): terms.append(lax.ppermute(partial, 'split', pairs))  7.48 us
    all_to_all x1, starting transfers between devices, exchange(): lax.all_to_all(send.reshape(devices, send.size // devices), AXES, split_a...  6.27 us
    all_to_all x1, waiting for transfers between devices, exchange(): lax.all_to_all(send.reshape(devices, send.size // devices), AXES, split_a...  4.46 us
  transfers between devices with their start and end apart: 7, of which 2 were waited for; matrix products, arithmetic and copies ran while one was open for 0% of the time, Pallas kernels for 19%

profile of v3, /device:TPU:0, one launch (start us, length us, event | category | flops | bytes accessed | tf_op | source)
XLA Modules:
  0.0 79.4 jit_solution(5909209124551882583)
XLA Ops:
  0.6 8.0 %shard_map.165 = (f32[32,4096]{1,0:T(8,128)S(1)}, f32[32,4096]{1,0:T(8,128)S(1)}, f32[32,4096]{1,0:T(8,128)S(1)}, f32[32,4096]{1,0:T(8,128)S(1)}, s32[4,4096]{1,...) custom-call(f32[32,4096]{1,0:T(8,128)} %bitcast.24, ...), custom_call_target="tpu_custom_call" | custom-call | bytes 1048576 | tf_op jit(solution)/shard_map/pallas_call | solution.py:443
  8.7 22.2 %all_to_all.18 = f32[128,1,640]{2,1,0:T(1,128)S(1)} all-to-all(f32[128,1,640]{2,1,0:T(1,128)S(1)} %bitcast.23), channel_id=1, replica_groups=mesh['cells'=32,'split'=4] {'cells','split'}, dimensions={0} | all-to-all | bytes 655360 | tf_op jit(solution)/shard_map/all_to_all | solution.py:459
  30.8 3.0 %shard_map.166 = (f32[32,4096]{1,0:T(8,128)S(1)}, f32[1,4096]{1,0:T(1,128)S(1)}, s32[1,4096]{1,0:T(1,128)S(1)}, f32[1,4096]{1,0:T(1,128)S(1)}, f32[1,4096]{1,0:T...) custom-call(f32[640,128]{1,0:T(8,128)S(1)} %bitcast.22, f32[32,4096]{1,0:T(8,128)S(1)} %get-tuple-element.45.refs_1_, ...), custom_call_target="tpu_custom_call" | custom-call | bytes 1048576 | tf_op jit(solution)/shard_map/pallas_call | solution.py:443
  33.9 0.7 collective-permute-start.2
  34.6 2.4 %collective-permute-start.1 = (f32[1,4096]{1,0:T(1,128)S(1)}, f32[1,4096]{1,0:T(1,128)S(1)}, u32[]{:S(2)}, u32[]{:S(2)}) collective-permute-start(f32[1,4096]{1,0:T(1,128)S(1)} %get-tuple-element.54.refs_1_), channel_id=1, source_target_pairs={{0,2},{1,3},{2,0},{3,1},{4,6},{5,7},{6,4},{7,5},{8,10},{9,11},{10,... | collective-permute-start | bytes 49160 | tf_op jit(solution)/shard_map/ppermute | solution.py:469
  37.0 0.9 %collective-permute-start = (f32[1,4096]{1,0:T(1,128)S(1)}, f32[1,4096]{1,0:T(1,128)S(1)}, u32[]{:S(2)}, u32[]{:S(2)}) collective-permute-start(f32[1,4096]{1,0:T(1,128)S(1)} %get-tuple-element.54.refs_1_), channel_id=1, source_target_pairs={{0,3},{1,0},{2,1},{3,2},{4,7},{5,4},{6,5},{7,6},{8,11},{9,8},{10,9... | collective-permute-start | bytes 49160 | tf_op jit(solution)/shard_map/ppermute | solution.py:469
  37.9 2.9 %shard_map.167.refs_0_ = f32[32,4096]{1,0:T(8,128)S(1)} custom-call(f32[32,4096]{1,0:T(8,128)S(1)} %get-tuple-element.51.base_ref, s32[1,4096]{1,0:T(1,128)S(1)} %get-tuple-element.52.target_ref.refs_1_.refs_6_, f32[1,4096]{1,0:T(1,128)S(1)} %get-tuple-element.53.gap_ref, f32[32,128]{1,0:T(8,128)S(1)} %get-tuple-element.48.refs_4_.inverse_ref.refs_7_.refs_10_), custom_call_target="tpu_custom_call" | custom-call | flops 3000000000 | bytes 1048576 | tf_op jit(solution)/shard_map/pallas_call | solution.py:443
  40.8 0.0 collective-permute-done.2.refs_4_
  40.8 0.0 collective-permute-done.1.refs_3_
  40.8 0.0 collective-permute-done.refs_2_
  40.8 7.3 %shard_map.168 = (f32[1152,128]{1,0:T(8,128)}, f32[32,4096]{1,0:T(8,128)}, f32[1,4096]{1,0:T(1,128)S(1)}, f32[32,4096]{1,0:T(8,128)S(1)}, bf16[512,512]{1,0:T(8,128)(2,1)S(1)}) custom-call(f32[32,4096]{1,0:T(8,128)S(1)} %shard_map.167.refs_0_, f32[1,4096]{1,0:T(1,128)S(1)} %get-tuple-element.54.refs_1_, f32[1,4096]{1,0:T(1,128)S(1)} %collective-permute-done.refs_2_, ...), custom_call_target="tpu_custom_call" | custom-call | bytes 1048576 | tf_op jit(solution)/shard_map/pallas_call | solution.py:443
  48.1 6.3 %all-to-all-start.1 = ((f32[128,1,1152]{2,1,0:T(1,128)}), f32[128,1,1152]{2,1,0:T(1,128)S(1)}, u32[]{:S(2)}, u32[]{:S(2)}) async-start(f32[128,1,1152]{2,1,0:T(1,128)} %bitcast.15), calls=%async_computation.1 | async-start | bytes 1179648 | tf_op jit(solution)/shard_map/all_to_all | solution.py:459
  54.4 9.3 %shard_map.169 = (f32[1,4096]{1,0:T(1,128)S(1)}, s32[4,4096]{1,0:T(4,128)S(1)}, s32[4,4096]{1,0:T(4,128)S(1)}, s32[72,256]{1,0:T(8,128)S(1)}, s32[1,1]{1,0:T(1,128)}) custom-call(bf16[512,512]{1,0:T(8,128)(2,1)S(1)} %get-tuple-element.67.refs_0_, s32[1,4096]{1,0:T(1,128)S(1)} %get-tuple-element.52.target_ref.refs_1_.refs_6_, ...), custom_call_target="tpu_custom_call" | custom-call | flops 8000000000 | bytes 1048576 | tf_op jit(solution)/shard_map/pallas_call | solution.py:443
  63.8 4.5 %all-to-all-done.1 = f32[128,1,1152]{2,1,0:T(1,128)S(1)} async-done(((f32[128,1,1152]{2,1,0:T(1,128)}), f32[128,1,1152]{2,1,0:T(1,128)S(1)}, u32[]{:S(2)}, u32[]{:S(2)}) %all-to-all-start.1) | async-done | bytes 589856 | tf_op jit(solution)/shard_map/all_to_all | solution.py:459
  68.2 3.5 %shard_map.170 = (f32[32,4096]{1,0:T(8,128)S(1)}, f32[1,4096]{1,0:T(1,128)S(1)}, f32[1,4096]{1,0:T(1,128)S(1)}, f32[4,128]{1,0:T(4,128)}) custom-call(f32[1152,128]{1,0:T(8,128)S(1)} %bitcast.21, f32[1,4096]{1,0:T(1,128)S(1)} %get-tuple-element.69.refs_1_, s32[4,4096]{1,0:T(4,128)S(1)} %get-tuple-element.70.refs_2_, ...), custom_call_target="tpu_custom_call" | custom-call | bytes 1048576 | tf_op jit(solution)/shard_map/pallas_call | solution.py:443
  71.7 0.6 collective-permute-start.5
  72.3 2.4 %collective-permute-start.4 = (f32[1,4096]{1,0:T(1,128)S(1)}, f32[1,4096]{1,0:T(1,128)S(1)}, u32[]{:S(2)}, u32[]{:S(2)}) collective-permute-start(f32[1,4096]{1,0:T(1,128)S(1)} %get-tuple-element.78.p0_ref), channel_id=1, source_target_pairs={{0,2},{1,3},{2,0},{3,1},{4,6},{5,7},{6,4},{7,5},{8,10},{9,11},{10,... | collective-permute-start | bytes 49160 | tf_op jit(solution)/shard_map/ppermute | solution.py:469
  74.7 0.5 collective-permute-start.3
  75.2 2.9 %shard_map.171.solved_ref = f32[32,4096]{1,0:T(8,128)S(1)} custom-call(f32[32,4096]{1,0:T(8,128)S(1)} %get-tuple-element.76.base_ref, s32[1,4096]{1,0:T(1,128)S(1)} %get-tuple-element.52.target_ref.refs_1_.refs_6_, f32[1,4096]{1,0:T(1,128)S(1)} %get-tuple-element.77.gap_ref, f32[32,128]{1,0:T(8,128)S(1)} %get-tuple-element.48.refs_4_.inverse_ref.refs_7_.refs_10_), custom_call_target="tpu_custom_call" | custom-call | flops 3000000000 | bytes 1048576 | tf_op jit(solution)/shard_map/pallas_call | solution.py:443
  78.1 0.0 collective-permute-done.5.p3_ref
  78.1 0.0 collective-permute-done.4.p2_ref
  78.1 0.3 collective-permute-done.3.p1_ref
  78.4 0.9 %shard_map.172 = (f32[32,4096]{1,0:T(8,128)}, f32[1,4096]{1,0:T(1,128)}) custom-call(f32[32,4096]{1,0:T(8,128)S(1)} %shard_map.171.solved_ref, f32[1,4096]{1,0:T(1,128)S(1)} %get-tuple-element.78.p0_ref, f32[1,4096]{1,0:T(1,128)S(1)} %collective-permute-done.3.p1_ref, f32[1,4096]{1,0:T(1,128)S(1)} %collective-permute-done.4.p2_ref, ...), custom_call_target="tpu_custom_call" | custom-call | bytes 1048576 | tf_op jit(solution)/shard_map/pallas_call | solution.py:443
Async XLA Ops:
  33.9 6.9 %collective-permute-start.2 = (f32[1,4096]{1,0:T(1,128)S(1)}, f32[1,4096]{1,0:T(1,128)S(1)}, u32[]{:S(2)}, u32[]{:S(2)}) collective-permute-start(f32[1,4096]{1,0:T(1,128)S(1)} %get-tuple-element.54.refs_1_), channel_id=1, source_target_pairs={{0,1},{1,2},{2,3},{3,0},{4,5},{5,6},{6,7},{7,4},{8,9},{9,10},{10,1... | collective-permute-start | bytes 49160 | tf_op jit(solution)/shard_map/ppermute | solution.py:469
  34.6 6.2 %collective-permute-start.1 = (f32[1,4096]{1,0:T(1,128)S(1)}, f32[1,4096]{1,0:T(1,128)S(1)}, u32[]{:S(2)}, u32[]{:S(2)}) collective-permute-start(f32[1,4096]{1,0:T(1,128)S(1)} %get-tuple-element.54.refs_1_), channel_id=1, source_target_pairs={{0,2},{1,3},{2,0},{3,1},{4,6},{5,7},{6,4},{7,5},{8,10},{9,11},{10,... | collective-permute-start | bytes 49160 | tf_op jit(solution)/shard_map/ppermute | solution.py:469
  37.0 3.8 %collective-permute-start = (f32[1,4096]{1,0:T(1,128)S(1)}, f32[1,4096]{1,0:T(1,128)S(1)}, u32[]{:S(2)}, u32[]{:S(2)}) collective-permute-start(f32[1,4096]{1,0:T(1,128)S(1)} %get-tuple-element.54.refs_1_), channel_id=1, source_target_pairs={{0,3},{1,0},{2,1},{3,2},{4,7},{5,4},{6,5},{7,6},{8,11},{9,8},{10,9... | collective-permute-start | bytes 49160 | tf_op jit(solution)/shard_map/ppermute | solution.py:469
  48.1 20.1 %all-to-all-start.1 = ((f32[128,1,1152]{2,1,0:T(1,128)}), f32[128,1,1152]{2,1,0:T(1,128)S(1)}, u32[]{:S(2)}, u32[]{:S(2)}) async-start(f32[128,1,1152]{2,1,0:T(1,128)} %bitcast.15), calls=%async_computation.1 | async-start | bytes 1179648 | tf_op jit(solution)/shard_map/all_to_all | solution.py:459
  71.7 6.4 %collective-permute-start.5 = (f32[1,4096]{1,0:T(1,128)S(1)}, f32[1,4096]{1,0:T(1,128)S(1)}, u32[]{:S(2)}, u32[]{:S(2)}) collective-permute-start(f32[1,4096]{1,0:T(1,128)S(1)} %get-tuple-element.78.p0_ref), channel_id=1, source_target_pairs={{0,1},{1,2},{2,3},{3,0},{4,5},{5,6},{6,7},{7,4},{8,9},{9,10},{10,1... | collective-permute-start | bytes 49160 | tf_op jit(solution)/shard_map/ppermute | solution.py:469
  72.3 5.8 %collective-permute-start.4 = (f32[1,4096]{1,0:T(1,128)S(1)}, f32[1,4096]{1,0:T(1,128)S(1)}, u32[]{:S(2)}, u32[]{:S(2)}) collective-permute-start(f32[1,4096]{1,0:T(1,128)S(1)} %get-tuple-element.78.p0_ref), channel_id=1, source_target_pairs={{0,2},{1,3},{2,0},{3,1},{4,6},{5,7},{6,4},{7,5},{8,10},{9,11},{10,... | collective-permute-start | bytes 49160 | tf_op jit(solution)/shard_map/ppermute | solution.py:469
  74.7 3.7 %collective-permute-start.3 = (f32[1,4096]{1,0:T(1,128)S(1)}, f32[1,4096]{1,0:T(1,128)S(1)}, u32[]{:S(2)}, u32[]{:S(2)}) collective-permute-start(f32[1,4096]{1,0:T(1,128)S(1)} %get-tuple-element.78.p0_ref), channel_id=1, source_target_pairs={{0,3},{1,0},{2,1},{3,2},{4,7},{5,4},{6,5},{7,6},{8,11},{9,8},{10,9... | collective-permute-start | bytes 49160 | tf_op jit(solution)/shard_map/ppermute | solution.py:469

commit v4 on v3

--- a/solution.py
+++ b/solution.py
@@ -8,7 +8,6 @@
 SUB = 2
 CAP = 32
 LOW = 512
-STEP = 4096
 
 membrane_diag = 4.0
 soma_diag = 8.0
@@ -98,37 +97,66 @@
 
 
 def pick_rows(table_ref, source, comp_count, cell_dev):
+    high, low = comp_digits(source, cell_dev, comp_count)
+    return pick_hot(table_ref, high, hot(low, LOW))
+
+
+def pick_hot(table_ref, high, low_hot):
     size = table_ref.shape[0] // 2
-    pieces = []
-    for at in range(0, source.shape[1], STEP):
-        high, low = comp_digits(source[:, at : at + STEP], cell_dev, comp_count)
-        found = jnp.dot(table_ref[...], hot(low, LOW), preferred_element_type=f32)
-        rows = lax.broadcasted_iota(jnp.int32, (size, high.shape[1]), 0)
-        both = jnp.where(rows == high, found[:size] + found[size:], 0.0)
-        pieces.append(jnp.sum(both, axis=0, keepdims=True))
-    return jnp.concatenate(pieces, axis=1)
-
-
-def put_voxels(send_ref, vox, current, devices, stride):
-    block_count = vox.shape[0]
-    block_size = current.shape[0] // block_count
+    found = jnp.dot(table_ref[...], low_hot, preferred_element_type=f32)
+    rows = lax.broadcasted_iota(jnp.int32, (size, high.shape[1]), 0)
+    both = jnp.where(rows == high, found[:size] + found[size:], 0.0)
+    return jnp.sum(both, axis=0, keepdims=True)
+
+
+def block_sums(current, block_count):
+    size = current.shape[0] // block_count
+    return jnp.concatenate(
+        [
+            jnp.sum(current[k * size : (k + 1) * size], axis=0, keepdims=True)
+            for k in range(block_count)
+        ],
+        axis=0,
+    )
+
+
+def half_sums(vox, blocks, devices, half):
     owners, voxels = [], []
-    for k in range(block_count):
+    for k in range(vox.shape[0]):
         index = vox[k : k + 1, :]
-        rows = slice(k * block_size, (k + 1) * block_size)
-        high, low = halves(jnp.sum(current[rows], axis=0, keepdims=True))
+        high, low = halves(blocks[k : k + 1, :])
         mask = hits(index // LOW, devices)
         owners.append(jnp.concatenate([chosen(mask, high), chosen(mask, low)], axis=0))
-        voxels.append(hot(index % LOW, LOW))
+        voxels.append(hot(index % LOW - half * (LOW // 2), LOW // 2))
     sums = lax.dot_general(
         jnp.concatenate(owners, axis=1),
         jnp.concatenate(voxels, axis=1),
         LANES,
         preferred_element_type=f32,
     )
-    sums = sums[:devices] + sums[devices:]
-    for j in range(LOW // 128):
-        send_ref[pl.ds(j, devices, stride=stride), :] = sums[:, j * 128 : (j + 1) * 128]
+    return sums[:devices] + sums[devices:]
+
+
+def core():
+    return lax.axis_index("cells") % 2
+
+
+def put_rows(send_ref, first, values, devices, stride):
+    for j in range(values.shape[1] // 128):
+        send_ref[pl.ds(first + j, devices, stride=stride), :] = values[:, j * 128 : (j + 1) * 128]
+
+
+def own_potential(potential_ref, recv_ref, resist_ref, devices, stride, n_split, field_scale):
+    source = lax.broadcasted_iota(jnp.int32, (devices, 128), 0)
+    odd = (source // n_split) % 2 == 1
+    rows = LOW // 256
+    for j in range(rows):
+        each = recv_ref[pl.ds(j, devices, stride=stride), :]
+        for half in range(2):
+            mine = jnp.where(odd if half else ~odd, each, 0.0)
+            own = jnp.sum(mine, axis=0, keepdims=True)
+            at = half * rows + j
+            potential_ref[at : at + 1, :] = resist_ref[at : at + 1, :] * own * field_scale
 
 
 def slot_rows(values, dest_hot, rank_mask):
@@ -164,46 +192,60 @@
 
 
 def first_kernel(
-    devices, stride,
+    devices,
     volts_hbm, rate_hbm, cond_hbm, stim_hbm, vox_hbm, source_hbm, route_hbm, weight_hbm,
-    soma_v_hbm, soma_stim_hbm, resist_hbm, gate_hbm, target_hbm, axial_hbm,
+    target_hbm, soma_v_hbm, soma_stim_hbm, resist_hbm, gate_hbm, axial_hbm,
     volts_ref, rate_ref, cond_ref, stim_ref, vox_ref, source_ref, route_ref, weight_ref,
-    soma_v_ref, soma_stim_ref, resist_ref,
-    send_ref, rank_ref, gate_out, current_out, inverse_ref, soma_ref,
-    gate_ref, target_ref, axial_ref, table_ref, sems,
+    target_ref, soma_v_ref, soma_stim_ref, resist_ref,
+    rank_ref, gate_out, base_ref, blocks_ref, inverse_ref, soma_ref, other_ref,
+    gate_ref, axial_ref, sems,
 ):
     pairs = [
         (axial_hbm, axial_ref), (route_hbm, route_ref), (volts_hbm, volts_ref),
-        (source_hbm, source_ref), (target_hbm, target_ref), (weight_hbm, weight_ref),
         (gate_hbm, gate_ref), (rate_hbm, rate_ref), (cond_hbm, cond_ref), (vox_hbm, vox_ref),
-        (stim_hbm, stim_ref), (soma_v_hbm, soma_v_ref), (soma_stim_hbm, soma_stim_ref),
+        (stim_hbm, stim_ref), (source_hbm, source_ref), (target_hbm, target_ref),
+        (weight_hbm, weight_ref), (soma_v_hbm, soma_v_ref), (soma_stim_hbm, soma_stim_ref),
         (resist_hbm, resist_ref),
     ]
     copies = [pltpu.make_async_copy(a, b, sems.at[i]) for i, (a, b) in enumerate(pairs)]
     for copy in copies:
         copy.start()
-    comp_count, cell_dev = volts_ref.shape
-    rows = source_ref.shape[1]
     copies[0].wait()
     write_inverse(axial_ref[...], lax.axis_index("split"), inverse_ref, soma_ref)
     copies[1].wait()
-    rank, dest_hot = ranks_of(route_ref[...], devices)
-    rank_ref[...] = rank
-    for copy in copies[2:10]:
+    rank_ref[...], unused = ranks_of(route_ref[...], devices)
+    for copy in copies[2:8]:
         copy.wait()
     volts = volts_ref[...]
     gating, current = membrane(volts, gate_ref[...], rate_ref[...], cond_ref[...])
     gate_out[...] = gating
-    current_out[...] = current
-    put_voxels(send_ref, vox_ref[...], current, devices, stride)
-    fill_table(table_ref, volts, comp_count, cell_dev)
+    base_ref[...] = membrane_diag * volts + stim_ref[...] - current
+    blocks = block_sums(current, vox_ref.shape[0])
+    blocks_ref[...] = blocks
+    other_ref[...] = half_sums(vox_ref[...], blocks, devices, 1 - core())
+    for copy in copies[8:]:
+        copy.wait()
+
+
+def first_rows_kernel(
+    devices,
+    vox_ref, blocks_ref, volts_ref, source_ref, route_ref, target_ref, weight_ref, rank_ref,
+    own_ref, rows_ref, table_ref,
+):
+    comp_count, cell_dev = volts_ref.shape
+    own_ref[...] = half_sums(vox_ref[...], blocks_ref[...], devices, core())
+    fill_table(table_ref, volts_ref[...], comp_count, cell_dev)
     weight = weight_ref[...]
     sent = weight * pick_rows(table_ref, source_ref[...], comp_count, cell_dev)
-    slots = slot_rows([target_ref[...].astype(f32), weight, sent], dest_hot, hits(rank, CAP))
+    values = [target_ref[...].astype(f32), weight, sent]
+    slots = slot_rows(values, hot(route_ref[...], devices), hits(rank_ref[...], CAP))
     slots.append(jnp.zeros((128 - 3 * CAP, devices), f32))
-    send_ref[pl.ds(LOW // 128, devices, stride=stride), :] = jnp.concatenate(slots, axis=0).T
-    for copy in copies[10:]:
-        copy.wait()
+    rows_ref[...] = jnp.concatenate(slots, axis=0).T
+
+
+def first_send_kernel(devices, stride, own_ref, other_ref, rows_ref, send_ref):
+    put_rows(send_ref, 0, own_ref[...] + other_ref[...], devices, stride)
+    put_rows(send_ref, stride - 1, rows_ref[...], devices, stride)
 
 
 def wide(slots):
@@ -242,35 +284,28 @@
 
 
 def second_kernel(
-    devices, stride, field_scale,
-    recv_ref, volts_ref, stim_ref, current_ref, inverse_ref, soma_ref, resist_ref,
-    base_ref, partial_ref, target_ref, weight_ref, factor_ref, gap_ref, potential_ref,
-    table_ref,
-):
-    comp_count, cell_dev = volts_ref.shape
-    slots = recv_ref[pl.ds(LOW // 128, devices, stride=stride), :].T
+    devices, stride, n_split, field_scale,
+    recv_ref, base_ref, table_ref, inverse_ref, soma_ref, resist_ref,
+    partial_ref, target_ref, weight_ref, factor_ref, gap_ref, potential_ref,
+):
+    comp_count, cell_dev = base_ref.shape
+    slots = recv_ref[pl.ds(stride - 1, devices, stride=stride), :].T
     target = wide(slots[:CAP].astype(jnp.int32))
     target_ref[...] = target
     weight = wide(slots[CAP : 2 * CAP])
     weight_ref[...] = weight
-    volts = volts_ref[...]
-    base = membrane_diag * volts + stim_ref[...] - current_ref[...]
-    base_ref[...] = base
     comps = lax.broadcasted_iota(jnp.int32, (comp_count, CAP * devices), 0)
     factor = jnp.sum(
         jnp.where(comps == target // cell_dev, inverse_ref[:, 0:1], 0.0),
         axis=0, keepdims=True,
     )
     factor_ref[...] = factor
-    fill_table(table_ref, volts, comp_count, cell_dev)
     here = pick_rows(table_ref, target, comp_count, cell_dev)
     gap = wide(slots[2 * CAP : 3 * CAP]) - weight * here
     gap_ref[...] = gap
-    first = head_term(inverse_ref, base) + add_heads(factor * gap, target, cell_dev)
+    first = head_term(inverse_ref, base_ref[...]) + add_heads(factor * gap, target, cell_dev)
     partial_ref[...] = soma_ref[1:2, 0:1] * first
-    for j in range(LOW // 128):
-        own = jnp.sum(recv_ref[pl.ds(j, devices, stride=stride), :], axis=0, keepdims=True)
-        potential_ref[j : j + 1, :] = resist_ref[j : j + 1, :] * own * field_scale
+    own_potential(potential_ref, recv_ref, resist_ref, devices, stride, n_split, field_scale)
 
 
 def solve(inverse_ref, rhs):
@@ -326,41 +361,58 @@
 
 
 def third_kernel(
-    devices, stride,
+    devices,
     solved_ref, p0_ref, p1_ref, p2_ref, p3_ref, soma_v_ref, soma_stim_ref,
-    inverse_ref, soma_ref, gate_ref, rate_ref, cond_ref, stim_ref,
-    vox_ref, source_ref, route_ref, rank_ref, weight_ref, potential_ref,
-    send_ref, gate_hbm, soma_out, base_ref, table_ref,
+    inverse_ref, soma_ref, gate_ref, rate_ref, cond_ref, stim_ref, vox_ref,
+    gate_hbm, soma_out, base_ref, blocks_ref, volts_ref, other_ref,
     gate_out, sem,
 ):
-    comp_count, cell_dev = solved_ref.shape
     soma = next_soma(
         soma_v_ref[...], soma_stim_ref[...],
         [p0_ref[...], p1_ref[...], p2_ref[...], p3_ref[...]], soma_ref[0:1, 0:1],
     )
     soma_out[...] = soma
     volts = solved_ref[...] + soma_ref[1:2, 0:1] * inverse_ref[:, 0:1] * soma
-    fill_table(table_ref, volts, comp_count, cell_dev)
+    volts_ref[...] = volts
     gating, current = membrane(volts, gate_ref[...], rate_ref[...], cond_ref[...])
     gate_out[...] = gating
     copy = pltpu.make_async_copy(gate_out, gate_hbm, sem)
     copy.start()
     base_ref[...] = membrane_diag * volts + stim_ref[...] - current
+    blocks = block_sums(current, vox_ref.shape[0])
+    blocks_ref[...] = blocks
+    other_ref[...] = half_sums(vox_ref[...], blocks, devices, 1 - core())
+    copy.wait()
+
+
+def third_rows_kernel(
+    devices,
+    vox_ref, blocks_ref, volts_ref, source_ref, route_ref, weight_ref, rank_ref,
+    own_ref, rows_ref, table_ref,
+):
+    comp_count, cell_dev = volts_ref.shape
+    own_ref[...] = half_sums(vox_ref[...], blocks_ref[...], devices, core())
+    fill_table(table_ref, volts_ref[...], comp_count, cell_dev)
     sent = weight_ref[...] * pick_rows(table_ref, source_ref[...], comp_count, cell_dev)
     slots = slot_rows([sent], hot(route_ref[...], devices), hits(rank_ref[...], CAP))
     slots.append(jnp.zeros((128 - CAP, devices), f32))
-    parts = LOW // 128
-    send_ref[pl.ds(2 * parts, devices, stride=stride), :] = jnp.concatenate(slots, axis=0).T
-    put_voxels(send_ref, vox_ref[...], current, devices, stride)
-    for j in range(parts):
-        send_ref[pl.ds(parts + j, devices, stride=stride), :] = jnp.broadcast_to(
-            potential_ref[j : j + 1, :], (devices, 128)
-        )
-    copy.wait()
+    rows_ref[...] = jnp.concatenate(slots, axis=0).T
+
+
+def third_send_kernel(
+    devices, stride, own_ref, other_ref, rows_ref, potential_ref, target_ref,
+    send_ref, target_out,
+):
+    target_out[...] = target_ref[...]
+    put_rows(send_ref, 0, own_ref[...] + other_ref[...], devices, stride)
+    for j in range(LOW // 128):
+        each = jnp.broadcast_to(potential_ref[j : j + 1, :], (devices, 128))
+        put_rows(send_ref, LOW // 256 + j, each, devices, stride)
+    put_rows(send_ref, stride - 1, rows_ref[...], devices, stride)
 
 
 def fourth_kernel(
-    devices, stride, field_scale,
+    devices, stride, n_split, field_scale,
     recv_ref, here_ref, group_ref, column_ref, within_ref, heavy_ref,
     target_ref, weight_ref, factor_ref, base_ref, inverse_ref, soma_ref, resist_ref,
     rhs_ref, partial_ref, gap_ref, potential_ref,
@@ -369,7 +421,8 @@
     block_count = group_ref.shape[0]
     block_size = comp_count // block_count
     parts = LOW // 128
-    slots = recv_ref[pl.ds(2 * parts, devices, stride=stride), :].T
+    first = LOW // 256
+    slots = recv_ref[pl.ds(stride - 1, devices, stride=stride), :].T
     gap = wide(slots[:CAP]) - weight_ref[...] * here_ref[...]
     gap_ref[...] = gap
     half = devices // 2
@@ -377,14 +430,14 @@
     sides = []
     for side in range(2):
         owners = [
-            recv_ref[pl.ds(side * stride + parts + j, half, stride=2 * stride), :]
+            recv_ref[pl.ds(side * stride + first + j, half, stride=2 * stride), :]
             for j in range(parts)
         ]
         sides.append(look_up(owners, within_ref[:half, side * 128 : (side + 1) * 128]))
     heavy = lax.broadcasted_iota(jnp.int32, (devices, 128), 0) == heavy_ref[...]
     owner = []
     for j in range(parts):
-        rows = recv_ref[pl.ds(parts + j, devices, stride=stride), :]
+        rows = recv_ref[pl.ds(first + j, devices, stride=stride), :]
         one = jnp.sum(jnp.where(heavy, rows, 0.0), axis=0, keepdims=True)
         owner.append(jnp.broadcast_to(one, (size - half, 128)))
     rest = look_up(owner, within_ref[half:, :128])
@@ -410,9 +463,7 @@
     rhs_ref[...] = rhs
     heads = add_heads(factor_ref[...] * gap, target_ref[...], cell_dev)
     partial_ref[...] = soma_ref[1:2, 0:1] * (head_term(inverse_ref, rhs) + heads)
-    for j in range(parts):
-        own = jnp.sum(recv_ref[pl.ds(j, devices, stride=stride), :], axis=0, keepdims=True)
-        potential_ref[j : j + 1, :] = resist_ref[j : j + 1, :] * own * field_scale
+    own_potential(potential_ref, recv_ref, resist_ref, devices, stride, n_split, field_scale)
 
 
 def last_kernel(
@@ -462,6 +513,10 @@
     return flat.reshape(send.shape)
 
 
+def other_core(array, n_cells):
+    return lax.ppermute(array, "cells", [(i, i ^ 1) for i in range(n_cells)])
+
+
 def split_terms(partial, n_split):
     terms = [partial]
     for k in range(n_split - 1, 0, -1):
@@ -475,7 +530,8 @@
     axial_conductance, gap_source, gap_route, gap_target, gap_conductance, vox_index, field_resist,
 ):
     n_split = lax.axis_size("split")
-    devices = lax.axis_size("cells") * n_split
+    n_cells = lax.axis_size("cells")
+    devices = n_cells * n_split
     comp_count, cell_dev = voltage.shape[1:]
     rows = gap_source.shape[0]
     vox_dev = field_resist.shape[0]
@@ -503,46 +559,69 @@
     row = ((1, CAP * devices), f32, False)
     row_i32 = ((1, CAP * devices), i32, False)
 
-    stride = parts + 1
-    kept = (volts, rate, cond, stim, vox, source, route, weight, soma_v, soma_stim, resist)
-    used = (gate, target, axial_conductance)
+    blocks_shape = (vox.shape, f32, False)
+    sums = ((devices, vox_dev // 2), f32, False)
+    gap_rows = ((devices, 128), f32, False)
+    table_out = (table.shape, bf16, False)
+
+    stride = parts // 2 + 1
+    kept = (
+        volts, rate, cond, stim, vox, source, route, weight, target, soma_v, soma_stim, resist,
+    )
+    used = (gate, axial_conductance)
     outs = call(
-        bind(first_kernel, devices, stride),
+        bind(first_kernel, devices),
         [True] * (len(kept) + len(used)),
         [(x.shape, x.dtype, False) for x in kept]
         + [
-            ((devices * stride, 128), f32, False), ((1, rows), i32, False), full, full,
-            ((comp_count, 128), f32, False), ((2, 128), f32, False),
+            ((1, rows), i32, False), full, full, blocks_shape,
+            ((comp_count, 128), f32, False), ((2, 128), f32, False), sums,
         ],
         [pltpu.VMEM(x.shape, x.dtype) for x in used]
-        + [table, pltpu.SemaphoreType.DMA((len(kept) + len(used),))],
+        + [pltpu.SemaphoreType.DMA((len(kept) + len(used),))],
     )(*kept, *used)
-    volts, rate, cond, stim, vox, source, route, weight, soma_v, soma_stim, resist = outs[: len(kept)]
-    send, rank, gate, current, inverse, soma_consts = outs[len(kept) :]
+    (
+        volts, rate, cond, stim, vox, source, route, weight, target, soma_v, soma_stim, resist,
+    ) = outs[: len(kept)]
+    rank, gate, base, blocks, inverse, soma_consts, other = outs[len(kept) :]
+    other = other_core(other, n_cells)
+    own, slot_rows_out, volts_table = call(
+        bind(first_rows_kernel, devices), [False] * 8, [sums, gap_rows, table_out], flops=4 * 10**9
+    )(vox, blocks, volts, source, route, target, weight, rank)
+    (send,) = call(
+        bind(first_send_kernel, devices, stride), [False] * 3,
+        [((devices * stride, 128), f32, False)],
+    )(own, other, slot_rows_out)
     received = exchange(send, devices)
-    base, partial, slot_target, slot_weight, factor, gap, potential = call(
-        bind(second_kernel, devices, stride, field_scale),
-        [False] * 7,
-        [full, line, row_i32, row, row, row, quads],
-        [table],
-    )(received, volts, stim, current, inverse, soma_consts, resist)
+    partial, slot_target, slot_weight, factor, gap, potential = call(
+        bind(second_kernel, devices, stride, n_split, field_scale),
+        [False] * 6,
+        [line, row_i32, row, row, row, quads],
+    )(received, base, volts_table, inverse, soma_consts, resist)
     terms = split_terms(partial, n_split)
     solve = call(solve_kernel, [False] * 4, [full], flops=3 * 10**9)
     (solved,) = solve(base, slot_target, gap, inverse)
 
-    stride = 2 * parts + 1
+    stride = parts // 2 + parts + 1
     operands = (
-        solved, *terms, soma_v, soma_stim, inverse, soma_consts,
-        gate, rate, cond, stim, vox, source, route, rank, weight, potential,
-    )
-    send, gate, soma, base, volts_table = call(
-        bind(third_kernel, devices, stride),
+        solved, *terms, soma_v, soma_stim, inverse, soma_consts, gate, rate, cond, stim, vox,
+    )
+    gate, soma, base, blocks, volts, other = call(
+        bind(third_kernel, devices),
         [False] * len(operands),
-        [((devices * stride, 128), f32, False), full_hbm, line, full, (table.shape, bf16, False)],
+        [full_hbm, line, full, blocks_shape, full, sums],
         [field, pltpu.SemaphoreType.DMA],
     )(*operands)
+    other = other_core(other, n_cells)
+    own, slot_rows_out, volts_table = call(
+        bind(third_rows_kernel, devices), [False] * 7, [sums, gap_rows, table_out], flops=4 * 10**9
+    )(vox, blocks, volts, source, route, weight, rank)
+    send, slot_target = call(
+        bind(third_send_kernel, devices, stride), [False] * 5,
+        [((devices * stride, 128), f32, False), row_i32],
+    )(own, other, slot_rows_out, potential, slot_target)
     received = exchange(send, devices)
-    groups = devices // 2 + 8
+    groups = devices // 2 + 16
     here, group, column, within, heavy = call(
         bind(beside_kernel, devices),
         [False] * 4,
@@ -553,7 +632,7 @@
         flops=8 * 10**9,
     )(volts_table, slot_target, base, vox)
     rhs, partial, gap, potential = call(
-        bind(fourth_kernel, devices, stride, field_scale),
+        bind(fourth_kernel, devices, stride, n_split, field_scale),
         [False] * 13,
         [full, line, row, quads],
     )(

time: 79.7 us -> 77 us (0.966)
  waiting for transfers between devices: 4.76 us -> 3.22 us
  blocking collectives: 22.2 us -> 21 us
    all_to_all x1, waiting for transfers between devices: 4.46 us -> 3.04 us  [exchange(): lax.all_to_all(send.reshape(devices, send.size // devices), AXES, split_a...]
    all_to_all x1, blocking collectives: 22.2 us -> 21 us  [exchange(): lax.all_to_all(send.reshape(devices, send.size // devices), AXES, split_a...]
    pallas_call x8 -> x12, Pallas kernels: 38 us -> 37.7 us  [placed(): run(*[pltpu.with_memory_space_constraint(x, pltpu.HBM) if stays else x fo...]
  transfers between devices with their start and end apart: 7 -> 9, of which waited for: 2 -> 2; matrix products, arithmetic and copies ran while one was open for 0% -> 0% of each run, Pallas kernels for 19% -> 30%
where the time goes in v4:
time: 77 us; the launch traced here: 76.7 us
  Pallas kernels  37.7 us (49%)
  blocking collectives  21 us (27%)
  starting transfers between devices  14 us (18%)
  waiting for transfers between devices  3.22 us (4%)
    pallas_call x12, Pallas kernels, placed(): run(*[pltpu.with_memory_space_constraint(x, pltpu.HBM) if stays else x fo...  37.7 us
    all_to_all x1, blocking collectives, exchange(): lax.all_to_all(send.reshape(devices, send.size // devices), AXES, split_a...  21 us
    ppermute x6, starting transfers between devices, split_terms(): terms.append(lax.ppermute(partial, 'split', pairs))  7.66 us
    all_to_all x1, starting transfers between devices, exchange(): lax.all_to_all(send.reshape(devices, send.size // devices), AXES, split_a...  6.22 us
    all_to_all x1, waiting for transfers between devices, exchange(): lax.all_to_all(send.reshape(devices, send.size // devices), AXES, split_a...  3.04 us
  transfers between devices with their start and end apart: 9, of which 2 were waited for; matrix products, arithmetic and copies ran while one was open for 0% of the time, Pallas kernels for 30%

profile of v4, /device:TPU:0, one launch (start us, length us, event | category | flops | bytes accessed | tf_op | source)
XLA Modules:
  0.0 76.7 jit_solution(17178299734912987234)
XLA Ops:
  0.6 4.3 %shard_map.165 = (f32[32,4096]{1,0:T(8,128)S(1)}, f32[32,4096]{1,0:T(8,128)S(1)}, f32[32,4096]{1,0:T(8,128)S(1)}, f32[32,4096]{1,0:T(8,128)S(1)}, s32[4,4096]{1,...) custom-call(f32[32,4096]{1,0:T(8,128)} %bitcast.24, ...), custom_call_target="tpu_custom_call" | custom-call | bytes 1048576 | tf_op jit(solution)/shard_map/pallas_call | solution.py:494
  4.9 0.1 collective-permute-start
  5.0 3.8 %shard_map.166 = (f32[128,256]{1,0:T(8,128)S(1)}, f32[128,128]{1,0:T(8,128)S(1)}, bf16[512,512]{1,0:T(8,128)(2,1)S(1)}) custom-call(s32[4,4096]{1,0:T(4,128)S(1)} %get-tuple-element.54.refs_0_.refs_13_.refs_3_, f32[4,4096]{1,0:T(4,128)S(1)} %get-tuple-element.56.refs_1_, f32[32,4096]{1,0:T(8,128)S(1)} %get-tuple-element.57.refs_2_, ...), custom_call_target="tpu_custom_call" | custom-call | flops 4000000000 | bytes 1048576 | tf_op jit(solution)/shard_map/pallas_call | solution.py:494
  8.8 0.0 collective-permute-done.refs_1_
  8.8 21.0 %all_to_all.18 = f32[128,1,384]{2,1,0:T(1,128)S(1)} all-to-all(f32[128,1,384]{2,1,0:T(1,128)S(1)} %bitcast.22), channel_id=1, replica_groups=mesh['cells'=32,'split'=4] {'cells','split'}, dimensions={0} | all-to-all | bytes 393216 | tf_op jit(solution)/shard_map/all_to_all | solution.py:510
  29.8 3.0 %shard_map.168 = (f32[1,4096]{1,0:T(1,128)S(1)}, s32[1,4096]{1,0:T(1,128)S(1)}, f32[1,4096]{1,0:T(1,128)S(1)}, f32[1,4096]{1,0:T(1,128)S(1)}, f32[1,4096]{1,0:T(1,128)S(1)}, /*index=5*/f32[4,128]{1,0:T(4,128)S(1)}) custom-call(f32[384,128]{1,0:T(8,128)S(1)} %bitcast.23, f32[32,4096]{1,0:T(8,128)S(1)} %get-tuple-element.55.refs_1_.base_ref, ...), custom_call_target="tpu_custom_call" | custom-call | bytes 1048576 | tf_op jit(solution)/shard_map/pallas_call | solution.py:494
  32.8 0.7 collective-permute-start.3
  33.5 2.3 %collective-permute-start.2 = (f32[1,4096]{1,0:T(1,128)S(1)}, f32[1,4096]{1,0:T(1,128)S(1)}, u32[]{:S(2)}, u32[]{:S(2)}) collective-permute-start(f32[1,4096]{1,0:T(1,128)S(1)} %get-tuple-element.72.refs_1_), channel_id=1, source_target_pairs={{0,2},{1,3},{2,0},{3,1},{4,6},{5,7},{6,4},{7,5},{8,10},{9,11},{10,... | collective-permute-start | bytes 49160 | tf_op jit(solution)/shard_map/ppermute | solution.py:524
  35.8 1.1 %collective-permute-start.1 = (f32[1,4096]{1,0:T(1,128)S(1)}, f32[1,4096]{1,0:T(1,128)S(1)}, u32[]{:S(2)}, u32[]{:S(2)}) collective-permute-start(f32[1,4096]{1,0:T(1,128)S(1)} %get-tuple-element.72.refs_1_), channel_id=1, source_target_pairs={{0,3},{1,0},{2,1},{3,2},{4,7},{5,4},{6,5},{7,6},{8,11},{9,8},{10,9... | collective-permute-start | bytes 49160 | tf_op jit(solution)/shard_map/ppermute | solution.py:524
  36.9 2.9 %shard_map.169.refs_0_ = f32[32,4096]{1,0:T(8,128)S(1)} custom-call(f32[32,4096]{1,0:T(8,128)S(1)} %get-tuple-element.55.refs_1_.base_ref, s32[1,4096]{1,0:T(1,128)S(1)} %get-tuple-element.70.target_ref.refs_4_, f32[1,4096]{1,0:T(1,128)S(1)} %get-tuple-element.71.gap_ref, f32[32,128]{1,0:T(8,128)S(1)} %get-tuple-element.67.refs_3_.inverse_ref.refs_7_.refs_10_), custom_call_target="tpu_custom_call" | custom-call | flops 3000000000 | bytes 1048576 | tf_op jit(solution)/shard_map/pallas_call | solution.py:494
  39.8 0.0 collective-permute-done.3.refs_4_
  39.8 0.0 collective-permute-done.2.refs_3_
  39.8 0.0 collective-permute-done.1.refs_2_
  39.8 2.5 %shard_map.170 = (f32[32,4096]{1,0:T(8,128)}, f32[1,4096]{1,0:T(1,128)S(1)}, f32[32,4096]{1,0:T(8,128)S(1)}, f32[4,4096]{1,0:T(4,128)S(1)}, f32[32,4096]{1,0:T(8,128)S(1)}, /*index=5*/f32[128,256]{1,0:T(8,128)S(1)}) custom-call(f32[32,4096]{1,0:T(8,128)S(1)} %shard_map.169.refs_0_, f32[1,4096]{1,0:T(1,128)S(1)} %get-tuple-element.72.refs_1_, ...), custom_call_target="tpu_custom_call" | custom-call | bytes 1048576 | tf_op jit(solution)/shard_map/pallas_call | solution.py:494
  42.3 0.1 collective-permute-start.4
  42.4 3.7 %shard_map.171 = (f32[128,256]{1,0:T(8,128)S(1)}, f32[128,128]{1,0:T(8,128)S(1)}, bf16[512,512]{1,0:T(8,128)(2,1)S(1)}) custom-call(s32[4,4096]{1,0:T(4,128)S(1)} %get-tuple-element.54.refs_0_.refs_13_.refs_3_, f32[4,4096]{1,0:T(4,128)S(1)} %get-tuple-element.79.refs_1_, f32[32,4096]{1,0:T(8,128)S(1)} %get-tuple-element.80.refs_2_, ...), custom_call_target="tpu_custom_call" | custom-call | flops 4000000000 | bytes 1048576 | tf_op jit(solution)/shard_map/pallas_call | solution.py:494
  46.1 0.0 collective-permute-done.4.refs_1_
  46.1 0.8 %shard_map.172 = (f32[896,128]{1,0:T(8,128)}, s32[1,4096]{1,0:T(1,128)S(1)}) custom-call(f32[128,256]{1,0:T(8,128)S(1)} %get-tuple-element.81.refs_0_, f32[128,256]{1,0:T(8,128)S(1)} %collective-permute-done.4.refs_1_, f32[128,128]{1,0:T(8,128)S(1)} %get-tuple-element.83.refs_2_, f32[4,128]{1,0:T(4,128)S(1)} %get-tuple-element.84.refs_3_, ...), custom_call_target="tpu_custom_call" | custom-call | bytes 1048576 | tf_op jit(solution)/shard_map/pallas_call | solution.py:494
  46.9 6.2 %all-to-all-start.1 = ((f32[128,1,896]{2,1,0:T(1,128)}), f32[128,1,896]{2,1,0:T(1,128)S(1)}, u32[]{:S(2)}, u32[]{:S(2)}) async-start(f32[128,1,896]{2,1,0:T(1,128)} %bitcast.15), calls=%async_computation.1 | async-start | bytes 917504 | tf_op jit(solution)/shard_map/all_to_all | solution.py:510
  53.2 9.3 %shard_map.173 = (f32[1,4096]{1,0:T(1,128)S(1)}, s32[4,4096]{1,0:T(4,128)S(1)}, s32[4,4096]{1,0:T(4,128)S(1)}, s32[80,256]{1,0:T(8,128)S(1)}, s32[1,1]{1,0:T(1,128)}) custom-call(bf16[512,512]{1,0:T(8,128)(2,1)S(1)} %get-tuple-element.86.refs_0_, s32[1,4096]{1,0:T(1,128)S(1)} %get-tuple-element.87.refs_1_.refs_6_.target_ref, ...), custom_call_target="tpu_custom_call" | custom-call | flops 8000000000 | bytes 1048576 | tf_op jit(solution)/shard_map/pallas_call | solution.py:494
  62.5 3.0 %all-to-all-done.1 = f32[128,1,896]{2,1,0:T(1,128)S(1)} async-done(((f32[128,1,896]{2,1,0:T(1,128)}), f32[128,1,896]{2,1,0:T(1,128)S(1)}, u32[]{:S(2)}, u32[]{:S(2)}) %all-to-all-start.1) | async-done | bytes 458784 | tf_op jit(solution)/shard_map/all_to_all | solution.py:510
  65.6 3.4 %shard_map.174 = (f32[32,4096]{1,0:T(8,128)S(1)}, f32[1,4096]{1,0:T(1,128)S(1)}, f32[1,4096]{1,0:T(1,128)S(1)}, f32[4,128]{1,0:T(4,128)}) custom-call(f32[896,128]{1,0:T(8,128)S(1)} %bitcast.21, f32[1,4096]{1,0:T(1,128)S(1)} %get-tuple-element.89.refs_1_, s32[4,4096]{1,0:T(4,128)S(1)} %get-tuple-element.90.refs_2_, s32[4,4096]{1,0:T(4,128)S(1)} %get-tuple-element.91.refs_3_, ...), custom_call_target="tpu_custom_call" | custom-call | bytes 1048576 | tf_op jit(solution)/shard_map/pallas_call | solution.py:494
  69.0 0.6 collective-permute-start.7
  69.6 2.4 %collective-permute-start.6 = (f32[1,4096]{1,0:T(1,128)S(1)}, f32[1,4096]{1,0:T(1,128)S(1)}, u32[]{:S(2)}, u32[]{:S(2)}) collective-permute-start(f32[1,4096]{1,0:T(1,128)S(1)} %get-tuple-element.98.p0_ref), channel_id=1, source_target_pairs={{0,2},{1,3},{2,0},{3,1},{4,6},{5,7},{6,4},{7,5},{8,10},{9,11},{10,... | collective-permute-start | bytes 49160 | tf_op jit(solution)/shard_map/ppermute | solution.py:524
  72.0 0.6 collective-permute-start.5
  72.6 2.9 %shard_map.175.solved_ref = f32[32,4096]{1,0:T(8,128)S(1)} custom-call(f32[32,4096]{1,0:T(8,128)S(1)} %get-tuple-element.96.base_ref, s32[1,4096]{1,0:T(1,128)S(1)} %get-tuple-element.87.refs_1_.refs_6_.target_ref, f32[1,4096]{1,0:T(1,128)S(1)} %get-tuple-element.97.gap_ref, f32[32,128]{1,0:T(8,128)S(1)} %get-tuple-element.67.refs_3_.inverse_ref.refs_7_.refs_10_), custom_call_target="tpu_custom_call" | custom-call | flops 3000000000 | bytes 1048576 | tf_op jit(solution)/shard_map/pallas_call | solution.py:494
  75.5 0.0 collective-permute-done.7.p3_ref
  75.6 0.0 collective-permute-done.6.p2_ref
  75.6 0.2 collective-permute-done.5.p1_ref
  75.7 0.9 %shard_map.176 = (f32[32,4096]{1,0:T(8,128)}, f32[1,4096]{1,0:T(1,128)}) custom-call(f32[32,4096]{1,0:T(8,128)S(1)} %shard_map.175.solved_ref, f32[1,4096]{1,0:T(1,128)S(1)} %get-tuple-element.98.p0_ref, f32[1,4096]{1,0:T(1,128)S(1)} %collective-permute-done.5.p1_ref, f32[1,4096]{1,0:T(1,128)S(1)} %collective-permute-done.6.p2_ref, ...), custom_call_target="tpu_custom_call" | custom-call | bytes 1048576 | tf_op jit(solution)/shard_map/pallas_call | solution.py:494
  (1 shorter events, 0.0 us)
Async XLA Ops:
  4.9 3.9 %collective-permute-start = (f32[128,256]{1,0:T(8,128)S(1)}, f32[128,256]{1,0:T(8,128)S(1)}, u32[]{:S(2)}, u32[]{:S(2)}) collective-permute-start(f32[128,256]{1,0:T(8,128)S(1)} %get-tuple-element.64), channel_id=1, source_target_pairs={{0,4},{4,0},{8,12},{12,8},{16,20},{20,16},{24,28},{28,24},{32,36},... | collective-permute-start | bytes 393224 | tf_op jit(solution)/shard_map/ppermute | solution.py:517
  32.8 7.0 %collective-permute-start.3 = (f32[1,4096]{1,0:T(1,128)S(1)}, f32[1,4096]{1,0:T(1,128)S(1)}, u32[]{:S(2)}, u32[]{:S(2)}) collective-permute-start(f32[1,4096]{1,0:T(1,128)S(1)} %get-tuple-element.72.refs_1_), channel_id=1, source_target_pairs={{0,1},{1,2},{2,3},{3,0},{4,5},{5,6},{6,7},{7,4},{8,9},{9,10},{10,1... | collective-permute-start | bytes 49160 | tf_op jit(solution)/shard_map/ppermute | solution.py:524
  33.5 6.3 %collective-permute-start.2 = (f32[1,4096]{1,0:T(1,128)S(1)}, f32[1,4096]{1,0:T(1,128)S(1)}, u32[]{:S(2)}, u32[]{:S(2)}) collective-permute-start(f32[1,4096]{1,0:T(1,128)S(1)} %get-tuple-element.72.refs_1_), channel_id=1, source_target_pairs={{0,2},{1,3},{2,0},{3,1},{4,6},{5,7},{6,4},{7,5},{8,10},{9,11},{10,... | collective-permute-start | bytes 49160 | tf_op jit(solution)/shard_map/ppermute | solution.py:524
  35.8 4.0 %collective-permute-start.1 = (f32[1,4096]{1,0:T(1,128)S(1)}, f32[1,4096]{1,0:T(1,128)S(1)}, u32[]{:S(2)}, u32[]{:S(2)}) collective-permute-start(f32[1,4096]{1,0:T(1,128)S(1)} %get-tuple-element.72.refs_1_), channel_id=1, source_target_pairs={{0,3},{1,0},{2,1},{3,2},{4,7},{5,4},{6,5},{7,6},{8,11},{9,8},{10,9... | collective-permute-start | bytes 49160 | tf_op jit(solution)/shard_map/ppermute | solution.py:524
  42.3 3.8 %collective-permute-start.4 = (f32[128,256]{1,0:T(8,128)S(1)}, f32[128,256]{1,0:T(8,128)S(1)}, u32[]{:S(2)}, u32[]{:S(2)}) collective-permute-start(f32[128,256]{1,0:T(8,128)S(1)} %get-tuple-element.82), channel_id=1, source_target_pairs={{0,4},{4,0},{8,12},{12,8},{16,20},{20,16},{24,28},{28,24},{32,36},... | collective-permute-start | bytes 393224 | tf_op jit(solution)/shard_map/ppermute | solution.py:517
  46.9 18.6 %all-to-all-start.1 = ((f32[128,1,896]{2,1,0:T(1,128)}), f32[128,1,896]{2,1,0:T(1,128)S(1)}, u32[]{:S(2)}, u32[]{:S(2)}) async-start(f32[128,1,896]{2,1,0:T(1,128)} %bitcast.15), calls=%async_computation.1 | async-start | bytes 917504 | tf_op jit(solution)/shard_map/all_to_all | solution.py:510
  69.0 6.6 %collective-permute-start.7 = (f32[1,4096]{1,0:T(1,128)S(1)}, f32[1,4096]{1,0:T(1,128)S(1)}, u32[]{:S(2)}, u32[]{:S(2)}) collective-permute-start(f32[1,4096]{1,0:T(1,128)S(1)} %get-tuple-element.98.p0_ref), channel_id=1, source_target_pairs={{0,1},{1,2},{2,3},{3,0},{4,5},{5,6},{6,7},{7,4},{8,9},{9,10},{10,1... | collective-permute-start | bytes 49160 | tf_op jit(solution)/shard_map/ppermute | solution.py:524
  69.6 6.0 %collective-permute-start.6 = (f32[1,4096]{1,0:T(1,128)S(1)}, f32[1,4096]{1,0:T(1,128)S(1)}, u32[]{:S(2)}, u32[]{:S(2)}) collective-permute-start(f32[1,4096]{1,0:T(1,128)S(1)} %get-tuple-element.98.p0_ref), channel_id=1, source_target_pairs={{0,2},{1,3},{2,0},{3,1},{4,6},{5,7},{6,4},{7,5},{8,10},{9,11},{10,... | collective-permute-start | bytes 49160 | tf_op jit(solution)/shard_map/ppermute | solution.py:524
  72.0 3.7 %collective-permute-start.5 = (f32[1,4096]{1,0:T(1,128)S(1)}, f32[1,4096]{1,0:T(1,128)S(1)}, u32[]{:S(2)}, u32[]{:S(2)}) collective-permute-start(f32[1,4096]{1,0:T(1,128)S(1)} %get-tuple-element.98.p0_ref), channel_id=1, source_target_pairs={{0,3},{1,0},{2,1},{3,2},{4,7},{5,4},{6,5},{7,6},{8,11},{9,8},{10,9... | collective-permute-start | bytes 49160 | tf_op jit(solution)/shard_map/ppermute | solution.py:524

commit v5 on v4

--- a/solution.py
+++ b/solution.py
@@ -324,7 +324,7 @@
 def beside_kernel(
     devices,
     table_ref, target_ref, cells_ref, vox_ref,
-    here_ref, group_ref, column_ref, within_ref, heavy_ref,
+    here_ref, group_ref, column_ref, within_ref,
 ):
     comp_count, cell_dev = cells_ref.shape
     here_ref[...] = pick_rows(table_ref, target_ref[...], comp_count, cell_dev)
@@ -338,13 +338,15 @@
     for k in range(block_count):
         group_ref[k : k + 1, :] = group[:, k * cell_dev : (k + 1) * cell_dev]
         column_ref[k : k + 1, :] = column[:, k * cell_dev : (k + 1) * cell_dev]
-    heavy_ref[...] = jnp.max(jnp.where(over, owner, -1), axis=1, keepdims=True)
+    heavy = jnp.max(jnp.where(over, owner, -1), axis=1, keepdims=True)
     size = within_ref.shape[0]
     mask = hits(group, size)
     high, low = halves((vox % LOW).astype(f32))
     left = jnp.concatenate([chosen(mask, high), chosen(mask, low)], axis=0)
     laid = lax.dot_general(left, hot(column, 256), LANES, preferred_element_type=f32)
+    half = devices // 2
     within_ref[...] = (laid[:size] + laid[size:]).astype(jnp.int32)
+    within_ref[half:, 128:] = jnp.broadcast_to(heavy, (size - half, 128))
 
 
 def look_up(parts, index):
@@ -413,7 +415,7 @@
 
 def fourth_kernel(
     devices, stride, n_split, field_scale,
-    recv_ref, here_ref, group_ref, column_ref, within_ref, heavy_ref,
+    recv_ref, here_ref, group_ref, column_ref, within_ref,
     target_ref, weight_ref, factor_ref, base_ref, inverse_ref, soma_ref, resist_ref,
     rhs_ref, partial_ref, gap_ref, potential_ref,
 ):
@@ -434,7 +436,7 @@
             for j in range(parts)
         ]
         sides.append(look_up(owners, within_ref[:half, side * 128 : (side + 1) * 128]))
-    heavy = lax.broadcasted_iota(jnp.int32, (devices, 128), 0) == heavy_ref[...]
+    heavy = lax.broadcasted_iota(jnp.int32, (devices, 128), 0) == within_ref[half : half + 1, 128:129]
     owner = []
     for j in range(parts):
         rows = recv_ref[pl.ds(first + j, devices, stride=stride), :]
@@ -468,8 +470,9 @@
 
 def last_kernel(
     solved_ref, p0_ref, p1_ref, p2_ref, p3_ref, soma_v_ref, soma_stim_ref,
-    inverse_ref, soma_ref, volts_ref, soma_out,
-):
+    inverse_ref, soma_ref, potential_ref, volts_ref, soma_out, potential_out,
+):
+    potential_out[...] = potential_ref[...]
     soma = next_soma(
         soma_v_ref[...], soma_stim_ref[...],
         [p0_ref[...], p1_ref[...], p2_ref[...], p3_ref[...]], soma_ref[0:1, 0:1],
@@ -622,31 +625,31 @@
     )(own, other, slot_rows_out, potential, slot_target)
     received = exchange(send, devices)
     groups = devices // 2 + 16
-    here, group, column, within, heavy = call(
+    here, group, column, within = call(
         bind(beside_kernel, devices),
         [False] * 4,
         [
             row, (vox.shape, i32, False), (vox.shape, i32, False),
-            ((groups, 256), i32, False), ((1, 1), i32, False),
+            ((groups, 256), i32, False),
         ],
         flops=8 * 10**9,
     )(volts_table, slot_target, base, vox)
     rhs, partial, gap, potential = call(
         bind(fourth_kernel, devices, stride, n_split, field_scale),
-        [False] * 13,
+        [False] * 12,
         [full, line, row, quads],
     )(
-        received, here, group, column, within, heavy,
+        received, here, group, column, within,
         slot_target, slot_weight, factor, base, inverse, soma_consts, resist,
     )
     terms = split_terms(partial, n_split)
     (solved,) = solve(rhs, slot_target, gap, inverse)
 
-    operands = (solved, *terms, soma, soma_stim, inverse, soma_consts)
-    volts, soma = call(
+    operands = (solved, *terms, soma, soma_stim, inverse, soma_consts, potential)
+    volts, soma, potential = call(
         last_kernel,
         [False] * len(operands),
-        [full, line],
+        [full, line, quads],
     )(*operands)
     return volts[None], gate[None], soma.reshape(cell_dev), potential.reshape(vox_dev)
 

time: 77 us -> 76 us (0.987)
  Pallas kernels: 37.7 us -> 36.5 us
    pallas_call x12, Pallas kernels: 37.7 us -> 36.5 us  [placed(): run(*[pltpu.with_memory_space_constraint(x, pltpu.HBM) if stays else x fo...]
where the time goes in v5:
time: 76 us; the launch traced here: 75.5 us
  Pallas kernels  36.5 us (48%)
  blocking collectives  21 us (28%)
  starting transfers between devices  14.1 us (19%)
  waiting for transfers between devices  3.22 us (4%)
  between operations  0.76 us (1%)
    pallas_call x12, Pallas kernels, placed(): run(*[pltpu.with_memory_space_constraint(x, pltpu.HBM) if stays else x fo...  36.5 us
    all_to_all x1, blocking collectives, exchange(): lax.all_to_all(send.reshape(devices, send.size // devices), AXES, split_a...  21 us
    ppermute x6, starting transfers between devices, split_terms(): terms.append(lax.ppermute(partial, 'split', pairs))  7.72 us
    all_to_all x1, starting transfers between devices, exchange(): lax.all_to_all(send.reshape(devices, send.size // devices), AXES, split_a...  6.22 us
    all_to_all x1, waiting for transfers between devices, exchange(): lax.all_to_all(send.reshape(devices, send.size // devices), AXES, split_a...  3.04 us
  transfers between devices with their start and end apart: 9, of which 2 were waited for; matrix products, arithmetic and copies ran while one was open for 0% of the time, Pallas kernels for 30%

profile of v5, /device:TPU:0, one launch (start us, length us, event | category | flops | bytes accessed | tf_op | source)
XLA Modules:
  0.0 75.5 jit_solution(16497160576192393391)
XLA Ops:
  0.6 4.3 %shard_map.165 = (f32[32,4096]{1,0:T(8,128)S(1)}, f32[32,4096]{1,0:T(8,128)S(1)}, f32[32,4096]{1,0:T(8,128)S(1)}, f32[32,4096]{1,0:T(8,128)S(1)}, s32[4,4096]{1,...) custom-call(f32[32,4096]{1,0:T(8,128)} %bitcast.24, ...), custom_call_target="tpu_custom_call" | custom-call | bytes 1048576 | tf_op jit(solution)/shard_map/pallas_call | solution.py:497
  4.9 0.1 collective-permute-start
  5.0 3.8 %shard_map.166 = (f32[128,256]{1,0:T(8,128)S(1)}, f32[128,128]{1,0:T(8,128)S(1)}, bf16[512,512]{1,0:T(8,128)(2,1)S(1)}) custom-call(s32[4,4096]{1,0:T(4,128)S(1)} %get-tuple-element.54.refs_0_.refs_13_.refs_3_, f32[4,4096]{1,0:T(4,128)S(1)} %get-tuple-element.56.refs_1_, f32[32,4096]{1,0:T(8,128)S(1)} %get-tuple-element.57.refs_2_, ...), custom_call_target="tpu_custom_call" | custom-call | flops 4000000000 | bytes 1048576 | tf_op jit(solution)/shard_map/pallas_call | solution.py:497
  8.8 0.0 collective-permute-done.refs_1_
  8.8 21.0 %all_to_all.18 = f32[128,1,384]{2,1,0:T(1,128)S(1)} all-to-all(f32[128,1,384]{2,1,0:T(1,128)S(1)} %bitcast.22), channel_id=1, replica_groups=mesh['cells'=32,'split'=4] {'cells','split'}, dimensions={0} | all-to-all | bytes 393216 | tf_op jit(solution)/shard_map/all_to_all | solution.py:513
  29.8 3.0 %shard_map.168 = (f32[1,4096]{1,0:T(1,128)S(1)}, s32[1,4096]{1,0:T(1,128)S(1)}, f32[1,4096]{1,0:T(1,128)S(1)}, f32[1,4096]{1,0:T(1,128)S(1)}, f32[1,4096]{1,0:T(1,128)S(1)}, /*index=5*/f32[4,128]{1,0:T(4,128)S(1)}) custom-call(f32[384,128]{1,0:T(8,128)S(1)} %bitcast.23, f32[32,4096]{1,0:T(8,128)S(1)} %get-tuple-element.55.refs_1_.base_ref, ...), custom_call_target="tpu_custom_call" | custom-call | bytes 1048576 | tf_op jit(solution)/shard_map/pallas_call | solution.py:497
  32.8 0.7 collective-permute-start.3
  33.5 2.3 %collective-permute-start.2 = (f32[1,4096]{1,0:T(1,128)S(1)}, f32[1,4096]{1,0:T(1,128)S(1)}, u32[]{:S(2)}, u32[]{:S(2)}) collective-permute-start(f32[1,4096]{1,0:T(1,128)S(1)} %get-tuple-element.72.refs_1_), channel_id=1, source_target_pairs={{0,2},{1,3},{2,0},{3,1},{4,6},{5,7},{6,4},{7,5},{8,10},{9,11},{10,... | collective-permute-start | bytes 49160 | tf_op jit(solution)/shard_map/ppermute | solution.py:527
  35.8 1.1 %collective-permute-start.1 = (f32[1,4096]{1,0:T(1,128)S(1)}, f32[1,4096]{1,0:T(1,128)S(1)}, u32[]{:S(2)}, u32[]{:S(2)}) collective-permute-start(f32[1,4096]{1,0:T(1,128)S(1)} %get-tuple-element.72.refs_1_), channel_id=1, source_target_pairs={{0,3},{1,0},{2,1},{3,2},{4,7},{5,4},{6,5},{7,6},{8,11},{9,8},{10,9... | collective-permute-start | bytes 49160 | tf_op jit(solution)/shard_map/ppermute | solution.py:527
  36.9 2.9 %shard_map.169.refs_0_ = f32[32,4096]{1,0:T(8,128)S(1)} custom-call(f32[32,4096]{1,0:T(8,128)S(1)} %get-tuple-element.55.refs_1_.base_ref, s32[1,4096]{1,0:T(1,128)S(1)} %get-tuple-element.70.target_ref.refs_4_, f32[1,4096]{1,0:T(1,128)S(1)} %get-tuple-element.71.gap_ref, f32[32,128]{1,0:T(8,128)S(1)} %get-tuple-element.67.refs_3_.inverse_ref.refs_7_.refs_9_), custom_call_target="tpu_custom_call" | custom-call | flops 3000000000 | bytes 1048576 | tf_op jit(solution)/shard_map/pallas_call | solution.py:497
  39.8 0.0 collective-permute-done.3.refs_4_
  39.8 0.0 collective-permute-done.2.refs_3_
  39.8 0.0 collective-permute-done.1.refs_2_
  39.8 2.5 %shard_map.170 = (f32[32,4096]{1,0:T(8,128)}, f32[1,4096]{1,0:T(1,128)S(1)}, f32[32,4096]{1,0:T(8,128)S(1)}, f32[4,4096]{1,0:T(4,128)S(1)}, f32[32,4096]{1,0:T(8,128)S(1)}, /*index=5*/f32[128,256]{1,0:T(8,128)S(1)}) custom-call(f32[32,4096]{1,0:T(8,128)S(1)} %shard_map.169.refs_0_, f32[1,4096]{1,0:T(1,128)S(1)} %get-tuple-element.72.refs_1_, ...), custom_call_target="tpu_custom_call" | custom-call | bytes 1048576 | tf_op jit(solution)/shard_map/pallas_call | solution.py:497
  42.3 0.1 collective-permute-start.4
  42.4 3.7 %shard_map.171 = (f32[128,256]{1,0:T(8,128)S(1)}, f32[128,128]{1,0:T(8,128)S(1)}, bf16[512,512]{1,0:T(8,128)(2,1)S(1)}) custom-call(s32[4,4096]{1,0:T(4,128)S(1)} %get-tuple-element.54.refs_0_.refs_13_.refs_3_, f32[4,4096]{1,0:T(4,128)S(1)} %get-tuple-element.79.refs_1_, f32[32,4096]{1,0:T(8,128)S(1)} %get-tuple-element.80.refs_2_, ...), custom_call_target="tpu_custom_call" | custom-call | flops 4000000000 | bytes 1048576 | tf_op jit(solution)/shard_map/pallas_call | solution.py:497
  46.1 0.0 collective-permute-done.4.refs_1_
  46.1 0.8 %shard_map.172 = (f32[896,128]{1,0:T(8,128)}, s32[1,4096]{1,0:T(1,128)S(1)}) custom-call(f32[128,256]{1,0:T(8,128)S(1)} %get-tuple-element.81.refs_0_, f32[128,256]{1,0:T(8,128)S(1)} %collective-permute-done.4.refs_1_, f32[128,128]{1,0:T(8,128)S(1)} %get-tuple-element.83.refs_2_, f32[4,128]{1,0:T(4,128)S(1)} %get-tuple-element.84.refs_3_, ...), custom_call_target="tpu_custom_call" | custom-call | bytes 1048576 | tf_op jit(solution)/shard_map/pallas_call | solution.py:497
  46.9 6.2 %all-to-all-start.1 = ((f32[128,1,896]{2,1,0:T(1,128)}), f32[128,1,896]{2,1,0:T(1,128)S(1)}, u32[]{:S(2)}, u32[]{:S(2)}) async-start(f32[128,1,896]{2,1,0:T(1,128)} %bitcast.15), calls=%async_computation.1 | async-start | bytes 917504 | tf_op jit(solution)/shard_map/all_to_all | solution.py:513
  53.2 9.3 %shard_map.173 = (f32[1,4096]{1,0:T(1,128)S(1)}, s32[4,4096]{1,0:T(4,128)S(1)}, s32[4,4096]{1,0:T(4,128)S(1)}, s32[80,256]{1,0:T(8,128)S(1)}) custom-call(bf16[512,512]{1,0:T(8,128)(2,1)S(1)} %get-tuple-element.86.refs_0_, s32[1,4096]{1,0:T(1,128)S(1)} %get-tuple-element.87.refs_1_.refs_5_.target_ref, f32[32,4096]{1,0:T(8,128)S(1)} %get-tuple-element.88.refs_2_.refs_8_, ...), custom_call_target="tpu_custom_call" | custom-call | flops 8000000000 | bytes 1048576 | tf_op jit(solution)/shard_map/pallas_call | solution.py:497
  62.5 3.0 %all-to-all-done.1 = f32[128,1,896]{2,1,0:T(1,128)S(1)} async-done(((f32[128,1,896]{2,1,0:T(1,128)}), f32[128,1,896]{2,1,0:T(1,128)S(1)}, u32[]{:S(2)}, u32[]{:S(2)}) %all-to-all-start.1) | async-done | bytes 458784 | tf_op jit(solution)/shard_map/all_to_all | solution.py:513
  65.6 2.2 %shard_map.174 = (f32[32,4096]{1,0:T(8,128)S(1)}, f32[1,4096]{1,0:T(1,128)S(1)}, f32[1,4096]{1,0:T(1,128)S(1)}, f32[4,128]{1,0:T(4,128)S(1)}) custom-call(f32[896,128]{1,0:T(8,128)S(1)} %bitcast.21, f32[1,4096]{1,0:T(1,128)S(1)} %get-tuple-element.89.refs_1_, s32[4,4096]{1,0:T(4,128)S(1)} %get-tuple-element.90.refs_2_, ...), custom_call_target="tpu_custom_call" | custom-call | bytes 1048576 | tf_op jit(solution)/shard_map/pallas_call | solution.py:497
  67.8 0.7 collective-permute-start.7
  68.5 2.4 %collective-permute-start.6 = (f32[1,4096]{1,0:T(1,128)S(1)}, f32[1,4096]{1,0:T(1,128)S(1)}, u32[]{:S(2)}, u32[]{:S(2)}) collective-permute-start(f32[1,4096]{1,0:T(1,128)S(1)} %get-tuple-element.97.p0_ref), channel_id=1, source_target_pairs={{0,2},{1,3},{2,0},{3,1},{4,6},{5,7},{6,4},{7,5},{8,10},{9,11},{10,... | collective-permute-start | bytes 49160 | tf_op jit(solution)/shard_map/ppermute | solution.py:527
  70.8 0.6 collective-permute-start.5
  71.5 2.9 %shard_map.175.solved_ref = f32[32,4096]{1,0:T(8,128)S(1)} custom-call(f32[32,4096]{1,0:T(8,128)S(1)} %get-tuple-element.95.base_ref, s32[1,4096]{1,0:T(1,128)S(1)} %get-tuple-element.87.refs_1_.refs_5_.target_ref, f32[1,4096]{1,0:T(1,128)S(1)} %get-tuple-element.96.gap_ref, f32[32,128]{1,0:T(8,128)S(1)} %get-tuple-element.67.refs_3_.inverse_ref.refs_7_.refs_9_), custom_call_target="tpu_custom_call" | custom-call | flops 3000000000 | bytes 1048576 | tf_op jit(solution)/shard_map/pallas_call | solution.py:497
  74.4 0.0 collective-permute-done.7.p3_ref
  74.4 0.0 collective-permute-done.6.p2_ref
  74.4 0.2 collective-permute-done.5.p1_ref
  74.6 0.9 %shard_map.176 = (f32[32,4096]{1,0:T(8,128)}, f32[1,4096]{1,0:T(1,128)}, f32[4,128]{1,0:T(4,128)}) custom-call(f32[32,4096]{1,0:T(8,128)S(1)} %shard_map.175.solved_ref, f32[1,4096]{1,0:T(1,128)S(1)} %get-tuple-element.97.p0_ref, f32[1,4096]{1,0:T(1,128)S(1)} %collective-permute-done.5.p1_ref, f32[1,4096]{1,0:T(1,128)S(1)} %collective-permute-done.6.p2_ref, ...), custom_call_target="tpu_custom_call" | custom-call | bytes 1048576 | tf_op jit(solution)/shard_map/pallas_call | solution.py:497
  (1 shorter events, 0.0 us)
Async XLA Ops:
  4.9 3.9 %collective-permute-start = (f32[128,256]{1,0:T(8,128)S(1)}, f32[128,256]{1,0:T(8,128)S(1)}, u32[]{:S(2)}, u32[]{:S(2)}) collective-permute-start(f32[128,256]{1,0:T(8,128)S(1)} %get-tuple-element.64), channel_id=1, source_target_pairs={{0,4},{4,0},{8,12},{12,8},{16,20},{20,16},{24,28},{28,24},{32,36},... | collective-permute-start | bytes 393224 | tf_op jit(solution)/shard_map/ppermute | solution.py:520
  32.8 7.0 %collective-permute-start.3 = (f32[1,4096]{1,0:T(1,128)S(1)}, f32[1,4096]{1,0:T(1,128)S(1)}, u32[]{:S(2)}, u32[]{:S(2)}) collective-permute-start(f32[1,4096]{1,0:T(1,128)S(1)} %get-tuple-element.72.refs_1_), channel_id=1, source_target_pairs={{0,1},{1,2},{2,3},{3,0},{4,5},{5,6},{6,7},{7,4},{8,9},{9,10},{10,1... | collective-permute-start | bytes 49160 | tf_op jit(solution)/shard_map/ppermute | solution.py:527
  33.5 6.3 %collective-permute-start.2 = (f32[1,4096]{1,0:T(1,128)S(1)}, f32[1,4096]{1,0:T(1,128)S(1)}, u32[]{:S(2)}, u32[]{:S(2)}) collective-permute-start(f32[1,4096]{1,0:T(1,128)S(1)} %get-tuple-element.72.refs_1_), channel_id=1, source_target_pairs={{0,2},{1,3},{2,0},{3,1},{4,6},{5,7},{6,4},{7,5},{8,10},{9,11},{10,... | collective-permute-start | bytes 49160 | tf_op jit(solution)/shard_map/ppermute | solution.py:527
  35.8 4.0 %collective-permute-start.1 = (f32[1,4096]{1,0:T(1,128)S(1)}, f32[1,4096]{1,0:T(1,128)S(1)}, u32[]{:S(2)}, u32[]{:S(2)}) collective-permute-start(f32[1,4096]{1,0:T(1,128)S(1)} %get-tuple-element.72.refs_1_), channel_id=1, source_target_pairs={{0,3},{1,0},{2,1},{3,2},{4,7},{5,4},{6,5},{7,6},{8,11},{9,8},{10,9... | collective-permute-start | bytes 49160 | tf_op jit(solution)/shard_map/ppermute | solution.py:527
  42.3 3.8 %collective-permute-start.4 = (f32[128,256]{1,0:T(8,128)S(1)}, f32[128,256]{1,0:T(8,128)S(1)}, u32[]{:S(2)}, u32[]{:S(2)}) collective-permute-start(f32[128,256]{1,0:T(8,128)S(1)} %get-tuple-element.82), channel_id=1, source_target_pairs={{0,4},{4,0},{8,12},{12,8},{16,20},{20,16},{24,28},{28,24},{32,36},... | collective-permute-start | bytes 393224 | tf_op jit(solution)/shard_map/ppermute | solution.py:520
  46.9 18.6 %all-to-all-start.1 = ((f32[128,1,896]{2,1,0:T(1,128)}), f32[128,1,896]{2,1,0:T(1,128)S(1)}, u32[]{:S(2)}, u32[]{:S(2)}) async-start(f32[128,1,896]{2,1,0:T(1,128)} %bitcast.15), calls=%async_computation.1 | async-start | bytes 917504 | tf_op jit(solution)/shard_map/all_to_all | solution.py:513
  67.8 6.6 %collective-permute-start.7 = (f32[1,4096]{1,0:T(1,128)S(1)}, f32[1,4096]{1,0:T(1,128)S(1)}, u32[]{:S(2)}, u32[]{:S(2)}) collective-permute-start(f32[1,4096]{1,0:T(1,128)S(1)} %get-tuple-element.97.p0_ref), channel_id=1, source_target_pairs={{0,1},{1,2},{2,3},{3,0},{4,5},{5,6},{6,7},{7,4},{8,9},{9,10},{10,1... | collective-permute-start | bytes 49160 | tf_op jit(solution)/shard_map/ppermute | solution.py:527
  68.5 6.0 %collective-permute-start.6 = (f32[1,4096]{1,0:T(1,128)S(1)}, f32[1,4096]{1,0:T(1,128)S(1)}, u32[]{:S(2)}, u32[]{:S(2)}) collective-permute-start(f32[1,4096]{1,0:T(1,128)S(1)} %get-tuple-element.97.p0_ref), channel_id=1, source_target_pairs={{0,2},{1,3},{2,0},{3,1},{4,6},{5,7},{6,4},{7,5},{8,10},{9,11},{10,... | collective-permute-start | bytes 49160 | tf_op jit(solution)/shard_map/ppermute | solution.py:527
  70.8 3.7 %collective-permute-start.5 = (f32[1,4096]{1,0:T(1,128)S(1)}, f32[1,4096]{1,0:T(1,128)S(1)}, u32[]{:S(2)}, u32[]{:S(2)}) collective-permute-start(f32[1,4096]{1,0:T(1,128)S(1)} %get-tuple-element.97.p0_ref), channel_id=1, source_target_pairs={{0,3},{1,0},{2,1},{3,2},{4,7},{5,4},{6,5},{7,6},{8,11},{9,8},{10,9... | collective-permute-start | bytes 49160 | tf_op jit(solution)/shard_map/ppermute | solution.py:527

commit v6 on v5

--- a/solution.py
+++ b/solution.py
@@ -308,11 +308,19 @@
     own_potential(potential_ref, recv_ref, resist_ref, devices, stride, n_split, field_scale)
 
 
+def thirds(x):
+    high = x.astype(bf16)
+    rest = x - high.astype(f32)
+    middle = rest.astype(bf16)
+    return high, middle, (rest - middle.astype(f32)).astype(bf16)
+
+
 def solve(inverse_ref, rhs):
-    return jnp.dot(
-        inverse_ref[:, : rhs.shape[0]], rhs, precision=lax.Precision.HIGHEST,
-        preferred_element_type=f32,
-    )
+    high, middle, low = thirds(inverse_ref[:, : rhs.shape[0]])
+    left = jnp.concatenate([high, high, middle, middle, high, low], axis=1)
+    high, middle, low = thirds(rhs)
+    right = jnp.concatenate([high, middle, high, middle, low, high], axis=0)
+    return jnp.dot(left, right, preferred_element_type=f32)
 
 
 def solve_kernel(base_ref, target_ref, gap_ref, inverse_ref, solved_ref):
@@ -402,44 +410,77 @@
 
 
 def third_send_kernel(
-    devices, stride, own_ref, other_ref, rows_ref, potential_ref, target_ref,
+    devices, stride, n_split, own_ref, other_ref, rows_ref, potential_ref, target_ref,
     send_ref, target_out,
 ):
     target_out[...] = target_ref[...]
     put_rows(send_ref, 0, own_ref[...] + other_ref[...], devices, stride)
-    for j in range(LOW // 128):
-        each = jnp.broadcast_to(potential_ref[j : j + 1, :], (devices, 128))
-        put_rows(send_ref, LOW // 256 + j, each, devices, stride)
+    rows = LOW // 256
+    target = lax.broadcasted_iota(jnp.int32, (devices, 128), 0)
+    odd = (target // n_split) % 2 == 1
+    for j in range(rows):
+        each = jnp.where(
+            odd, potential_ref[rows + j : rows + j + 1, :], potential_ref[j : j + 1, :]
+        )
+        put_rows(send_ref, rows + j, each, devices, stride)
     put_rows(send_ref, stride - 1, rows_ref[...], devices, stride)
 
 
+def fourth_half_kernel(devices, stride, recv_ref, within_ref, half_ref, within_out):
+    within_out[...] = within_ref[...]
+    rows = LOW // 256
+    for j in range(rows):
+        half_ref[j * devices : (j + 1) * devices, :] = recv_ref[
+            pl.ds(rows + j, devices, stride=stride), :
+        ]
+
+
+def fourth_rows_kernel(
+    devices, stride, n_split, field_scale,
+    recv_ref, half_ref, here_ref, target_ref, weight_ref, factor_ref, base_ref,
+    inverse_ref, resist_ref,
+    first_ref, gap_ref, potential_ref,
+):
+    cell_dev = base_ref.shape[1]
+    slots = recv_ref[pl.ds(stride - 1, devices, stride=stride), :].T
+    gap = wide(slots[:CAP]) - weight_ref[...] * here_ref[...]
+    gap_ref[...] = gap
+    heads = add_heads(factor_ref[...] * gap, target_ref[...], cell_dev)
+    first_ref[...] = head_term(inverse_ref, base_ref[...]) + heads
+    own_potential(potential_ref, recv_ref, resist_ref, devices, stride, n_split, field_scale)
+
+
 def fourth_kernel(
-    devices, stride, n_split, field_scale,
-    recv_ref, here_ref, group_ref, column_ref, within_ref,
-    target_ref, weight_ref, factor_ref, base_ref, inverse_ref, soma_ref, resist_ref,
-    rhs_ref, partial_ref, gap_ref, potential_ref,
+    devices,
+    half_ref, other_ref, group_ref, column_ref, within_ref,
+    base_ref, first_ref, inverse_ref, soma_ref,
+    rhs_ref, partial_ref,
 ):
     comp_count, cell_dev = base_ref.shape
     block_count = group_ref.shape[0]
     block_size = comp_count // block_count
-    parts = LOW // 128
-    first = LOW // 256
-    slots = recv_ref[pl.ds(stride - 1, devices, stride=stride), :].T
-    gap = wide(slots[:CAP]) - weight_ref[...] * here_ref[...]
-    gap_ref[...] = gap
+    even = core() == 0
+
+    def owners(first, count, step):
+        mine, other = (
+            [ref[pl.ds(j * devices + first, count, stride=step), :] for j in range(LOW // 256)]
+            for ref in (half_ref, other_ref)
+        )
+        low = [jnp.where(even, a, b) for a, b in zip(mine, other)]
+        return low + [jnp.where(even, b, a) for a, b in zip(mine, other)]
+
     half = devices // 2
     size = within_ref.shape[0]
-    sides = []
-    for side in range(2):
-        owners = [
-            recv_ref[pl.ds(side * stride + first + j, half, stride=2 * stride), :]
-            for j in range(parts)
-        ]
-        sides.append(look_up(owners, within_ref[:half, side * 128 : (side + 1) * 128]))
+    sides = [
+        look_up(
+            owners(side, half, 2),
+            within_ref[:half, side * 128 : (side + 1) * 128],
+        )
+        for side in range(2)
+    ]
     heavy = lax.broadcasted_iota(jnp.int32, (devices, 128), 0) == within_ref[half : half + 1, 128:129]
     owner = []
-    for j in range(parts):
-        rows = recv_ref[pl.ds(first + j, devices, stride=stride), :]
+    for rows in owners(0, devices, 1):
         one = jnp.sum(jnp.where(heavy, rows, 0.0), axis=0, keepdims=True)
         owner.append(jnp.broadcast_to(one, (size - half, 128)))
     rest = look_up(owner, within_ref[half:, :128])
@@ -461,11 +502,9 @@
         jnp.broadcast_to(phi[:, k * cell_dev : (k + 1) * cell_dev], (block_size, cell_dev))
         for k in range(block_count)
     ]
-    rhs = base_ref[...] - ephaptic * jnp.concatenate(looked, axis=0)
-    rhs_ref[...] = rhs
-    heads = add_heads(factor_ref[...] * gap, target_ref[...], cell_dev)
-    partial_ref[...] = soma_ref[1:2, 0:1] * (head_term(inverse_ref, rhs) + heads)
-    own_potential(potential_ref, recv_ref, resist_ref, devices, stride, n_split, field_scale)
+    field = ephaptic * jnp.concatenate(looked, axis=0)
+    rhs_ref[...] = base_ref[...] - field
+    partial_ref[...] = soma_ref[1:2, 0:1] * (first_ref[...] - head_term(inverse_ref, field))
 
 
 def last_kernel(
@@ -605,7 +644,7 @@
     solve = call(solve_kernel, [False] * 4, [full], flops=3 * 10**9)
     (solved,) = solve(base, slot_target, gap, inverse)
 
-    stride = parts // 2 + parts + 1
+    stride = parts // 2 + parts // 2 + 1
     operands = (
         solved, *terms, soma_v, soma_stim, inverse, soma_consts, gate, rate, cond, stim, vox,
     )
@@ -620,7 +659,7 @@
         bind(third_rows_kernel, devices), [False] * 7, [sums, gap_rows, table_out], flops=4 * 10**9
     )(vox, blocks, volts, source, route, weight, rank)
     send, slot_target = call(
-        bind(third_send_kernel, devices, stride), [False] * 5,
+        bind(third_send_kernel, devices, stride, n_split), [False] * 5,
         [((devices * stride, 128), f32, False), row_i32],
     )(own, other, slot_rows_out, potential, slot_target)
     received = exchange(send, devices)
@@ -634,13 +673,19 @@
         ],
         flops=8 * 10**9,
     )(volts_table, slot_target, base, vox)
-    rhs, partial, gap, potential = call(
-        bind(fourth_kernel, devices, stride, n_split, field_scale),
-        [False] * 12,
-        [full, line, row, quads],
-    )(
-        received, here, group, column, within,
-        slot_target, slot_weight, factor, base, inverse, soma_consts, resist,
+    half, within = call(
+        bind(fourth_half_kernel, devices, stride), [False] * 2,
+        [((parts // 2 * devices, 128), f32, False), (within.shape, i32, False)],
+    )(received, within)
+    other = other_core(half, n_cells)
+    first, gap, potential = call(
+        bind(fourth_rows_kernel, devices, stride, n_split, field_scale),
+        [False] * 9,
+        [line, row, quads],
+        flops=10**9,
+    )(received, half, here, slot_target, slot_weight, factor, base, inverse, resist)
+    rhs, partial = call(bind(fourth_kernel, devices), [False] * 9, [full, line])(
+        half, other, group, column, within, base, first, inverse, soma_consts
     )
     terms = split_terms(partial, n_split)
     (solved,) = solve(rhs, slot_target, gap, inverse)

time: 76 us -> 75.3 us (level)
  waiting for transfers between devices: 3.22 us -> 2.29 us
    all_to_all x1, waiting for transfers between devices: 3.04 us -> 1.65 us  [exchange(): lax.all_to_all(send.reshape(devices, send.size // devices), AXES, split_a...]
    pallas_call x12 -> x14, Pallas kernels: 36.5 us -> 36.3 us  [placed(): run(*[pltpu.with_memory_space_constraint(x, pltpu.HBM) if stays else x fo...]
  transfers between devices with their start and end apart: 9 -> 10, of which waited for: 2 -> 3; matrix products, arithmetic and copies ran while one was open for 0% -> 0% of each run, Pallas kernels for 30% -> 30%
where the time goes in v6:
time: 75.3 us; the launch traced here: 75 us
  Pallas kernels  36.3 us (48%)
  blocking collectives  21 us (28%)
  starting transfers between devices  14.7 us (20%)
  waiting for transfers between devices  2.29 us (3%)
  between operations  0.77 us (1%)
    pallas_call x14, Pallas kernels, placed(): run(*[pltpu.with_memory_space_constraint(x, pltpu.HBM) if stays else x fo...  36.3 us
    all_to_all x1, blocking collectives, exchange(): lax.all_to_all(send.reshape(devices, send.size // devices), AXES, split_a...  21 us
    ppermute x6, starting transfers between devices, split_terms(): terms.append(lax.ppermute(partial, 'split', pairs))  7.98 us
    all_to_all x1, starting transfers between devices, exchange(): lax.all_to_all(send.reshape(devices, send.size // devices), AXES, split_a...  6.22 us
    all_to_all x1, waiting for transfers between devices, exchange(): lax.all_to_all(send.reshape(devices, send.size // devices), AXES, split_a...  1.65 us
  transfers between devices with their start and end apart: 10, of which 3 were waited for; matrix products, arithmetic and copies ran while one was open for 0% of the time, Pallas kernels for 30%

profile of v6, /device:TPU:0, one launch (start us, length us, event | category | flops | bytes accessed | tf_op | source)
XLA Modules:
  0.0 75.0 jit_solution(2158045680703199923)
XLA Ops:
  0.6 4.3 %shard_map.165 = (f32[32,4096]{1,0:T(8,128)S(1)}, f32[32,4096]{1,0:T(8,128)S(1)}, f32[32,4096]{1,0:T(8,128)S(1)}, f32[32,4096]{1,0:T(8,128)S(1)}, s32[4,4096]{1,...) custom-call(f32[32,4096]{1,0:T(8,128)} %bitcast.25, ...), custom_call_target="tpu_custom_call" | custom-call | bytes 1048576 | tf_op jit(solution)/shard_map/pallas_call | solution.py:536
  4.9 0.1 collective-permute-start
  5.0 3.8 %shard_map.166 = (f32[128,256]{1,0:T(8,128)S(1)}, f32[128,128]{1,0:T(8,128)S(1)}, bf16[512,512]{1,0:T(8,128)(2,1)S(1)}) custom-call(s32[4,4096]{1,0:T(4,128)S(1)} %get-tuple-element.57.refs_0_.refs_13_.refs_3_, f32[4,4096]{1,0:T(4,128)S(1)} %get-tuple-element.59.refs_1_, f32[32,4096]{1,0:T(8,128)S(1)} %get-tuple-element.60.refs_2_, ...), custom_call_target="tpu_custom_call" | custom-call | flops 4000000000 | bytes 1048576 | tf_op jit(solution)/shard_map/pallas_call | solution.py:536
  8.8 0.0 collective-permute-done.refs_1_
  8.8 21.0 %all_to_all.18 = f32[128,1,384]{2,1,0:T(1,128)S(1)} all-to-all(f32[128,1,384]{2,1,0:T(1,128)S(1)} %bitcast.23), channel_id=1, replica_groups=mesh['cells'=32,'split'=4] {'cells','split'}, dimensions={0} | all-to-all | bytes 393216 | tf_op jit(solution)/shard_map/all_to_all | solution.py:552
  29.8 3.0 %shard_map.168 = (f32[1,4096]{1,0:T(1,128)S(1)}, s32[1,4096]{1,0:T(1,128)S(1)}, f32[1,4096]{1,0:T(1,128)S(1)}, f32[1,4096]{1,0:T(1,128)S(1)}, f32[1,4096]{1,0:T(1,128)S(1)}, /*index=5*/f32[4,128]{1,0:T(4,128)S(1)}) custom-call(f32[384,128]{1,0:T(8,128)S(1)} %bitcast.24, f32[32,4096]{1,0:T(8,128)S(1)} %get-tuple-element.58.refs_1_.base_ref, ...), custom_call_target="tpu_custom_call" | custom-call | bytes 1048576 | tf_op jit(solution)/shard_map/pallas_call | solution.py:536
  32.8 0.7 collective-permute-start.3
  33.5 2.3 %collective-permute-start.2 = (f32[1,4096]{1,0:T(1,128)S(1)}, f32[1,4096]{1,0:T(1,128)S(1)}, u32[]{:S(2)}, u32[]{:S(2)}) collective-permute-start(f32[1,4096]{1,0:T(1,128)S(1)} %get-tuple-element.75.refs_1_), channel_id=1, source_target_pairs={{0,2},{1,3},{2,0},{3,1},{4,6},{5,7},{6,4},{7,5},{8,10},{9,11},{10,... | collective-permute-start | bytes 49160 | tf_op jit(solution)/shard_map/ppermute | solution.py:566
  35.8 1.1 %collective-permute-start.1 = (f32[1,4096]{1,0:T(1,128)S(1)}, f32[1,4096]{1,0:T(1,128)S(1)}, u32[]{:S(2)}, u32[]{:S(2)}) collective-permute-start(f32[1,4096]{1,0:T(1,128)S(1)} %get-tuple-element.75.refs_1_), channel_id=1, source_target_pairs={{0,3},{1,0},{2,1},{3,2},{4,7},{5,4},{6,5},{7,6},{8,11},{9,8},{10,9... | collective-permute-start | bytes 49160 | tf_op jit(solution)/shard_map/ppermute | solution.py:566
  36.9 2.7 %shard_map.169.refs_0_ = f32[32,4096]{1,0:T(8,128)S(1)} custom-call(f32[32,4096]{1,0:T(8,128)S(1)} %get-tuple-element.58.refs_1_.base_ref, s32[1,4096]{1,0:T(1,128)S(1)} %get-tuple-element.73.target_ref.refs_4_, f32[1,4096]{1,0:T(1,128)S(1)} %get-tuple-element.74.gap_ref, f32[32,128]{1,0:T(8,128)S(1)} %get-tuple-element.70.refs_3_.inverse_ref.refs_7_), custom_call_target="tpu_custom_call" | custom-call | flops 3000000000 | bytes 1048576 | tf_op jit(solution)/shard_map/pallas_call | solution.py:536
  39.6 0.0 collective-permute-done.3.refs_4_
  39.6 0.0 collective-permute-done.2.refs_3_
  39.6 0.0 collective-permute-done.1.refs_2_
  39.6 2.5 %shard_map.170 = (f32[32,4096]{1,0:T(8,128)}, f32[1,4096]{1,0:T(1,128)S(1)}, f32[32,4096]{1,0:T(8,128)S(1)}, f32[4,4096]{1,0:T(4,128)S(1)}, f32[32,4096]{1,0:T(8,128)S(1)}, /*index=5*/f32[128,256]{1,0:T(8,128)S(1)}) custom-call(f32[32,4096]{1,0:T(8,128)S(1)} %shard_map.169.refs_0_, f32[1,4096]{1,0:T(1,128)S(1)} %get-tuple-element.75.refs_1_, ...), custom_call_target="tpu_custom_call" | custom-call | bytes 1048576 | tf_op jit(solution)/shard_map/pallas_call | solution.py:536
  42.1 0.1 collective-permute-start.4
  42.2 3.7 %shard_map.171 = (f32[128,256]{1,0:T(8,128)S(1)}, f32[128,128]{1,0:T(8,128)S(1)}, bf16[512,512]{1,0:T(8,128)(2,1)S(1)}) custom-call(s32[4,4096]{1,0:T(4,128)S(1)} %get-tuple-element.57.refs_0_.refs_13_.refs_3_, f32[4,4096]{1,0:T(4,128)S(1)} %get-tuple-element.82.refs_1_, f32[32,4096]{1,0:T(8,128)S(1)} %get-tuple-element.83.refs_2_, ...), custom_call_target="tpu_custom_call" | custom-call | flops 4000000000 | bytes 1048576 | tf_op jit(solution)/shard_map/pallas_call | solution.py:536
  45.9 0.0 collective-permute-done.4.refs_1_
  45.9 0.8 %shard_map.172 = (f32[640,128]{1,0:T(8,128)}, s32[1,4096]{1,0:T(1,128)S(1)}) custom-call(f32[128,256]{1,0:T(8,128)S(1)} %get-tuple-element.84.refs_0_, f32[128,256]{1,0:T(8,128)S(1)} %collective-permute-done.4.refs_1_, f32[128,128]{1,0:T(8,128)S(1)} %get-tuple-element.86.refs_2_, f32[4,128]{1,0:T(4,128)S(1)} %get-tuple-element.87.refs_3_, ...), custom_call_target="tpu_custom_call" | custom-call | bytes 1048576 | tf_op jit(solution)/shard_map/pallas_call | solution.py:536
  46.7 6.2 %all-to-all-start.1 = ((f32[128,1,640]{2,1,0:T(1,128)}), f32[128,1,640]{2,1,0:T(1,128)S(1)}, u32[]{:S(2)}, u32[]{:S(2)}) async-start(f32[128,1,640]{2,1,0:T(1,128)} %bitcast.15), calls=%async_computation.1 | async-start | bytes 655360 | tf_op jit(solution)/shard_map/all_to_all | solution.py:552
  52.9 9.3 %shard_map.173 = (f32[1,4096]{1,0:T(1,128)S(1)}, s32[4,4096]{1,0:T(4,128)S(1)}, s32[4,4096]{1,0:T(4,128)S(1)}, s32[80,256]{1,0:T(8,128)S(1)}) custom-call(bf16[512,512]{1,0:T(8,128)(2,1)S(1)} %get-tuple-element.89.refs_0_, s32[1,4096]{1,0:T(1,128)S(1)} %get-tuple-element.90.refs_1_.refs_3_.target_ref, ...), custom_call_target="tpu_custom_call" | custom-call | flops 8000000000 | bytes 1048576 | tf_op jit(solution)/shard_map/pallas_call | solution.py:536
  62.3 1.7 %all-to-all-done.1 = f32[128,1,640]{2,1,0:T(1,128)S(1)} async-done(((f32[128,1,640]{2,1,0:T(1,128)}), f32[128,1,640]{2,1,0:T(1,128)S(1)}, u32[]{:S(2)}, u32[]{:S(2)}) %all-to-all-start.1) | async-done | bytes 327712 | tf_op jit(solution)/shard_map/all_to_all | solution.py:552
  63.9 0.3 collective-permute-start.5
  64.3 0.6 shard_map.175
  64.8 0.5 collective-permute-done.5.refs_1_
  65.4 1.9 %shard_map.176 = (f32[32,4096]{1,0:T(8,128)S(1)}, f32[1,4096]{1,0:T(1,128)S(1)}) custom-call(f32[256,128]{1,0:T(8,128)S(1)} %get-tuple-element.93.refs_1_.refs_0_, f32[256,128]{1,0:T(8,128)S(1)} %collective-permute-done.5.refs_1_, s32[4,4096]{1,0:T(4,128)S(1)} %get-tuple-element.94.refs_2_, s32[4,4096]{1,0:T(4,128)S(1)} %get-tuple-element.95.refs_3_, ...), custom_call_target="tpu_custom_call" | custom-call | bytes 1048576 | tf_op jit(solution)/shard_map/pallas_call | solution.py:536
  67.2 0.7 collective-permute-start.8
  67.9 2.4 %collective-permute-start.7 = (f32[1,4096]{1,0:T(1,128)S(1)}, f32[1,4096]{1,0:T(1,128)S(1)}, u32[]{:S(2)}, u32[]{:S(2)}) collective-permute-start(f32[1,4096]{1,0:T(1,128)S(1)} %get-tuple-element.103.p0_ref), channel_id=1, source_target_pairs={{0,2},{1,3},{2,0},{3,1},{4,6},{5,7},{6,4},{7,5},{8,10},{9,11},{10,... | collective-permute-start | bytes 49160 | tf_op jit(solution)/shard_map/ppermute | solution.py:566
  70.3 0.9 %collective-permute-start.6 = (f32[1,4096]{1,0:T(1,128)S(1)}, f32[1,4096]{1,0:T(1,128)S(1)}, u32[]{:S(2)}, u32[]{:S(2)}) collective-permute-start(f32[1,4096]{1,0:T(1,128)S(1)} %get-tuple-element.103.p0_ref), channel_id=1, source_target_pairs={{0,3},{1,0},{2,1},{3,2},{4,7},{5,4},{6,5},{7,6},{8,11},{9,8},{10,9... | collective-permute-start | bytes 49160 | tf_op jit(solution)/shard_map/ppermute | solution.py:566
  71.2 2.7 %shard_map.177.solved_ref = f32[32,4096]{1,0:T(8,128)S(1)} custom-call(f32[32,4096]{1,0:T(8,128)S(1)} %get-tuple-element.101.base_ref, s32[1,4096]{1,0:T(1,128)S(1)} %get-tuple-element.90.refs_1_.refs_3_.target_ref, f32[1,4096]{1,0:T(1,128)S(1)} %get-tuple-element.102.gap_ref, f32[32,128]{1,0:T(8,128)S(1)} %get-tuple-element.70.refs_3_.inverse_ref.refs_7_), custom_call_target="tpu_custom_call" | custom-call | flops 3000000000 | bytes 1048576 | tf_op jit(solution)/shard_map/pallas_call | solution.py:536
  73.9 0.0 collective-permute-done.7.p2_ref
  74.0 0.1 collective-permute-done.6.p1_ref
  74.0 0.9 %shard_map.178 = (f32[32,4096]{1,0:T(8,128)}, f32[1,4096]{1,0:T(1,128)}, f32[4,128]{1,0:T(4,128)}) custom-call(f32[32,4096]{1,0:T(8,128)S(1)} %shard_map.177.solved_ref, f32[1,4096]{1,0:T(1,128)S(1)} %get-tuple-element.103.p0_ref, f32[1,4096]{1,0:T(1,128)S(1)} %collective-permute-done.6.p1_ref, f32[1,4096]{1,0:T(1,128)S(1)} %collective-permute-done.7.p2_ref, ...), custom_call_target="tpu_custom_call" | custom-call | bytes 1048576 | tf_op jit(solution)/shard_map/pallas_call | solution.py:536
  (3 shorter events, 0.0 us)
Async XLA Ops:
  4.9 3.9 %collective-permute-start = (f32[128,256]{1,0:T(8,128)S(1)}, f32[128,256]{1,0:T(8,128)S(1)}, u32[]{:S(2)}, u32[]{:S(2)}) collective-permute-start(f32[128,256]{1,0:T(8,128)S(1)} %get-tuple-element.67), channel_id=1, source_target_pairs={{0,4},{4,0},{8,12},{12,8},{16,20},{20,16},{24,28},{28,24},{32,36},... | collective-permute-start | bytes 393224 | tf_op jit(solution)/shard_map/ppermute | solution.py:559
  32.8 6.8 %collective-permute-start.3 = (f32[1,4096]{1,0:T(1,128)S(1)}, f32[1,4096]{1,0:T(1,128)S(1)}, u32[]{:S(2)}, u32[]{:S(2)}) collective-permute-start(f32[1,4096]{1,0:T(1,128)S(1)} %get-tuple-element.75.refs_1_), channel_id=1, source_target_pairs={{0,1},{1,2},{2,3},{3,0},{4,5},{5,6},{6,7},{7,4},{8,9},{9,10},{10,1... | collective-permute-start | bytes 49160 | tf_op jit(solution)/shard_map/ppermute | solution.py:566
  33.5 6.1 %collective-permute-start.2 = (f32[1,4096]{1,0:T(1,128)S(1)}, f32[1,4096]{1,0:T(1,128)S(1)}, u32[]{:S(2)}, u32[]{:S(2)}) collective-permute-start(f32[1,4096]{1,0:T(1,128)S(1)} %get-tuple-element.75.refs_1_), channel_id=1, source_target_pairs={{0,2},{1,3},{2,0},{3,1},{4,6},{5,7},{6,4},{7,5},{8,10},{9,11},{10,... | collective-permute-start | bytes 49160 | tf_op jit(solution)/shard_map/ppermute | solution.py:566
  35.8 3.8 %collective-permute-start.1 = (f32[1,4096]{1,0:T(1,128)S(1)}, f32[1,4096]{1,0:T(1,128)S(1)}, u32[]{:S(2)}, u32[]{:S(2)}) collective-permute-start(f32[1,4096]{1,0:T(1,128)S(1)} %get-tuple-element.75.refs_1_), channel_id=1, source_target_pairs={{0,3},{1,0},{2,1},{3,2},{4,7},{5,4},{6,5},{7,6},{8,11},{9,8},{10,9... | collective-permute-start | bytes 49160 | tf_op jit(solution)/shard_map/ppermute | solution.py:566
  42.1 3.8 %collective-permute-start.4 = (f32[128,256]{1,0:T(8,128)S(1)}, f32[128,256]{1,0:T(8,128)S(1)}, u32[]{:S(2)}, u32[]{:S(2)}) collective-permute-start(f32[128,256]{1,0:T(8,128)S(1)} %get-tuple-element.85), channel_id=1, source_target_pairs={{0,4},{4,0},{8,12},{12,8},{16,20},{20,16},{24,28},{28,24},{32,36},... | collective-permute-start | bytes 393224 | tf_op jit(solution)/shard_map/ppermute | solution.py:559
  46.7 17.2 %all-to-all-start.1 = ((f32[128,1,640]{2,1,0:T(1,128)}), f32[128,1,640]{2,1,0:T(1,128)S(1)}, u32[]{:S(2)}, u32[]{:S(2)}) async-start(f32[128,1,640]{2,1,0:T(1,128)} %bitcast.15), calls=%async_computation.1 | async-start | bytes 655360 | tf_op jit(solution)/shard_map/all_to_all | solution.py:552
  63.9 1.4 %collective-permute-start.5 = (f32[256,128]{1,0:T(8,128)S(1)}, f32[256,128]{1,0:T(8,128)S(1)}, u32[]{:S(2)}, u32[]{:S(2)}) collective-permute-start(f32[256,128]{1,0:T(8,128)S(1)} %get-tuple-element.93.refs_1_.refs_0_), channel_id=1, source_target_pairs={{0,4},{4,0},{8,12},{12,8},{16,20},{20,16},{24,28},{28,24},{32,36},... | collective-permute-start | bytes 393224 | tf_op jit(solution)/shard_map/ppermute | solution.py:559
  67.2 6.7 %collective-permute-start.8 = (f32[1,4096]{1,0:T(1,128)S(1)}, f32[1,4096]{1,0:T(1,128)S(1)}, u32[]{:S(2)}, u32[]{:S(2)}) collective-permute-start(f32[1,4096]{1,0:T(1,128)S(1)} %get-tuple-element.103.p0_ref), channel_id=1, source_target_pairs={{0,1},{1,2},{2,3},{3,0},{4,5},{5,6},{6,7},{7,4},{8,9},{9,10},{10,1... | collective-permute-start | bytes 49160 | tf_op jit(solution)/shard_map/ppermute | solution.py:566
  67.9 6.0 %collective-permute-start.7 = (f32[1,4096]{1,0:T(1,128)S(1)}, f32[1,4096]{1,0:T(1,128)S(1)}, u32[]{:S(2)}, u32[]{:S(2)}) collective-permute-start(f32[1,4096]{1,0:T(1,128)S(1)} %get-tuple-element.103.p0_ref), channel_id=1, source_target_pairs={{0,2},{1,3},{2,0},{3,1},{4,6},{5,7},{6,4},{7,5},{8,10},{9,11},{10,... | collective-permute-start | bytes 49160 | tf_op jit(solution)/shard_map/ppermute | solution.py:566
  70.3 3.7 %collective-permute-start.6 = (f32[1,4096]{1,0:T(1,128)S(1)}, f32[1,4096]{1,0:T(1,128)S(1)}, u32[]{:S(2)}, u32[]{:S(2)}) collective-permute-start(f32[1,4096]{1,0:T(1,128)S(1)} %get-tuple-element.103.p0_ref), channel_id=1, source_target_pairs={{0,3},{1,0},{2,1},{3,2},{4,7},{5,4},{6,5},{7,6},{8,11},{9,8},{10,9... | collective-permute-start | bytes 49160 | tf_op jit(solution)/shard_map/ppermute | solution.py:566

commit v7 on v6

--- a/solution.py
+++ b/solution.py
@@ -308,18 +308,11 @@
     own_potential(potential_ref, recv_ref, resist_ref, devices, stride, n_split, field_scale)
 
 
-def thirds(x):
-    high = x.astype(bf16)
-    rest = x - high.astype(f32)
-    middle = rest.astype(bf16)
-    return high, middle, (rest - middle.astype(f32)).astype(bf16)
-
-
 def solve(inverse_ref, rhs):
-    high, middle, low = thirds(inverse_ref[:, : rhs.shape[0]])
-    left = jnp.concatenate([high, high, middle, middle, high, low], axis=1)
-    high, middle, low = thirds(rhs)
-    right = jnp.concatenate([high, middle, high, middle, low, high], axis=0)
+    high, low = halves(inverse_ref[:, : rhs.shape[0]])
+    left = jnp.concatenate([high, high, low, low], axis=1)
+    high, low = halves(rhs)
+    right = jnp.concatenate([high, low, high, low], axis=0)
     return jnp.dot(left, right, preferred_element_type=f32)
 
 

time: 75.3 us -> 75 us (level)
  transfers between devices with their start and end apart: 10 -> 10, of which waited for: 3 -> 4; matrix products, arithmetic and copies ran while one was open for 0% -> 0% of each run, Pallas kernels for 30% -> 30%
where the time goes in v7:
time: 75 us; the launch traced here: 74.8 us
  Pallas kernels  36 us (48%)
  blocking collectives  21 us (28%)
  starting transfers between devices  14.6 us (19%)
  waiting for transfers between devices  2.51 us (3%)
  between operations  0.76 us (1%)
    pallas_call x14, Pallas kernels, placed(): run(*[pltpu.with_memory_space_constraint(x, pltpu.HBM) if stays else x fo...  36 us
    all_to_all x1, blocking collectives, exchange(): lax.all_to_all(send.reshape(devices, send.size // devices), AXES, split_a...  21 us
    ppermute x6, starting transfers between devices, split_terms(): terms.append(lax.ppermute(partial, 'split', pairs))  7.98 us
    all_to_all x1, starting transfers between devices, exchange(): lax.all_to_all(send.reshape(devices, send.size // devices), AXES, split_a...  6.14 us
    all_to_all x1, waiting for transfers between devices, exchange(): lax.all_to_all(send.reshape(devices, send.size // devices), AXES, split_a...  1.65 us
  transfers between devices with their start and end apart: 10, of which 4 were waited for; matrix products, arithmetic and copies ran while one was open for 0% of the time, Pallas kernels for 30%

profile of v7, /device:TPU:0, one launch (start us, length us, event | category | flops | bytes accessed | tf_op | source)
XLA Modules:
  0.0 74.8 jit_solution(17051972265283113994)
XLA Ops:
  0.6 4.3 %shard_map.165 = (f32[32,4096]{1,0:T(8,128)S(1)}, f32[32,4096]{1,0:T(8,128)S(1)}, f32[32,4096]{1,0:T(8,128)S(1)}, f32[32,4096]{1,0:T(8,128)S(1)}, s32[4,4096]{1,...) custom-call(f32[32,4096]{1,0:T(8,128)} %bitcast.25, ...), custom_call_target="tpu_custom_call" | custom-call | bytes 1048576 | tf_op jit(solution)/shard_map/pallas_call | solution.py:529
  4.9 0.1 collective-permute-start
  5.0 3.8 %shard_map.166 = (f32[128,256]{1,0:T(8,128)S(1)}, f32[128,128]{1,0:T(8,128)S(1)}, bf16[512,512]{1,0:T(8,128)(2,1)S(1)}) custom-call(s32[4,4096]{1,0:T(4,128)S(1)} %get-tuple-element.57.refs_0_.refs_13_.refs_3_, f32[4,4096]{1,0:T(4,128)S(1)} %get-tuple-element.59.refs_1_, f32[32,4096]{1,0:T(8,128)S(1)} %get-tuple-element.60.refs_2_, ...), custom_call_target="tpu_custom_call" | custom-call | flops 4000000000 | bytes 1048576 | tf_op jit(solution)/shard_map/pallas_call | solution.py:529
  8.8 0.0 collective-permute-done.refs_1_
  8.8 21.0 %all_to_all.18 = f32[128,1,384]{2,1,0:T(1,128)S(1)} all-to-all(f32[128,1,384]{2,1,0:T(1,128)S(1)} %bitcast.23), channel_id=1, replica_groups=mesh['cells'=32,'split'=4] {'cells','split'}, dimensions={0} | all-to-all | bytes 393216 | tf_op jit(solution)/shard_map/all_to_all | solution.py:545
  29.8 3.0 %shard_map.168 = (f32[1,4096]{1,0:T(1,128)S(1)}, s32[1,4096]{1,0:T(1,128)S(1)}, f32[1,4096]{1,0:T(1,128)S(1)}, f32[1,4096]{1,0:T(1,128)S(1)}, f32[1,4096]{1,0:T(1,128)S(1)}, /*index=5*/f32[4,128]{1,0:T(4,128)S(1)}) custom-call(f32[384,128]{1,0:T(8,128)S(1)} %bitcast.24, f32[32,4096]{1,0:T(8,128)S(1)} %get-tuple-element.58.refs_1_.base_ref, ...), custom_call_target="tpu_custom_call" | custom-call | bytes 1048576 | tf_op jit(solution)/shard_map/pallas_call | solution.py:529
  32.8 0.7 collective-permute-start.3
  33.5 2.3 %collective-permute-start.2 = (f32[1,4096]{1,0:T(1,128)S(1)}, f32[1,4096]{1,0:T(1,128)S(1)}, u32[]{:S(2)}, u32[]{:S(2)}) collective-permute-start(f32[1,4096]{1,0:T(1,128)S(1)} %get-tuple-element.75.refs_1_), channel_id=1, source_target_pairs={{0,2},{1,3},{2,0},{3,1},{4,6},{5,7},{6,4},{7,5},{8,10},{9,11},{10,... | collective-permute-start | bytes 49160 | tf_op jit(solution)/shard_map/ppermute | solution.py:559
  35.8 1.1 %collective-permute-start.1 = (f32[1,4096]{1,0:T(1,128)S(1)}, f32[1,4096]{1,0:T(1,128)S(1)}, u32[]{:S(2)}, u32[]{:S(2)}) collective-permute-start(f32[1,4096]{1,0:T(1,128)S(1)} %get-tuple-element.75.refs_1_), channel_id=1, source_target_pairs={{0,3},{1,0},{2,1},{3,2},{4,7},{5,4},{6,5},{7,6},{8,11},{9,8},{10,9... | collective-permute-start | bytes 49160 | tf_op jit(solution)/shard_map/ppermute | solution.py:559
  36.9 2.6 %shard_map.169.refs_0_ = f32[32,4096]{1,0:T(8,128)S(1)} custom-call(f32[32,4096]{1,0:T(8,128)S(1)} %get-tuple-element.58.refs_1_.base_ref, s32[1,4096]{1,0:T(1,128)S(1)} %get-tuple-element.73.target_ref.refs_4_, f32[1,4096]{1,0:T(1,128)S(1)} %get-tuple-element.74.gap_ref, f32[32,128]{1,0:T(8,128)S(1)} %get-tuple-element.70.refs_3_.inverse_ref.refs_7_), custom_call_target="tpu_custom_call" | custom-call | flops 3000000000 | bytes 1048576 | tf_op jit(solution)/shard_map/pallas_call | solution.py:529
  39.4 0.0 collective-permute-done.3.refs_4_
  39.5 0.0 collective-permute-done.2.refs_3_
  39.5 0.1 collective-permute-done.1.refs_2_
  39.5 2.5 %shard_map.170 = (f32[32,4096]{1,0:T(8,128)}, f32[1,4096]{1,0:T(1,128)S(1)}, f32[32,4096]{1,0:T(8,128)S(1)}, f32[4,4096]{1,0:T(4,128)S(1)}, f32[32,4096]{1,0:T(8,128)S(1)}, /*index=5*/f32[128,256]{1,0:T(8,128)S(1)}) custom-call(f32[32,4096]{1,0:T(8,128)S(1)} %shard_map.169.refs_0_, f32[1,4096]{1,0:T(1,128)S(1)} %get-tuple-element.75.refs_1_, ...), custom_call_target="tpu_custom_call" | custom-call | bytes 1048576 | tf_op jit(solution)/shard_map/pallas_call | solution.py:529
  42.0 0.1 collective-permute-start.4
  42.1 3.7 %shard_map.171 = (f32[128,256]{1,0:T(8,128)S(1)}, f32[128,128]{1,0:T(8,128)S(1)}, bf16[512,512]{1,0:T(8,128)(2,1)S(1)}) custom-call(s32[4,4096]{1,0:T(4,128)S(1)} %get-tuple-element.57.refs_0_.refs_13_.refs_3_, f32[4,4096]{1,0:T(4,128)S(1)} %get-tuple-element.82.refs_1_, f32[32,4096]{1,0:T(8,128)S(1)} %get-tuple-element.83.refs_2_, ...), custom_call_target="tpu_custom_call" | custom-call | flops 4000000000 | bytes 1048576 | tf_op jit(solution)/shard_map/pallas_call | solution.py:529
  45.9 0.0 collective-permute-done.4.refs_1_
  45.9 0.8 %shard_map.172 = (f32[640,128]{1,0:T(8,128)}, s32[1,4096]{1,0:T(1,128)S(1)}) custom-call(f32[128,256]{1,0:T(8,128)S(1)} %get-tuple-element.84.refs_0_, f32[128,256]{1,0:T(8,128)S(1)} %collective-permute-done.4.refs_1_, f32[128,128]{1,0:T(8,128)S(1)} %get-tuple-element.86.refs_2_, f32[4,128]{1,0:T(4,128)S(1)} %get-tuple-element.87.refs_3_, ...), custom_call_target="tpu_custom_call" | custom-call | bytes 1048576 | tf_op jit(solution)/shard_map/pallas_call | solution.py:529
  46.6 6.1 %all-to-all-start.1 = ((f32[128,1,640]{2,1,0:T(1,128)}), f32[128,1,640]{2,1,0:T(1,128)S(1)}, u32[]{:S(2)}, u32[]{:S(2)}) async-start(f32[128,1,640]{2,1,0:T(1,128)} %bitcast.15), calls=%async_computation.1 | async-start | bytes 655360 | tf_op jit(solution)/shard_map/all_to_all | solution.py:545
  52.8 9.3 %shard_map.173 = (f32[1,4096]{1,0:T(1,128)S(1)}, s32[4,4096]{1,0:T(4,128)S(1)}, s32[4,4096]{1,0:T(4,128)S(1)}, s32[80,256]{1,0:T(8,128)S(1)}) custom-call(bf16[512,512]{1,0:T(8,128)(2,1)S(1)} %get-tuple-element.89.refs_0_, s32[1,4096]{1,0:T(1,128)S(1)} %get-tuple-element.90.refs_1_.refs_3_.target_ref, ...), custom_call_target="tpu_custom_call" | custom-call | flops 8000000000 | bytes 1048576 | tf_op jit(solution)/shard_map/pallas_call | solution.py:529
  62.1 1.7 %all-to-all-done.1 = f32[128,1,640]{2,1,0:T(1,128)S(1)} async-done(((f32[128,1,640]{2,1,0:T(1,128)}), f32[128,1,640]{2,1,0:T(1,128)S(1)}, u32[]{:S(2)}, u32[]{:S(2)}) %all-to-all-start.1) | async-done | bytes 327712 | tf_op jit(solution)/shard_map/all_to_all | solution.py:545
  63.8 0.3 collective-permute-start.5
  64.1 0.6 shard_map.175
  64.7 0.5 collective-permute-done.5.refs_1_
  65.2 1.9 %shard_map.176 = (f32[32,4096]{1,0:T(8,128)S(1)}, f32[1,4096]{1,0:T(1,128)S(1)}) custom-call(f32[256,128]{1,0:T(8,128)S(1)} %get-tuple-element.93.refs_1_.refs_0_, f32[256,128]{1,0:T(8,128)S(1)} %collective-permute-done.5.refs_1_, s32[4,4096]{1,0:T(4,128)S(1)} %get-tuple-element.94.refs_2_, s32[4,4096]{1,0:T(4,128)S(1)} %get-tuple-element.95.refs_3_, ...), custom_call_target="tpu_custom_call" | custom-call | bytes 1048576 | tf_op jit(solution)/shard_map/pallas_call | solution.py:529
  67.1 0.7 collective-permute-start.8
  67.8 2.4 %collective-permute-start.7 = (f32[1,4096]{1,0:T(1,128)S(1)}, f32[1,4096]{1,0:T(1,128)S(1)}, u32[]{:S(2)}, u32[]{:S(2)}) collective-permute-start(f32[1,4096]{1,0:T(1,128)S(1)} %get-tuple-element.103.p0_ref), channel_id=1, source_target_pairs={{0,2},{1,3},{2,0},{3,1},{4,6},{5,7},{6,4},{7,5},{8,10},{9,11},{10,... | collective-permute-start | bytes 49160 | tf_op jit(solution)/shard_map/ppermute | solution.py:559
  70.1 0.9 %collective-permute-start.6 = (f32[1,4096]{1,0:T(1,128)S(1)}, f32[1,4096]{1,0:T(1,128)S(1)}, u32[]{:S(2)}, u32[]{:S(2)}) collective-permute-start(f32[1,4096]{1,0:T(1,128)S(1)} %get-tuple-element.103.p0_ref), channel_id=1, source_target_pairs={{0,3},{1,0},{2,1},{3,2},{4,7},{5,4},{6,5},{7,6},{8,11},{9,8},{10,9... | collective-permute-start | bytes 49160 | tf_op jit(solution)/shard_map/ppermute | solution.py:559
  71.0 2.6 %shard_map.177.solved_ref = f32[32,4096]{1,0:T(8,128)S(1)} custom-call(f32[32,4096]{1,0:T(8,128)S(1)} %get-tuple-element.101.base_ref, s32[1,4096]{1,0:T(1,128)S(1)} %get-tuple-element.90.refs_1_.refs_3_.target_ref, f32[1,4096]{1,0:T(1,128)S(1)} %get-tuple-element.102.gap_ref, f32[32,128]{1,0:T(8,128)S(1)} %get-tuple-element.70.refs_3_.inverse_ref.refs_7_), custom_call_target="tpu_custom_call" | custom-call | flops 3000000000 | bytes 1048576 | tf_op jit(solution)/shard_map/pallas_call | solution.py:529
  73.6 0.0 collective-permute-done.7.p2_ref
  73.6 0.2 collective-permute-done.6.p1_ref
  73.9 0.9 %shard_map.178 = (f32[32,4096]{1,0:T(8,128)}, f32[1,4096]{1,0:T(1,128)}, f32[4,128]{1,0:T(4,128)}) custom-call(f32[32,4096]{1,0:T(8,128)S(1)} %shard_map.177.solved_ref, f32[1,4096]{1,0:T(1,128)S(1)} %get-tuple-element.103.p0_ref, f32[1,4096]{1,0:T(1,128)S(1)} %collective-permute-done.6.p1_ref, f32[1,4096]{1,0:T(1,128)S(1)} %collective-permute-done.7.p2_ref, ...), custom_call_target="tpu_custom_call" | custom-call | bytes 1048576 | tf_op jit(solution)/shard_map/pallas_call | solution.py:529
  (3 shorter events, 0.0 us)
Async XLA Ops:
  4.9 3.9 %collective-permute-start = (f32[128,256]{1,0:T(8,128)S(1)}, f32[128,256]{1,0:T(8,128)S(1)}, u32[]{:S(2)}, u32[]{:S(2)}) collective-permute-start(f32[128,256]{1,0:T(8,128)S(1)} %get-tuple-element.67), channel_id=1, source_target_pairs={{0,4},{4,0},{8,12},{12,8},{16,20},{20,16},{24,28},{28,24},{32,36},... | collective-permute-start | bytes 393224 | tf_op jit(solution)/shard_map/ppermute | solution.py:552
  32.8 6.6 %collective-permute-start.3 = (f32[1,4096]{1,0:T(1,128)S(1)}, f32[1,4096]{1,0:T(1,128)S(1)}, u32[]{:S(2)}, u32[]{:S(2)}) collective-permute-start(f32[1,4096]{1,0:T(1,128)S(1)} %get-tuple-element.75.refs_1_), channel_id=1, source_target_pairs={{0,1},{1,2},{2,3},{3,0},{4,5},{5,6},{6,7},{7,4},{8,9},{9,10},{10,1... | collective-permute-start | bytes 49160 | tf_op jit(solution)/shard_map/ppermute | solution.py:559
  33.5 5.9 %collective-permute-start.2 = (f32[1,4096]{1,0:T(1,128)S(1)}, f32[1,4096]{1,0:T(1,128)S(1)}, u32[]{:S(2)}, u32[]{:S(2)}) collective-permute-start(f32[1,4096]{1,0:T(1,128)S(1)} %get-tuple-element.75.refs_1_), channel_id=1, source_target_pairs={{0,2},{1,3},{2,0},{3,1},{4,6},{5,7},{6,4},{7,5},{8,10},{9,11},{10,... | collective-permute-start | bytes 49160 | tf_op jit(solution)/shard_map/ppermute | solution.py:559
  35.8 3.7 %collective-permute-start.1 = (f32[1,4096]{1,0:T(1,128)S(1)}, f32[1,4096]{1,0:T(1,128)S(1)}, u32[]{:S(2)}, u32[]{:S(2)}) collective-permute-start(f32[1,4096]{1,0:T(1,128)S(1)} %get-tuple-element.75.refs_1_), channel_id=1, source_target_pairs={{0,3},{1,0},{2,1},{3,2},{4,7},{5,4},{6,5},{7,6},{8,11},{9,8},{10,9... | collective-permute-start | bytes 49160 | tf_op jit(solution)/shard_map/ppermute | solution.py:559
  42.0 3.8 %collective-permute-start.4 = (f32[128,256]{1,0:T(8,128)S(1)}, f32[128,256]{1,0:T(8,128)S(1)}, u32[]{:S(2)}, u32[]{:S(2)}) collective-permute-start(f32[128,256]{1,0:T(8,128)S(1)} %get-tuple-element.85), channel_id=1, source_target_pairs={{0,4},{4,0},{8,12},{12,8},{16,20},{20,16},{24,28},{28,24},{32,36},... | collective-permute-start | bytes 393224 | tf_op jit(solution)/shard_map/ppermute | solution.py:552
  46.6 17.1 %all-to-all-start.1 = ((f32[128,1,640]{2,1,0:T(1,128)}), f32[128,1,640]{2,1,0:T(1,128)S(1)}, u32[]{:S(2)}, u32[]{:S(2)}) async-start(f32[128,1,640]{2,1,0:T(1,128)} %bitcast.15), calls=%async_computation.1 | async-start | bytes 655360 | tf_op jit(solution)/shard_map/all_to_all | solution.py:545
  63.8 1.4 %collective-permute-start.5 = (f32[256,128]{1,0:T(8,128)S(1)}, f32[256,128]{1,0:T(8,128)S(1)}, u32[]{:S(2)}, u32[]{:S(2)}) collective-permute-start(f32[256,128]{1,0:T(8,128)S(1)} %get-tuple-element.93.refs_1_.refs_0_), channel_id=1, source_target_pairs={{0,4},{4,0},{8,12},{12,8},{16,20},{20,16},{24,28},{28,24},{32,36},... | collective-permute-start | bytes 393224 | tf_op jit(solution)/shard_map/ppermute | solution.py:552
  67.1 6.6 %collective-permute-start.8 = (f32[1,4096]{1,0:T(1,128)S(1)}, f32[1,4096]{1,0:T(1,128)S(1)}, u32[]{:S(2)}, u32[]{:S(2)}) collective-permute-start(f32[1,4096]{1,0:T(1,128)S(1)} %get-tuple-element.103.p0_ref), channel_id=1, source_target_pairs={{0,1},{1,2},{2,3},{3,0},{4,5},{5,6},{6,7},{7,4},{8,9},{9,10},{10,1... | collective-permute-start | bytes 49160 | tf_op jit(solution)/shard_map/ppermute | solution.py:559
  67.8 5.9 %collective-permute-start.7 = (f32[1,4096]{1,0:T(1,128)S(1)}, f32[1,4096]{1,0:T(1,128)S(1)}, u32[]{:S(2)}, u32[]{:S(2)}) collective-permute-start(f32[1,4096]{1,0:T(1,128)S(1)} %get-tuple-element.103.p0_ref), channel_id=1, source_target_pairs={{0,2},{1,3},{2,0},{3,1},{4,6},{5,7},{6,4},{7,5},{8,10},{9,11},{10,... | collective-permute-start | bytes 49160 | tf_op jit(solution)/shard_map/ppermute | solution.py:559
  70.1 3.7 %collective-permute-start.6 = (f32[1,4096]{1,0:T(1,128)S(1)}, f32[1,4096]{1,0:T(1,128)S(1)}, u32[]{:S(2)}, u32[]{:S(2)}) collective-permute-start(f32[1,4096]{1,0:T(1,128)S(1)} %get-tuple-element.103.p0_ref), channel_id=1, source_target_pairs={{0,3},{1,0},{2,1},{3,2},{4,7},{5,4},{6,5},{7,6},{8,11},{9,8},{10,9... | collective-permute-start | bytes 49160 | tf_op jit(solution)/shard_map/ppermute | solution.py:559
